TPU v7x, 256 devices: a whole 4x4x8 slice. The times are simulated.
256 devices in a mesh: dp: 32 (over z, x), row: 2 (over core), col: 4 (over y).
Axes of the slice: x: 4, y: 4, z: 8, core: 2. Of those that a mesh axis runs over, the one named last changes fastest.
Arguments:
- tokens: bfloat16 [5120, 3584], P('dp'), may hold values from -6 to 6
- routes: int32 [5120, 8], P(('dp', 'col')), may hold values from 0 to 127, all different within a row; in each aligned block of 40 rows (0 to 39, 40 to 79, ...) at most 3 rows name the same one
- route_weights: float32 [5120, 8], P(('dp', 'col')), may hold values from 0.05 to 0.6
- teacher_in: bfloat16 [128, 2, 3584, 1024], P(('dp', 'col'), None, None, 'row'), may hold values from -0.09375 to 0.09375
- teacher_out: bfloat16 [128, 1024, 3584], P(('dp', 'col'), 'row'), may hold values from -0.1875 to 0.1875
- student_in: bfloat16 [2, 3584, 9216], P(None, 'dp', ('row', 'col')), may hold values from -0.09375 to 0.09375
- student_out: bfloat16 [9216, 3584], P(('row', 'col'), 'dp'), may hold values from -0.0625 to 0.0625
Outputs:
- token_loss: float32 [5120], P('dp')
- grad_down: float32 [9216, 3584], P(('row', 'col'), 'dp')
Inputs may be any that keep to these rules, and one draw needn't show every extreme that they name: `routes`: each token names 8 different experts; in each block of 40 consecutive tokens (the tokens of one index of dp and col) no expert is named more than 3 times, a bound that some block reaches.
All inputs are finite; a program needn't handle non-finite values.
Results may differ from a plain program's by a relative error of at most 0.02.
Values may be sent and summed in bfloat16 or wider, within the bound.
A program may use at most 128 MiB of HBM per device.

v0:
```python
import jax
import jax.numpy as jnp
from jax import lax
from jax.sharding import PartitionSpec as P


def on_device(tokens, routes, route_weights, teacher_in, teacher_out, student_in, student_out):
    group_cols = lax.axis_size("col")
    group_data = lax.axis_size("dp")
    experts = group_data * group_cols
    tok_rows = tokens.shape[0]
    model_width = tokens.shape[1]
    block_rows = routes.shape[0]
    top_count = routes.shape[1]
    capacity = max(2, 3 * block_rows * top_count // (2 * experts))
    col_index = lax.axis_index("col")
    local_tokens = lax.dynamic_slice_in_dim(tokens, col_index * block_rows, block_rows, 0)
    flat_routes = routes.reshape(-1)
    one_hot = (flat_routes[:, None] == jnp.arange(experts, dtype=jnp.int32)[None, :]).astype(
        jnp.int32
    )
    earlier = jnp.cumsum(one_hot, axis=0) - one_hot
    slot_index = jnp.sum(earlier * one_hot, axis=1)
    position = flat_routes * capacity + slot_index
    placing = (
        position[:, None] == jnp.arange(experts * capacity, dtype=jnp.int32)[None, :]
    ).astype(jnp.bfloat16)
    placing = jnp.sum(placing.reshape(block_rows, top_count, experts * capacity), axis=1)
    outgoing = lax.dot_general(
        placing, local_tokens, (((0,), (0,)), ((), ())), preferred_element_type=jnp.float32
    )
    outgoing = outgoing.astype(jnp.bfloat16).reshape(experts, capacity, model_width)
    arrived = lax.all_to_all(outgoing, ("dp", "col"), split_axis=0, concat_axis=0, tiled=True)
    arrived = arrived.reshape(experts * capacity, model_width)
    gate_part = jnp.dot(arrived, teacher_in[0, 0], preferred_element_type=jnp.float32)
    up_part = jnp.dot(arrived, teacher_in[0, 1], preferred_element_type=jnp.float32)
    activation = (jax.nn.silu(gate_part) * up_part).astype(jnp.bfloat16)
    partial_out = jnp.dot(activation, teacher_out[0], preferred_element_type=jnp.float32).astype(
        jnp.bfloat16
    )
    returned = lax.all_to_all(
        partial_out.reshape(experts, capacity, model_width),
        ("dp", "col"),
        split_axis=0,
        concat_axis=0,
        tiled=True,
    )
    returned = returned.reshape(experts * capacity, model_width)
    picked = jnp.take(returned, position, axis=0).reshape(block_rows, top_count, model_width)
    teacher_half = jnp.sum(route_weights[:, :, None] * picked.astype(jnp.float32), axis=1)
    inner_whole, down_whole = (
        lax.all_gather(student_in, "dp", axis=1, tiled=True),
        lax.all_gather(student_out, "dp", axis=1, tiled=True),
    )
    gate_acc = jnp.dot(tokens, inner_whole[0], preferred_element_type=jnp.float32)
    up_acc = jnp.dot(tokens, inner_whole[1], preferred_element_type=jnp.float32)
    hidden = (jax.nn.silu(gate_acc) * up_acc).astype(jnp.bfloat16)
    student_part = jnp.dot(hidden, down_whole, preferred_element_type=jnp.float32)
    placed = lax.dynamic_update_slice_in_dim(
        jnp.zeros((tok_rows, model_width), jnp.float32), teacher_half, col_index * block_rows, 0
    )
    gap_full = lax.psum((student_part - placed).astype(jnp.bfloat16), ("row", "col")).astype(
        jnp.float32
    )
    token_loss = jnp.mean(gap_full * gap_full, axis=1)
    gap_round = gap_full.astype(jnp.bfloat16)
    group_term = (
        lax.dot_general(
            hidden, gap_round, (((0,), (0,)), ((), ())), preferred_element_type=jnp.float32
        )
        / tok_rows
    )
    grad_down = lax.psum_scatter(
        group_term.astype(jnp.bfloat16), "dp", scatter_dimension=1, tiled=True
    ).astype(jnp.float32)
    return (token_loss, grad_down)


def solution(mesh):
    in_specs = (
        P("dp", None),
        P(("dp", "col"), None),
        P(("dp", "col"), None),
        P(("dp", "col"), None, None, "row"),
        P(("dp", "col"), "row", None),
        P(None, "dp", ("row", "col")),
        P(("row", "col"), "dp"),
    )
    out_specs = (P("dp"), P(("row", "col"), "dp"))
    return jax.shard_map(
        on_device, mesh=mesh, in_specs=in_specs, out_specs=out_specs, check_vma=False
    )
```

profile of v0, /device:TPU:1, one launch (start us, length us, event | category | flops | bytes accessed | tf_op | source)
XLA Modules:
  0.0 679.5 jit_solution(15036371026859774085)
XLA Ops:
  7.2 0.7 all-gather.3.cloned.1.call-update
  8.0 0.7 all-gather.5.cloned.1.call-update
  8.7 0.8 copy.18
  10.5 2.5 convolution_convert_fusion.1
  13.0 6.7 reshape.91
  19.8 125.5 %all_to_all.10 = bf16[128,3,3584]{2,1,0:T(4,128)(2,1)} all-to-all(bf16[128,3,3584]{2,1,0:T(4,128)(2,1)} %reshape.91), channel_id=1, replica_groups=mesh['dp'=32,'row'=2,'col'=4] {'dp','col'}, dimensions={0} | all-to-all | bytes 5505024 | tf_op jit(solution)/shard_map/all_to_all | solution.py:33
  145.2 7.1 %reshape.92 = bf16[384,3584]{1,0:T(8,128)(2,1)} reshape(bf16[128,3,3584]{2,1,0:T(4,128)(2,1)} %all_to_all.10) | data formatting | bytes 5505024 | tf_op jit(solution)/shard_map/reshape | solution.py:34
  152.4 4.5 fusion.7
  156.9 8.8 %convolution_convert_fusion = bf16[384,3584]{1,0:T(8,128)(2,1)} fusion(bf16[1,512,3584]{2,1,0:T(8,128)(2,1)} %param.11, bf16[384,3584]{1,0:T(8,128)(2,1)} %reshape.92, bf16[1,2,3584,512]{3,2,1,0:T(8,128)(2,1)} %param.10, f32[384,512]{1,0:T(8,128)S(1)} %fusion.7), kind=kOutput, calls=%fused_computation.7 | convolution fusion | flops 2821128192 | bytes 13631488 | tf_op jit(solution)/shard_map/dot_general | solution.py:38
  165.7 6.7 reshape.93
  172.4 10.6 %all-to-all-start.1 = ((bf16[128,3,3584]{2,1,0:T(4,128)(2,1)}), bf16[128,3,3584]{2,1,0:T(4,128)(2,1)}, u32[]{:S(2)}, u32[]{:S(2)}) async-start(bf16[128,3,3584]{2,1,0:T(4,128)(2,1)} %reshape.93), calls=%async_computation.1 | async-start | bytes 7340032 | tf_op jit(solution)/shard_map/all_to_all | solution.py:41
  183.5 106.2 %all-to-all-done.1 = bf16[128,3,3584]{2,1,0:T(4,128)(2,1)} async-done(((bf16[128,3,3584]{2,1,0:T(4,128)(2,1)}), bf16[128,3,3584]{2,1,0:T(4,128)(2,1)}, u32[]{:S(2)}, u32[]{:S(2)}) %all-to-all-start.1) | async-done | bytes 2752544 | tf_op jit(solution)/shard_map/all_to_all | solution.py:41
  289.7 7.1 %reshape.94 = bf16[384,3584]{1,0:T(8,128)(2,1)} reshape(bf16[128,3,3584]{2,1,0:T(4,128)(2,1)} %all-to-all-done.1) | data formatting | bytes 5505024 | tf_op jit(solution)/shard_map/reshape | solution.py:48
  296.8 9.0 %gather_fusion = bf16[320,3584]{1,0:T(8,128)(2,1)S(1)} fusion(bf16[384,3584]{1,0:T(8,128)(2,1)} %reshape.94, s32[1024]{0:T(1024)S(1)} %pad_clamp_fusion), kind=kCustom, calls=%fused_computation | custom fusion | bytes 4588800 | tf_op jit(solution)/shard_map/jit(_take)/gather | solution.py:49
  305.8 2.2 multiply_reduce_fusion
  308.3 5.0 fusion.2
  313.3 5.8 fusion.12
  319.1 55.9 %all-gather.5.cloned.1.call-done = bf16[1152,3584]{0,1:T(8,128)(2,1)} async-done(((bf16[1152,112]{0,1:T(8,128)(2,1)}), bf16[1152,3584]{0,1:T(8,128)(2,1)}) %all-gather.5.cloned.1.call-update) | async-done | bytes 8257552 | tf_op jit(solution)/shard_map/all_gather | solution.py:53
  375.0 7.3 %fusion.3 = bf16[160,3584]{1,0:T(8,128)(2,1)} fusion(f32[160,3584]{1,0:T(8,128)S(1)} %constant_dynamic-update-slice_fusion, bf16[160,1152]{1,0:T(8,128)(2,1)} %fusion.12, bf16[1152,3584]{0,1:T(8,128)(2,1)} %all-gather.5.cloned.1.call-done), kind=kOutput, calls=%fused_computation.10 | convolution fusion | flops 1322352640 | bytes 12066816 | tf_op jit(solution)/shard_map/dot_general | solution.py:58
  382.6 63.3 %all-reduce.3.cloned.1.call-done = bf16[160,3584]{1,0:T(8,128)(2,1)} async-done(((bf16[160,3584]{1,0:T(8,128)(2,1)}), bf16[160,3584]{1,0:T(8,128)(2,1)}) %all-reduce.3.cloned.1.call-update) | async-done | bytes 1146896 | tf_op jit(solution)/shard_map/psum | solution.py:62
  445.9 7.2 %fusion = bf16[1152,3584]{0,1:T(8,128)(2,1)} fusion(bf16[160,1152]{1,0:T(8,128)(2,1)} %fusion.12, bf16[160,3584]{1,0:T(8,128)(2,1)} %all-reduce.3.cloned.1.call-done), kind=kOutput, calls=%fused_computation.2 | convolution fusion | flops 1329463296 | bytes 9773056 | tf_op jit(solution)/shard_map/dot_general | solution.py:68
  453.1 1.2 copy-done.1
  455.2 216.0 %reduce-scatter.2.cloned.1.call-done = bf16[1152,112]{0,1:T(8,128)(2,1)} async-done(((bf16[1152,3584]{0,1:T(8,128)(2,1)}), bf16[1152,112]{0,1:T(8,128)(2,1)}) %reduce-scatter.2.cloned.1.call-update) | async-done | bytes 258064 | tf_op jit(solution)/shard_map/reduce_scatter | solution.py:73
  671.2 1.8 convert_element_type.48
  (33 shorter events, 3.0 us)
Async XLA Ops:
  7.2 3.3 copy-start
  7.2 301.1 %all-gather.3.cloned.1.call-start = ((), (), s32[]{:S(2)}) async-start(), calls=%async_computation.3 | async-start | bytes 17031168 | tf_op jit(solution)/shard_map/all_gather | solution.py:52
  7.9 367.1 %all-gather.5.cloned.1.call-start = ((), (), s32[]{:S(2)}) async-start(), calls=%async_computation.4 | async-start | bytes 8515584 | tf_op jit(solution)/shard_map/all_gather | solution.py:53
  172.4 11.0 %copy-start.2 = (f32[40,8]{0,1:T(8,128)S(1)}, f32[40,8]{0,1:T(8,128)}, u32[]{:S(2)}) copy-start(f32[40,8]{0,1:T(8,128)} %param.9) | copy-start | bytes 3844
  172.4 117.2 %all-to-all-start.1 = ((bf16[128,3,3584]{2,1,0:T(4,128)(2,1)}), bf16[128,3,3584]{2,1,0:T(4,128)(2,1)}, u32[]{:S(2)}, u32[]{:S(2)}) async-start(bf16[128,3,3584]{2,1,0:T(4,128)(2,1)} %reshape.93), calls=%async_computation.1 | async-start | bytes 7340032 | tf_op jit(solution)/shard_map/all_to_all | solution.py:41
  183.1 262.8 %all-reduce.3.cloned.1.call-start = ((), (), s32[]{:S(2)}) async-start(), calls=%async_computation.5 | async-start | bytes 2293760 | tf_op jit(solution)/shard_map/psum | solution.py:62
  382.3 288.9 %reduce-scatter.2.cloned.1.call-start = ((), (), s32[]{:S(2)}) async-start(), calls=%async_computation.6 | async-start | bytes 8515584 | tf_op jit(solution)/shard_map/reduce_scatter | solution.py:73
  453.1 1.3 copy-start.1
Sparse Core Ops, SparseCore 0:
  10.6 258.9 all-gather.2
  272.2 102.7 all-gather.4
  382.4 63.3 all-reduce.2
  453.2 217.9 reduce-scatter.1
where the time goes:
time: 684 us; the launch traced here: 679 us
  waiting for transfers between devices  443 us (65%)
  blocking collectives  125 us (18%)
  matrix products  41.2 us (6%)
  local copies, waits for them, and re-layouts  39.3 us (6%)
  between operations  13.9 us (2%)
  starting transfers between devices  11.2 us (2%)
    reduce_scatter x1, waiting for transfers between devices, on_device(): lax.psum_scatter(group_term.astype(jnp.bfloat16), 'dp', scatter_dimension...  216 us
    all_to_all x1, blocking collectives, on_device(): lax.all_to_all(outgoing, ('dp', 'col'), split_axis=0, concat_axis=0, tile...  125 us
    all_to_all x1, waiting for transfers between devices, on_device(): lax.all_to_all(partial_out.reshape(experts, capacity, model_width), ('dp'...  106 us
    psum x1, waiting for transfers between devices, on_device(): lax.psum((student_part - placed).astype(jnp.bfloat16), ('row', 'col'))  63.3 us
    all_gather x1, waiting for transfers between devices, on_device(): lax.all_gather(student_out, 'dp', axis=1, tiled=True)  55.9 us
  transfers between devices with their start and end apart: 5, of which 4 were waited for; matrix products, arithmetic and copies ran while one was open for 10% of the time, Pallas kernels for 0%

commit v1 on v0

v1 whole, which is shorter than its diff:
```python
import jax
import jax.numpy as jnp
from jax import lax
from jax.sharding import Mesh, PartitionSpec as P

NX = 4
F32 = jnp.float32
BF = jnp.bfloat16


def split_mesh(mesh):
    dp, row, col = mesh.devices.shape
    return Mesh(mesh.devices.reshape(dp // NX, NX, row, col), ("z", "x", "row", "col"))


def dot(a, b, dims):
    return lax.dot_general(a, b, (dims, ((), ())), preferred_element_type=F32)


def pad_lanes(a):
    lanes = a.shape[-1]
    wide = -(-lanes // 128) * 128
    return jnp.pad(a, [(0, 0)] * (a.ndim - 1) + [(0, wide - lanes)])


def routing(routes, weights, plane, ny, cap):
    nz, block, _ = routes.shape
    experts = NX * ny
    local = routes - plane * experts
    ids = jnp.arange(experts, dtype=jnp.int32)
    hit = local[..., None] == ids
    named = jnp.any(hit, axis=2)
    weight = jnp.sum(jnp.where(hit, weights[..., None], 0.0), axis=2)
    count = named.astype(jnp.int32)
    slot = jnp.cumsum(count, axis=1) - count
    place = named[..., None] & (slot[..., None] == jnp.arange(cap, dtype=jnp.int32))
    same = jnp.eye(nz, dtype=bool)
    full = place[:, :, :, None, :] & same[:, None, None, :, None]
    combine = jnp.where(full, weight[:, :, :, None, None], 0.0)
    rows = experts * nz * cap
    return full.reshape(nz * block, rows).astype(BF), combine.reshape(nz * block, rows)


def on_device(tokens, routes, route_weights, teacher_in, teacher_out, student_in, student_out):
    nz, nr, ny = lax.axis_size("z"), lax.axis_size("row"), lax.axis_size("col")
    z, x, r, y = (lax.axis_index(a) for a in ("z", "x", "row", "col"))
    tok, width = tokens.shape
    block, top = routes.shape
    blk = student_in.shape[1]
    ff = student_in.shape[2]
    sub = ff // NX
    half = width // nr
    plane_experts = NX * ny
    cap = max(2, 3 * block * top // (2 * nz * plane_experts))
    blocks = nz * NX

    parts = jnp.concatenate([jnp.swapaxes(student_in, 1, 2), student_out[None]], axis=0)
    parts = pad_lanes(parts)
    lanes = parts.shape[-1]
    wide = blocks * lanes
    parts = lax.all_to_all(parts.reshape(3, NX, sub, lanes), "x", split_axis=1, concat_axis=1, tiled=True)
    parts = jnp.swapaxes(parts, 1, 2).reshape(3, sub, NX * lanes)
    inner = lax.all_gather(parts[:2], "z", axis=2, tiled=True)
    outer = lax.all_gather(parts[2], "z", axis=1, tiled=True)

    padded = pad_lanes(tokens.reshape(tok, blocks, blk)).reshape(tok, wide)
    plane_tokens = lax.all_gather(padded, "x", axis=0, tiled=True)

    mine = lax.dynamic_slice(tokens, (y * block, r * half), (block, half))
    column = lax.all_gather(mine, "z", axis=0, tiled=True)
    routes_z = lax.all_gather(routes, "z")
    weights_z = lax.all_gather(route_weights, "z")
    place, combine = routing(routes_z, weights_z, z, ny, cap)
    slots = nz * cap
    outgoing = dot(place, column, ((0,), (0,))).astype(BF).reshape(plane_experts, slots, half)
    arrived = lax.all_to_all(outgoing, ("x", "col"), split_axis=0, concat_axis=0, tiled=True)
    arrived = lax.all_gather(arrived.reshape(plane_experts * slots, half), "row", axis=1, tiled=True)
    gate = dot(arrived, teacher_in[0, 0], ((1,), (0,)))
    up = dot(arrived, teacher_in[0, 1], ((1,), (0,)))
    act = (jax.nn.silu(gate) * up).astype(BF)
    part = dot(act, teacher_out[0], ((1,), (0,))).astype(BF)
    both = lax.all_to_all(part.reshape(-1, nr, half), "row", split_axis=1, concat_axis=1, tiled=True)
    summed = jnp.sum(both.astype(F32), axis=1).astype(BF).reshape(plane_experts, slots, half)
    back = lax.all_to_all(summed, ("x", "col"), split_axis=0, concat_axis=0, tiled=True)
    back = back.reshape(plane_experts * slots, half)
    high = combine.astype(BF)
    low = (combine - high.astype(F32)).astype(BF)
    teacher = dot(high, back, ((1,), (0,))) + dot(low, back, ((1,), (0,)))
    teacher = lax.psum_scatter(teacher.astype(BF).reshape(nz, block, half), "z", scatter_dimension=0, tiled=False)
    teacher = pad_lanes(teacher.reshape(block, blocks // nr, blk)).reshape(block, wide // nr)

    gate = dot(plane_tokens, inner[0], ((1,), (1,)))
    up = dot(plane_tokens, inner[1], ((1,), (1,)))
    hidden = (jax.nn.silu(gate) * up).astype(BF)
    hidden_both = lax.all_gather(hidden, "row", axis=1, tiled=True)
    outer_both = lax.all_to_all(outer.reshape(sub, nr, wide // nr), "row", split_axis=1, concat_axis=0, tiled=True)
    outer_both = outer_both.reshape(nr * sub, wide // nr)
    y_part = dot(hidden_both, outer_both, ((1,), (0,))).astype(BF)
    student = lax.all_to_all(y_part.reshape(plane_experts, block, -1), ("x", "col"), split_axis=0, concat_axis=0, tiled=True)
    student = jnp.sum(student.astype(F32), axis=0)
    gap = student - teacher.astype(F32)
    loss = lax.psum(jnp.sum(gap * gap, axis=1), "row") / width
    token_loss = lax.all_gather(loss, "col", axis=0, tiled=True)
    gap_round = lax.all_gather(gap.astype(BF), ("x", "col"), axis=0, tiled=True)
    term = (dot(hidden_both, gap_round, ((0,), (0,))) / tok).astype(BF)
    term = lax.all_to_all(term.reshape(nr, sub, wide // nr), "row", split_axis=0, concat_axis=2, tiled=True)
    term = term.reshape(sub, nz, NX * lanes).swapaxes(0, 1)
    grad = lax.psum_scatter(term, "z", scatter_dimension=0, tiled=False)
    grad = grad.reshape(sub, NX, lanes)
    grad = lax.all_to_all(grad, "x", split_axis=1, concat_axis=0, tiled=True)
    grad = grad.reshape(ff, lanes)[:, :blk].astype(F32)
    return token_loss, grad


def solution(mesh):
    dp = ("z", "x")
    in_specs = (
        P(dp, None),
        P(dp + ("col",), None),
        P(dp + ("col",), None),
        P(dp + ("col",), None, None, "row"),
        P(dp + ("col",), "row", None),
        P(None, dp, ("row", "col")),
        P(("row", "col"), dp),
    )
    out_specs = (P(dp), P(("row", "col"), dp))
    return jax.shard_map(
        on_device, mesh=split_mesh(mesh), in_specs=in_specs, out_specs=out_specs, check_vma=False
    )
```

time: 684 us -> 464 us (0.68)
  waiting for transfers between devices: 443 us -> 237 us
  blocking collectives: 125 us -> 109 us
  starting transfers between devices: 11.2 us -> 24.8 us
  local copies, waits for them, and re-layouts: 39.3 us -> 27 us
    reduce_scatter x1 -> x2, waiting for transfers between devices: 216 us -> 68 us  [the longest x1 34.2 us: on_device(): lax.psum_scatter(teacher.astype(BF).reshape(nz, block, half), 'z', scatte...]
    all_gather x2 -> x6, waiting for transfers between devices: 55.9 us -> 169 us  [the longest x1 62 us: on_device(): inner = lax.all_gather(parts[:2], 'z', axis=2, tiled=True)]
    all_to_all x1 -> x4, waiting for transfers between devices: 106 us -> 0.01 us  [the longest x1 0.01 us: on_device(): lax.all_to_all(summed, ('x', 'col'), split_axis=0, concat_axis=0, tiled=T...]
    all_to_all x1 -> x4, blocking collectives: 125 us -> 51.6 us  [the longest x1 21.7 us: on_device(): lax.all_to_all(outgoing, ('x', 'col'), split_axis=0, concat_axis=0, tiled...]
    psum x1 -> x0, waiting for transfers between devices: 63.3 us -> none  [on_device(): lax.psum((student_part - placed).astype(jnp.bfloat16), ('row', 'col'))]
    all_gather x0 -> x3, blocking collectives: none -> 45.8 us  [the longest x1 22.9 us: on_device(): routes_z = lax.all_gather(routes, 'z')]
    reshape x5, local copies, waits for them, and re-layouts: 27.8 us -> 7.58 us  [the longest x1 3.33 us: on_device(): outer.reshape(sub, nr, wide // nr)]
    all_to_all x1 -> x4, starting transfers between devices: 10.6 us -> 24.4 us  [the longest x1 10.1 us: on_device(): lax.all_to_all(outer.reshape(sub, nr, wide // nr), 'row', split_axis=1, c...]
  transfers between devices with their start and end apart: 5 -> 12, of which waited for: 4 -> 7; matrix products, arithmetic and copies ran while one was open for 10% -> 9% of each run, Pallas kernels for 0% -> 0%
where the time goes in v1:
time: 464 us; the launch traced here: 456 us
  waiting for transfers between devices  237 us (51%)
  blocking collectives  109 us (23%)
  matrix products  36.9 us (8%)
  local copies, waits for them, and re-layouts  27 us (6%)
  starting transfers between devices  24.8 us (5%)
  between operations  15.1 us (3%)
  other arithmetic  7 us (2%)
    all_gather x1, waiting for transfers between devices, on_device(): inner = lax.all_gather(parts[:2], 'z', axis=2, tiled=True)  62 us
    all_gather x1, waiting for transfers between devices, on_device(): gap_round = lax.all_gather(gap.astype(BF), ('x', 'col'), axis=0, tiled=True)  53.4 us
    dot_general x9, matrix products, dot(): return lax.dot_general(a, b, (dims, ((), ())), preferred_element_type=F32)  36.9 us
    all_gather x1, waiting for transfers between devices, on_device(): plane_tokens = lax.all_gather(padded, 'x', axis=0, tiled=True)  36.2 us
    reduce_scatter x1, waiting for transfers between devices, on_device(): lax.psum_scatter(teacher.astype(BF).reshape(nz, block, half), 'z', scatte...  34.2 us
    reduce_scatter x1, waiting for transfers between devices, on_device(): grad = lax.psum_scatter(term, 'z', scatter_dimension=0, tiled=False)  33.8 us
    all_gather x1, blocking collectives, on_device(): routes_z = lax.all_gather(routes, 'z')  22.9 us
    all_to_all x1, blocking collectives, on_device(): lax.all_to_all(outgoing, ('x', 'col'), split_axis=0, concat_axis=0, tiled...  21.7 us
  transfers between devices with their start and end apart: 12, of which 7 were waited for; matrix products, arithmetic and copies ran while one was open for 9% of the time, Pallas kernels for 0%

profile of v1, /device:TPU:1, one launch (start us, length us, event | category | flops | bytes accessed | tf_op | source)
XLA Modules:
  0.0 456.3 jit_solution(17836005755417253970)
XLA Ops:
  8.9 22.9 %all-gather.2 = s32[8,40,8]{1,2,0:T(8,128)S(1)} all-gather(s32[1,40,8]{1,2,0:T(8,128)} %bitcast.139), channel_id=2, replica_groups=mesh['z'=8,'x'=4,'row'=2,'col'=4] {'z'}, dimensions={0}, use_global_device_ids=true | all-gather | bytes 11520 | tf_op jit(solution)/shard_map/all_gather | solution.py:71
  33.1 15.8 %all-gather.17.cloned.1.call-done = bf16[320,1792]{1,0:T(8,128)(2,1)} async-done(((bf16[40,1792]{1,0:T(8,128)(2,1)}), bf16[320,1792]{1,0:T(8,128)(2,1)}) %all-gather.17.cloned.1.call-update) | async-done | bytes 1146896 | tf_op jit(solution)/shard_map/all_gather | solution.py:70
  51.1 21.7 %all_to_all.70 = bf16[16,24,1792]{2,1,0:T(8,128)(2,1)} all-to-all(bf16[16,24,1792]{2,1,0:T(8,128)(2,1)S(1)} %bitcast.121), channel_id=1, replica_groups=mesh['z'=8,'x'=4,'row'=2,'col'=4] {'x','col'}, dimensions={0} | all-to-all | bytes 2752512 | tf_op jit(solution)/shard_map/all_to_all | solution.py:76
  73.8 11.4 %all_to_all.71 = bf16[3,4,288,128]{3,2,0,1:T(8,128)(2,1)S(1)} all-to-all(bf16[3,4,288,128]{3,2,0,1:T(8,128)(2,1)S(1)} %copy.42), channel_id=1, replica_groups=mesh['z'=8,'x'=4,'row'=2,'col'=4] {'x'}, dimensions={1} | all-to-all | bytes 1769472 | tf_op jit(solution)/shard_map/all_to_all | solution.py:61
  92.0 5.4 %fusion.3 = f32[384,512]{1,0:T(8,128)} fusion(bf16[384,3584]{1,0:T(8,128)(2,1)} %all-gather.19.cloned.1.call-done, bf16[1,2,3584,512]{3,2,1,0:T(8,128)(2,1)} %param.10), kind=kOutput, calls=%fused_computation.6 | convolution fusion | flops 1409286144 | bytes 7208960 | tf_op jit(solution)/shard_map/dot_general | solution.py:17
  97.4 7.3 %convolution_convert_fusion = bf16[384,3584]{1,0:T(8,128)(2,1)S(1)} fusion(bf16[1,512,3584]{2,1,0:T(8,128)(2,1)} %param.11, bf16[384,3584]{1,0:T(8,128)(2,1)} %all-gather.19.cloned.1.call-done, bf16[1,2,3584,512]{3,2,1,0:T(8,128)(2,1)} %param.10, f32[384,512]{1,0:T(8,128)} %fusion.3), kind=kOutput, calls=%fused_computation | convolution fusion | flops 2821128192 | bytes 13631488 | tf_op jit(solution)/shard_map/dot_general | solution.py:17
  104.9 12.1 %all_to_all.72 = bf16[384,2,1792]{2,0,1:T(8,128)(2,1)S(1)} all-to-all(bf16[384,2,1792]{2,0,1:T(8,128)(2,1)S(1)} %bitcast.115), channel_id=1, replica_groups=mesh['z'=8,'x'=4,'row'=2,'col'=4] {'row'}, dimensions={1} | all-to-all | bytes 5505024 | tf_op jit(solution)/shard_map/all_to_all | solution.py:82
  119.0 3.7 all-to-all-start.5
  122.7 20.1 %all-gather.3 = f32[8,40,8]{1,2,0:T(8,128)S(1)} all-gather(f32[1,40,8]{1,2,0:T(8,128)S(1)} %bitcast.140), channel_id=3, replica_groups=mesh['z'=8,'x'=4,'row'=2,'col'=4] {'z'}, dimensions={0}, use_global_device_ids=true | all-gather | bytes 11520 | tf_op jit(solution)/shard_map/all_gather | solution.py:72
  144.7 3.3 copy.69
  148.0 10.1 %all-to-all-start.1 = ((bf16[288,2,2048]{2,0,1:T(8,128)(2,1)}), bf16[288,2,2048]{2,0,1:T(8,128)(2,1)}, u32[]{:S(2)}, u32[]{:S(2)}) async-start(bf16[288,2,2048]{2,0,1:T(8,128)(2,1)} %bitcast.116), calls=%async_computation.1 | async-start | bytes 4718592 | tf_op jit(solution)/shard_map/all_to_all | solution.py:96
  160.3 36.2 %all-gather.11.cloned.1.call-done = bf16[640,4096]{1,0:T(8,128)(2,1)} async-done(((bf16[160,4096]{1,0:T(8,128)(2,1)}), bf16[640,4096]{1,0:T(8,128)(2,1)}) %all-gather.11.cloned.1.call-update) | async-done | bytes 5242896 | tf_op jit(solution)/shard_map/all_gather | solution.py:67
  196.5 62.0 %all-gather.13.cloned.1.call-done = bf16[2,288,4096]{2,1,0:T(8,128)(2,1)} async-done(((bf16[2,288,512]{2,1,0:T(8,128)(2,1)}), bf16[2,288,4096]{2,1,0:T(8,128)(2,1)}) %all-gather.13.cloned.1.call-update) | async-done | bytes 4718608 | tf_op jit(solution)/shard_map/all_gather | solution.py:63
  258.5 5.4 %fusion.9 = f32[640,288]{0,1:T(8,128)S(1)} fusion(bf16[640,4096]{1,0:T(8,128)(2,1)} %all-gather.11.cloned.1.call-done, bf16[2,288,4096]{2,1,0:T(8,128)(2,1)} %all-gather.13.cloned.1.call-done), kind=kOutput, calls=%fused_computation.19 | convolution fusion | flops 1509949440 | bytes 8339456 | tf_op jit(solution)/shard_map/dot_general | solution.py:17
  269.5 5.7 %convolution_convert_fusion.1 = bf16[640,2048]{1,0:T(8,128)(2,1)} fusion(bf16[640,576]{0,1:T(8,128)(2,1)} %all_gather.38, bf16[576,2048]{1,0:T(8,128)(2,1)} %bitcast.8), kind=kOutput, calls=%fused_computation.10 | convolution fusion | flops 1511260160 | bytes 5718016 | tf_op jit(solution)/shard_map/dot_general | solution.py:17
  275.1 6.6 %all-to-all-start.2 = ((bf16[16,40,2048]{2,1,0:T(8,128)(2,1)}), bf16[16,40,2048]{2,1,0:T(8,128)(2,1)}, u32[]{:S(2)}, u32[]{:S(2)}) async-start(bf16[16,40,2048]{2,1,0:T(8,128)(2,1)} %bitcast.130), calls=%async_computation.2 | async-start | bytes 5242880 | tf_op jit(solution)/shard_map/all_to_all | solution.py:99
  285.0 34.2 %reduce-scatter.3.cloned.1.call-done = bf16[1,40,1792]{2,1,0:T(8,128)(2,1)} async-done(((bf16[8,40,1792]{2,1,0:T(8,128)(2,1)}), bf16[1,40,1792]{2,1,0:T(8,128)(2,1)}) %reduce-scatter.3.cloned.1.call-update) | async-done | bytes 143376 | tf_op jit(solution)/shard_map/reduce_scatter | solution.py:89
  323.6 53.4 %all-gather.21.cloned.1.call-done = bf16[640,2048]{1,0:T(8,128)(2,1)} async-done(((bf16[40,2048]{1,0:T(8,128)(2,1)}), bf16[640,2048]{1,0:T(8,128)(2,1)}) %all-gather.21.cloned.1.call-update) | async-done | bytes 2621456 | tf_op jit(solution)/shard_map/all_gather | solution.py:104
  377.0 3.7 multiply_convert_fusion
  380.8 6.4 %all_to_all.73 = bf16[2,288,2048]{2,1,0:T(8,128)(2,1)S(1)} all-to-all(bf16[2,288,2048]{2,1,0:T(8,128)(2,1)S(1)} %bitcast.133), channel_id=1, replica_groups=mesh['z'=8,'x'=4,'row'=2,'col'=4] {'row'}, dimensions={0} | all-to-all | bytes 4718592 | tf_op jit(solution)/shard_map/all_to_all | solution.py:106
  391.8 3.9 copy.52
  399.8 33.8 %reduce-scatter.5.cloned.1.call-done = bf16[1,288,512]{2,1,0:T(8,128)(2,1)} async-done(((bf16[8,288,512]{2,1,0:T(8,128)(2,1)}), bf16[1,288,512]{2,1,0:T(8,128)(2,1)}) %reduce-scatter.5.cloned.1.call-update) | async-done | bytes 294928 | tf_op jit(solution)/shard_map/reduce_scatter | solution.py:108
  435.4 4.0 all-to-all-start.7
  439.5 8.9 %all-reduce.3 = f32[160]{0:T(256)} all-reduce(f32[160]{0:T(256)S(1)} %multiply_dynamic-update-slice_fusion), channel_id=1, replica_groups=mesh['z'=8,'x'=4,'row'=2,'col'=4] {'col'}, use_global_device_ids=true, to_apply=%add.3 | all-reduce | flops 160 | bytes 1280
  (91 shorter events, 43.1 us)
Async XLA Ops:
  7.2 41.8 %all-gather.17.cloned.1.call-start = ((), (), s32[]{:S(2)}) async-start(), calls=%async_computation.13 | async-start | bytes 1290240 | tf_op jit(solution)/shard_map/all_gather | solution.py:70
  8.8 83.2 %all-gather.19.cloned.1.call-start = ((), (), s32[]{:S(2)}) async-start(), calls=%async_computation.14 | async-start | bytes 4128768 | tf_op jit(solution)/shard_map/all_gather | solution.py:77
  51.0 21.8 %copy-start.4 = (bf16[1152,112]{0,1:T(8,128)(2,1)S(1)}, bf16[1152,112]{0,1:T(8,128)(2,1)}, u32[]{:S(2)}) copy-start(bf16[1152,112]{0,1:T(8,128)(2,1)} %param.13) | copy-start | bytes 774148
  51.1 22.0 %copy-start.3 = (bf16[2,112,1152]{2,1,0:T(8,128)(2,1)S(1)}, bf16[2,112,1152]{2,1,0:T(8,128)(2,1)}, u32[]{:S(2)}) copy-start(bf16[2,112,1152]{2,1,0:T(8,128)(2,1)} %param.12) | copy-start | bytes 1548292
  72.8 71.9 %all-gather.15.cloned.1.call-start = ((), (), s32[]{:S(2)}) async-start(), calls=%async_computation.12 | async-start | bytes 2654208 | tf_op jit(solution)/shard_map/all_gather | solution.py:64
  73.7 12.5 %copy-start.1 = (bf16[160,3584]{1,0:T(8,128)(2,1)S(1)}, bf16[160,3584]{1,0:T(8,128)(2,1)}, u32[]{:S(2)}) copy-start(bf16[160,3584]{1,0:T(8,128)(2,1)} %param.7) | copy-start | bytes 3440644
  86.2 110.4 %all-gather.11.cloned.1.call-start = ((), (), s32[]{:S(2)}) async-start(), calls=%async_computation.10 | async-start | bytes 6553600 | tf_op jit(solution)/shard_map/all_gather | solution.py:67
  90.0 168.5 %all-gather.13.cloned.1.call-start = ((), (), s32[]{:S(2)}) async-start(), calls=%async_computation.11 | async-start | bytes 5308416 | tf_op jit(solution)/shard_map/all_gather | solution.py:63
  117.0 5.7 %copy-start.5 = (f32[40,8]{0,1:T(8,128)S(1)}, f32[40,8]{0,1:T(8,128)}, u32[]{:S(2)}) copy-start(f32[40,8]{0,1:T(8,128)} %param.9) | copy-start | bytes 3844
  119.0 29.1 %all-to-all-start.5 = ((bf16[16,24,1792]{2,1,0:T(8,128)(2,1)}), bf16[16,24,1792]{2,1,0:T(8,128)(2,1)S(1)}, u32[]{:S(2)}, u32[]{:S(2)}) async-start(bf16[16,24,1792]{2,1,0:T(8,128)(2,1)} %bitcast.120), calls=%async_computation.5 | async-start | bytes 2752512 | tf_op jit(solution)/shard_map/all_to_all | solution.py:84
  148.0 10.1 %copy-start = (bf16[16,24,1792]{2,1,0:T(8,128)(2,1)}, bf16[16,24,1792]{2,1,0:T(8,128)(2,1)S(1)}, u32[]{:S(2)}) copy-start(bf16[16,24,1792]{2,1,0:T(8,128)(2,1)S(1)} %all-to-all-done.5) | copy-start | bytes 4128772
  148.0 121.5 %all-to-all-start.1 = ((bf16[288,2,2048]{2,0,1:T(8,128)(2,1)}), bf16[288,2,2048]{2,0,1:T(8,128)(2,1)}, u32[]{:S(2)}, u32[]{:S(2)}) async-start(bf16[288,2,2048]{2,0,1:T(8,128)(2,1)} %bitcast.116), calls=%async_computation.1 | async-start | bytes 4718592 | tf_op jit(solution)/shard_map/all_to_all | solution.py:96
  258.5 5.4 %copy-start.6 = (bf16[640,4096]{1,0:T(8,128)(2,1)S(1)}, bf16[640,4096]{1,0:T(8,128)(2,1)}, u32[]{:S(2)}) copy-start(bf16[640,4096]{1,0:T(8,128)(2,1)} %all-gather.11.cloned.1.call-done) | copy-start | bytes 15728644
  258.5 6.1 %copy-start.7 = (bf16[2,288,4096]{2,1,0:T(8,128)(2,1)S(1)}, bf16[2,288,4096]{2,1,0:T(8,128)(2,1)}, u32[]{:S(2)}) copy-start(bf16[2,288,4096]{2,1,0:T(8,128)(2,1)} %all-gather.13.cloned.1.call-done) | copy-start | bytes 14155780
  275.1 45.3 %all-to-all-start.2 = ((bf16[16,40,2048]{2,1,0:T(8,128)(2,1)}), bf16[16,40,2048]{2,1,0:T(8,128)(2,1)}, u32[]{:S(2)}, u32[]{:S(2)}) async-start(bf16[16,40,2048]{2,1,0:T(8,128)(2,1)} %bitcast.130), calls=%async_computation.2 | async-start | bytes 5242880 | tf_op jit(solution)/shard_map/all_to_all | solution.py:99
  281.7 37.5 %reduce-scatter.3.cloned.1.call-start = ((), (), s32[]{:S(2)}) async-start(), calls=%async_computation.15 | async-start | bytes 1290240 | tf_op jit(solution)/shard_map/reduce_scatter | solution.py:89
  285.0 92.0 %copy-start.2 = (bf16[640,576]{0,1:T(8,128)(2,1)S(1)}, bf16[640,576]{0,1:T(8,128)(2,1)}, u32[]{:S(2)}) copy-start(bf16[640,576]{0,1:T(8,128)(2,1)} %all_gather.38) | copy-start | bytes 2211844
  285.0 92.0 %all-gather.21.cloned.1.call-start = ((), (), s32[]{:S(2)}) async-start(), calls=%async_computation.16 | async-start | bytes 2785280 | tf_op jit(solution)/shard_map/all_gather | solution.py:104
  323.6 110.1 %reduce-scatter.5.cloned.1.call-start = ((), (), s32[]{:S(2)}) async-start(), calls=%async_computation.17 | async-start | bytes 2654208 | tf_op jit(solution)/shard_map/reduce_scatter | solution.py:108
  391.8 3.9 copy-start.8
  435.4 13.0 %all-to-all-start.7 = ((bf16[288,4,128]{2,0,1:T(8,128)(2,1)}), bf16[288,4,128]{2,0,1:T(8,128)(2,1)S(1)}, u32[]{:S(2)}, u32[]{:S(2)}) async-start(bf16[288,4,128]{2,0,1:T(8,128)(2,1)} %copy.53), calls=%async_computation.9 | async-start | bytes 589824 | tf_op jit(solution)/shard_map/all_to_all | solution.py:110
Sparse Core Ops, SparseCore 0:
  10.4 38.5 all-gather.16
  72.9 19.0 all-gather.18
  94.4 39.2 all-gather.14
  135.3 61.1 all-gather.10
  198.2 60.2 all-gather.12
  285.1 34.1 reduce-scatter.2
  323.7 53.3 all-gather.20
  395.8 37.7 reduce-scatter.4

commit v2 on v1

v2 whole, which is shorter than its diff:
```python
import functools

import jax
import jax.numpy as jnp
from jax import lax
from jax.experimental import pallas as pl
from jax.experimental.pallas import tpu as pltpu
from jax.sharding import Mesh, PartitionSpec as P

NX = 4
MESH = pl.DeviceIdType.MESH
F32 = jnp.float32
BF = jnp.bfloat16


def split_mesh(mesh):
    dp, row, col = mesh.devices.shape
    return Mesh(mesh.devices.reshape(dp // NX, NX, row, col), ("z", "x", "row", "col"))


def dot(a, b, dims):
    return lax.dot_general(a, b, (dims, ((), ())), preferred_element_type=F32)


def pad_lanes(a):
    lanes = a.shape[-1]
    wide = -(-lanes // 128) * 128
    return jnp.pad(a, [(0, 0)] * (a.ndim - 1) + [(0, wide - lanes)])


def here():
    return tuple(lax.axis_index(a) for a in ("z", "x", "row", "col"))


def remote(src, dst, send, recv, device):
    return pltpu.make_async_remote_copy(
        src_ref=src, dst_ref=dst, send_sem=send, recv_sem=recv, device_id=device, device_id_type=MESH
    )


def greet(devices):
    barrier = pltpu.get_barrier_semaphore()
    for device in devices:
        pl.semaphore_signal(barrier, inc=1, device_id=device, device_id_type=MESH)
    pl.semaphore_wait(barrier, len(devices))


def lanes_at(start, size):
    return pl.ds(pl.multiple_of(start * size, size), size)


def kernel_call(body, number, outs, scratch, *args):
    whole = pl.BlockSpec(memory_space=pltpu.VMEM)
    return pl.pallas_call(
        body,
        out_shape=outs,
        in_specs=[whole] * len(args),
        out_specs=[whole] * len(outs),
        scratch_shapes=scratch,
        compiler_params=pltpu.CompilerParams(
            collective_id=number, has_side_effects=True, vmem_limit_bytes=48 * 1024 * 1024
        ),
    )(*args)


def dma(*shape):
    return pltpu.SemaphoreType.DMA(shape)


def plane_steps(ny):
    steps = [(dx, dy) for dx in range(NX) for dy in range(ny) if dx or dy]
    far = lambda s: min(s[0], NX - s[0]) + min(s[1], ny - s[1])
    return sorted(steps, key=far, reverse=True)


def weights_kernel(parts, inner, outer, send, recv, own):
    z, x, r, y = here()
    greet([(z, (x + d) % NX, r, y) for d in (1, 2, 3)])
    copies = []
    for d in (2, 1, 3):
        to = (x + d) % NX
        device = (z, to, r, y)
        for kind in (0, 1, 2):
            dst = outer.at[:, lanes_at(x, 128)] if kind == 2 else inner.at[kind, :, lanes_at(x, 128)]
            copies.append(remote(parts.at[kind, to], dst, send.at[d - 1, kind], recv.at[d - 1, kind], device))
            copies[-1].start()
    local = []
    for kind in (0, 1, 2):
        dst = outer.at[:, lanes_at(x, 128)] if kind == 2 else inner.at[kind, :, lanes_at(x, 128)]
        local.append(pltpu.make_async_copy(parts.at[kind, x], dst, own.at[kind]))
        local[-1].start()
    for copy in copies + local:
        copy.wait()


def tokens_kernel(nz, padded, mine, meta, plane, column, metas, xs, xr, ys, yr, cs, cr, zs, zr, ms, mr, own):
    z, x, r, y = here()
    up, down = (z + 1) % nz, (z + nz - 1) % nz
    ny = lax.axis_size("col")
    north, south = (y + 1) % ny, (y + ny - 1) % ny
    sibling = (z, x, 1 - r, y)
    greet(
        [(z, (x + d) % NX, r, y) for d in (1, 2, 3)]
        + [(z, x, r, north), (z, x, r, south), (up, x, r, y), (down, x, r, y), sibling]
    )
    rows, wide = padded.shape
    high, span = rows // 2, wide // 2
    quarter = span // 2
    mine_rows = pl.ds(pl.multiple_of(r * high, high), high)
    parity = y % 2
    held = lanes_at(parity, span)
    started = []

    def go(copy):
        copy.start()
        started.append(copy)
        return copy

    local = [
        pltpu.make_async_copy(padded, plane.at[x], own.at[0]),
        pltpu.make_async_copy(mine, column.at[z], own.at[1]),
        pltpu.make_async_copy(meta, metas.at[z], own.at[2]),
    ]
    for copy in local:
        copy.start()

    def z_step(s):
        half = mine.shape[1] // 2
        a, b = (z + nz - s + 1) % nz, (z + s - 1) % nz
        if s == 1:
            one, two, three, four = mine, mine, meta, meta
        else:
            one, two, three, four = column.at[a], column.at[b], metas.at[a], metas.at[b]
        to_a, to_b = column.at[a], column.at[b]
        if s == nz // 2:
            low, top = pl.ds(0, half), pl.ds(half, half)
            one, to_a, two, to_b = column.at[a, :, low], column.at[a, :, low], column.at[b, :, top], column.at[b, :, top]
        out = [
            go(remote(one, to_a, zs.at[0, s - 1], zr.at[0, s - 1], (up, x, r, y))),
            go(remote(two, to_b, zs.at[1, s - 1], zr.at[1, s - 1], (down, x, r, y))),
            go(remote(three, metas.at[a], ms.at[0, s - 1], mr.at[0, s - 1], (up, x, r, y))),
        ]
        if s < nz // 2:
            out.append(go(remote(four, metas.at[b], ms.at[1, s - 1], mr.at[1, s - 1], (down, x, r, y))))
        return out

    def arrived(copies):
        for copy in copies:
            copy.wait_recv()

    ring = z_step(1)
    from_x = {}
    for d in (2, 1, 3):
        device = (z, (x + d) % NX, r, y)
        from_x[d] = go(remote(padded.at[mine_rows, held], plane.at[x, mine_rows, held], xs.at[d - 1], xr.at[d - 1], device))
    turn = 0
    from_sib, from_y = [], []
    for d in (1, 3, 2):
        arrived(ring)
        turn += 1
        ring = z_step(turn + 1)
        from_x[d].wait_recv()
        source = (x + NX - d) % NX
        for side, device in ((0, (z, x, r, north)), (1, (z, x, r, south))):
            piece = plane.at[source, mine_rows, lanes_at(parity * 2 + side, quarter)]
            from_y.append((d, side, go(remote(piece, piece, ys.at[side, d - 1], yr.at[side, d - 1], device))))
        piece = plane.at[source, mine_rows, held]
        from_sib.append(go(remote(piece, piece, cs.at[0, d - 1], cr.at[0, d - 1], sibling)))
    arrived(ring)
    for d, side, copy in from_y:
        copy.wait_recv()
        source = (x + NX - d) % NX
        piece = plane.at[source, mine_rows, lanes_at((1 - parity) * 2 + side, quarter)]
        from_sib.append(go(remote(piece, piece, cs.at[1 + side, d - 1], cr.at[1 + side, d - 1], sibling)))
    arrived(from_sib)
    for copy in started:
        copy.wait_send()
    for copy in local:
        copy.wait()


def dispatch_kernel(outgoing, got, send, recv, fsend, frecv, own):
    z, x, r, y = here()
    ny = lax.axis_size("col")
    steps = plane_steps(ny)
    sibling = (z, x, 1 - r, y)
    greet([(z, (x + dx) % NX, r, (y + dy) % ny) for dx, dy in steps] + [sibling])
    me = x * ny + y
    mine = lanes_at(r, outgoing.shape[2])
    local = pltpu.make_async_copy(outgoing.at[me], got.at[me, :, mine], own.at[0])
    local.start()
    sends, forwards = [], []
    for k, (dx, dy) in enumerate(steps):
        tx, ty = (x + dx) % NX, (y + dy) % ny
        sends.append(remote(outgoing.at[tx * ny + ty], got.at[me, :, mine], send.at[k], recv.at[k], (z, tx, r, ty)))
        sends[-1].start()
    forwards.append(remote(outgoing.at[me], got.at[me, :, mine], fsend.at[len(steps)], frecv.at[len(steps)], sibling))
    forwards[-1].start()
    for k, (dx, dy) in reversed(list(enumerate(steps))):
        sends[k].wait_recv()
        source = (x + NX - dx) % NX * ny + (y + ny - dy) % ny
        piece = got.at[source, :, mine]
        forwards.append(remote(piece, piece, fsend.at[k], frecv.at[k], sibling))
        forwards[-1].start()
    for copy in forwards:
        copy.wait()
    for copy in sends:
        copy.wait_send()
    local.wait()


def return_kernel(part, back, other, total, send, recv, csend, crecv):
    z, x, r, y = here()
    ny = lax.axis_size("col")
    steps = plane_steps(ny)
    sibling = (z, x, 1 - r, y)
    greet([(z, (x + dx) % NX, r, (y + dy) % ny) for dx, dy in steps] + [sibling])
    me = x * ny + y
    half = back.shape[2]
    keep, give = lanes_at(r, half), lanes_at(1 - r, half)
    steps = steps + [(0, 0)]
    swaps, sends = [], []
    for k, (dx, dy) in enumerate(steps):
        to = (x + dx) % NX * ny + (y + dy) % ny
        swaps.append(remote(part.at[to, :, give], other.at[to], csend.at[k], crecv.at[k], sibling))
        swaps[-1].start()
    for k, (dx, dy) in enumerate(steps):
        tx, ty = (x + dx) % NX, (y + dy) % ny
        to = tx * ny + ty
        swaps[k].wait_recv()
        value = (part[to, :, keep].astype(F32) + other[to].astype(F32)).astype(BF)
        if dx or dy:
            total[to] = value
            sends.append(remote(total.at[to], back.at[me], send.at[k], recv.at[k], (z, tx, r, ty)))
            sends[-1].start()
        else:
            back[me] = value
    for copy in sends:
        copy.wait()
    for copy in swaps:
        copy.wait_send()


def ring_sum(nz, z, up, down, chunks, slabs, low, top, came, leave, send, recv):
    half = nz // 2
    far = (z + half) % nz
    copies = [
        remote(chunks.at[(far,) + low], came.at[(0, 0) + low], send.at[0, 0], recv.at[0, 0], up),
        remote(chunks.at[(far,) + top], came.at[(1, 0) + top], send.at[1, 0], recv.at[1, 0], down),
    ]
    for copy in copies:
        copy.start()
    for s in range(1, half):
        for way, device in ((0, up), (1, down)):
            d = (z + half - s) % nz if way == 0 else (z + half + s) % nz
            copies[2 * (s - 1) + way].wait_recv()
            for slab in slabs:
                if s == 1 and slab[0] != way:
                    leave[(way, s - 1) + slab[1]] = chunks[(d,) + slab[1]]
                else:
                    value = chunks[(d,) + slab[1]].astype(F32) + came[(way, s - 1) + slab[1]].astype(F32)
                    leave[(way, s - 1) + slab[1]] = value.astype(BF)
            copies.append(remote(leave.at[way, s - 1], came.at[way, s], send.at[way, s], recv.at[way, s], device))
            copies[-1].start()
    return copies


def gap_kernel(nz, parts, teacher, gaps, loss, arrived, came, leave, total, send, recv, zsend, zrecv, gsend, grecv):
    z, x, r, y = here()
    ny = lax.axis_size("col")
    steps = plane_steps(ny)
    up, down = ((z + 1) % nz, x, r, y), ((z + nz - 1) % nz, x, r, y)
    greet([(z, (x + dx) % NX, r, (y + dy) % ny) for dx, dy in steps] + [up, down])
    me = x * ny + y
    half = teacher.shape[2] // 2
    low, top = (slice(None), pl.ds(0, half)), (slice(None), pl.ds(half, half))
    sends = []
    for k, (dx, dy) in enumerate(steps):
        tx, ty = (x + dx) % NX, (y + dy) % ny
        sends.append(remote(parts.at[tx * ny + ty], arrived.at[k], send.at[k], recv.at[k], (z, tx, r, ty)))
        sends[-1].start()
    ring = ring_sum(nz, z, up, down, teacher, [(0, low), (1, top)], low, top, came, leave, zsend, zrecv)
    total[...] = parts[me].astype(F32) - teacher[z].astype(F32)
    for k in reversed(range(len(steps))):
        sends[k].wait_recv()
        total[...] += arrived[k].astype(F32)
    for way in (0, 1):
        ring[-2 + way].wait_recv()
        total[...] -= came[way, nz // 2 - 1].astype(F32)
    gaps[me] = total[...].astype(BF)
    outs = []
    for k, (dx, dy) in enumerate(steps):
        tx, ty = (x + dx) % NX, (y + dy) % ny
        outs.append(remote(gaps.at[me], gaps.at[me], gsend.at[k], grecv.at[k], (z, tx, r, ty)))
        outs[-1].start()
    squares = jnp.zeros(loss.shape, F32)
    for tile in range(total.shape[1] // 128):
        value = total[:, pl.ds(tile * 128, 128)]
        squares += value * value
    loss[...] = squares
    for copy in outs:
        copy.wait()
    for copy in sends + ring:
        copy.wait_send()


def grad_kernel(nz, term, loss, grad, losses, chunks, came, leave, total, send, recv, csend, crecv, xsend, xrecv, lsend, lrecv, own):
    z, x, r, y = here()
    ny = lax.axis_size("col")
    up, down = ((z + 1) % nz, x, r, y), ((z + nz - 1) % nz, x, r, y)
    sibling = (z, x, 1 - r, y)
    mates = [(d, (z, x, r, (y + d) % ny)) for d in range(1, ny)]
    mates += [(ny + d, (z, x, 1 - r, (y + d) % ny)) for d in range(ny)]
    across = [(d, (x + d) % NX) for d in (2, 1, 3)]
    greet([up, down] + [m for _, m in mates] + [(z, tx, r, y) for _, tx in across])
    rows, span = chunks.shape[1], chunks.shape[2]
    keep = pl.ds(pl.multiple_of(r * rows, rows), rows)
    give = pl.ds(pl.multiple_of((1 - r) * rows, rows), rows)
    per = nz // 2
    local, swaps = [], []
    for q in range(per):
        columns = pl.ds(q * span, span)
        swaps.append(remote(term.at[give, columns], chunks.at[r * per + q], csend.at[q], crecv.at[q], sibling))
        swaps[-1].start()
        local.append(pltpu.make_async_copy(term.at[keep, columns], chunks.at[r * per + q], own.at[q]))
        local[-1].start()
    slot = r * ny + y
    local.append(pltpu.make_async_copy(loss, losses.at[slot], own.at[per]))
    local[-1].start()
    tells = []
    for k, (_, device) in enumerate(mates):
        tells.append(remote(loss, losses.at[slot], lsend.at[k], lrecv.at[k], device))
        tells[-1].start()
    for copy in local:
        copy.wait()
    for copy in swaps:
        copy.wait_recv()
    half = rows // 2
    low, top = (pl.ds(0, half), slice(None)), (pl.ds(half, half), slice(None))
    ring = ring_sum(nz, z, up, down, chunks, [(0, low), (1, top)], low, top, came, leave, send, recv)
    for way in (0, 1):
        ring[-2 + way].wait_recv()
    value = chunks[z].astype(F32) + came[0, per - 1].astype(F32) + came[1, per - 1].astype(F32)
    total[...] = value.astype(BF)
    lanes = span // NX
    outs = []
    for d, tx in across:
        outs.append(remote(total.at[:, lanes_at(tx, lanes)], grad.at[x], xsend.at[d - 1], xrecv.at[d - 1], (z, tx, r, y)))
        outs[-1].start()
    last = pltpu.make_async_copy(total.at[:, lanes_at(x, lanes)], grad.at[x], own.at[per + 1])
    last.start()
    last.wait()
    for copy in outs + tells:
        copy.wait()
    for copy in swaps + ring:
        copy.wait_send()


def routing(routes, weights, plane, ny, cap):
    nz, block, _ = routes.shape
    experts = NX * ny
    local = routes - plane * experts
    ids = jnp.arange(experts, dtype=jnp.int32)
    hit = local[..., None] == ids
    named = jnp.any(hit, axis=2)
    weight = jnp.sum(jnp.where(hit, weights[..., None], 0.0), axis=2)
    count = named.astype(jnp.int32)
    slot = jnp.cumsum(count, axis=1) - count
    place = named[..., None] & (slot[..., None] == jnp.arange(cap, dtype=jnp.int32))
    same = jnp.eye(nz, dtype=bool)
    full = place[:, :, :, None, :] & same[:, None, None, :, None]
    combine = jnp.where(full, weight[:, :, :, None, None], 0.0)
    rows = experts * nz * cap
    return full.reshape(nz * block, rows).astype(BF), combine.reshape(nz * block, rows)


def on_device(tokens, routes, route_weights, teacher_in, teacher_out, student_in, student_out):
    nz, nr, ny = lax.axis_size("z"), lax.axis_size("row"), lax.axis_size("col")
    z, x, r, y = here()
    tok, width = tokens.shape
    block, top = routes.shape
    blk = student_in.shape[1]
    ff = student_in.shape[2]
    sub = ff // NX
    half = width // nr
    experts = NX * ny
    cap = max(2, 3 * block * top // (2 * nz * experts))
    blocks = nz * NX
    shape = jax.ShapeDtypeStruct

    parts = jnp.concatenate([jnp.swapaxes(student_in, 1, 2), student_out[None]], axis=0)
    parts = pad_lanes(parts)
    lanes = parts.shape[-1]
    wide = blocks * lanes
    inner, outer = kernel_call(
        weights_kernel, 0,
        [shape((2, sub, NX * lanes), BF), shape((sub, NX * lanes), BF)],
        [dma(3, 3), dma(3, 3), dma(3)],
        parts.reshape(3, NX, sub, lanes),
    )
    padded = pad_lanes(tokens.reshape(tok, blocks, blk)).reshape(tok, wide)
    mine = lax.dynamic_slice(tokens, (y * block, r * half), (block, half))
    meta = jnp.concatenate([routes.astype(F32), route_weights], axis=1)
    meta = jnp.pad(meta, ((0, 0), (0, 128 - 2 * top)))
    inner, outer, padded, mine, meta = lax.optimization_barrier((inner, outer, padded, mine, meta))
    inner = lax.all_gather(inner, "z", axis=2, tiled=True)
    outer = lax.all_gather(outer, "z", axis=1, tiled=True)

    steps = nz // 2
    plane_tokens, column, metas = kernel_call(
        functools.partial(tokens_kernel, nz), 1,
        [shape((NX, tok, wide), BF), shape((nz, block, half), BF), shape((nz, block, 128), F32)],
        [dma(3), dma(3), dma(2, 3), dma(2, 3), dma(3, 3), dma(3, 3)] + [dma(2, steps)] * 4 + [dma(3)],
        padded, mine, meta,
    )
    routes_z = metas[:, :, :top].astype(jnp.int32)
    place, combine = routing(routes_z, metas[:, :, top:2 * top], z, ny, cap)
    slots = nz * cap
    outgoing = dot(place, column.reshape(nz * block, half), ((0,), (0,))).astype(BF)
    (arrived,) = kernel_call(
        dispatch_kernel, 2,
        [shape((experts, slots, width), BF)],
        [dma(experts)] * 4 + [dma(1)],
        outgoing.reshape(experts, slots, half),
    )
    arrived = arrived.reshape(experts * slots, width)
    gate = dot(arrived, teacher_in[0, 0], ((1,), (0,)))
    up = dot(arrived, teacher_in[0, 1], ((1,), (0,)))
    act = (jax.nn.silu(gate) * up).astype(BF)
    part = dot(act, teacher_out[0], ((1,), (0,))).astype(BF)
    (back,) = kernel_call(
        return_kernel, 3,
        [shape((experts, slots, half), BF)],
        [pltpu.VMEM((experts, slots, half), BF)] * 2 + [dma(experts)] * 4,
        part.reshape(experts, slots, width),
    )
    back = back.reshape(experts * slots, half)
    high = combine.astype(BF)
    low = (combine - high.astype(F32)).astype(BF)
    teacher = dot(jnp.concatenate([high, low], axis=1), jnp.concatenate([back, back], axis=0), ((1,), (0,))).astype(BF)
    teacher = pad_lanes(teacher.reshape(nz, block, blocks // nr, blk)).reshape(nz, block, wide // nr)

    plane_tokens = plane_tokens.reshape(NX * tok, wide)
    gate = dot(plane_tokens, inner[0], ((1,), (1,)))
    up = dot(plane_tokens, inner[1], ((1,), (1,)))
    hidden = (jax.nn.silu(gate) * up).astype(BF)
    hidden_both = lax.all_gather(hidden, "row", axis=1, tiled=True)
    outer_both = lax.all_to_all(outer.reshape(sub, nr, wide // nr), "row", split_axis=1, concat_axis=0, tiled=True)
    outer_both = outer_both.reshape(nr * sub, wide // nr)
    y_part = dot(hidden_both, outer_both, ((1,), (0,))).astype(BF)
    span = wide // nr
    gap_round, loss = kernel_call(
        functools.partial(gap_kernel, nz), 4,
        [shape((experts, block, span), BF), shape((block, 128), F32)],
        [pltpu.VMEM((experts - 1, block, span), BF)]
        + [pltpu.VMEM((2, steps, block, span), BF), pltpu.VMEM((2, steps - 1, block, span), BF)]
        + [pltpu.VMEM((block, span), F32)]
        + [dma(experts - 1)] * 2 + [dma(2, steps)] * 2 + [dma(experts - 1)] * 2,
        y_part.reshape(experts, block, span), teacher,
    )
    term = (dot(hidden_both, gap_round.reshape(experts * block, span), ((0,), (0,))) / tok).astype(BF)
    chunk = NX * lanes
    grad, losses = kernel_call(
        functools.partial(grad_kernel, nz), 5,
        [shape((NX, sub, lanes), BF), shape((nr * ny, block, 128), F32)],
        [pltpu.VMEM((nz, sub, chunk), BF), pltpu.VMEM((2, steps, sub, chunk), BF)]
        + [pltpu.VMEM((2, steps - 1, sub, chunk), BF), pltpu.VMEM((sub, chunk), BF)]
        + [dma(2, steps)] * 2 + [dma(steps)] * 2 + [dma(3)] * 2 + [dma(2 * ny - 1)] * 2 + [dma(steps + 2)],
        term, loss,
    )
    token_loss = jnp.sum(losses.reshape(nr, ny * block, 128), axis=(0, 2)) / width
    grad = grad.reshape(ff, lanes)[:, :blk].astype(F32)
    return token_loss, grad


def solution(mesh):
    dp = ("z", "x")
    in_specs = (
        P(dp, None),
        P(dp + ("col",), None),
        P(dp + ("col",), None),
        P(dp + ("col",), None, None, "row"),
        P(dp + ("col",), "row", None),
        P(None, dp, ("row", "col")),
        P(("row", "col"), dp),
    )
    out_specs = (P(dp), P(("row", "col"), dp))
    return jax.shard_map(
        on_device, mesh=split_mesh(mesh), in_specs=in_specs, out_specs=out_specs, check_vma=False
    )
```

time: 464 us -> 301 us (0.65); the launches traced: 456 us -> 299 us
  waiting for transfers between devices: 237 us -> 0.56 us
  Pallas kernels: 0 us -> 226 us
  blocking collectives: 109 us -> 2.33 us
  starting transfers between devices: 24.8 us -> 5.58 us
  local copies, waits for them, and re-layouts: 27 us -> 14.2 us
  matrix products: 36.9 us -> 32 us
    pallas_call x0 -> x6, Pallas kernels: none -> 226 us  [kernel_call(): pl.pallas_call(body, out_shape=outs, in_specs=[whole] * len(args), out_sp...]
    all_gather x6 -> x2, waiting for transfers between devices: 169 us -> 0.02 us  [the longest x1 0.02 us: on_device(): outer = lax.all_gather(outer, 'z', axis=1, tiled=True)]
    reduce_scatter x2 -> x0, waiting for transfers between devices: 68 us -> none  [the longest x1 34.2 us: on_device(): lax.psum_scatter(teacher.astype(BF).reshape(nz, block, half), 'z', scatte...]
    all_to_all x4 -> x0, blocking collectives: 51.6 us -> none  [the longest x1 21.7 us: on_device(): lax.all_to_all(outgoing, ('x', 'col'), split_axis=0, concat_axis=0, tiled...]
    all_gather x2 -> x0, blocking collectives: 43 us -> none  [the longest x1 22.9 us: on_device(): routes_z = lax.all_gather(routes, 'z')]
    all_to_all x3 -> x0, starting transfers between devices: 14.3 us -> none  [the longest x1 6.58 us: on_device(): lax.all_to_all(y_part.reshape(plane_experts, block, -1), ('x', 'col'), sp...]
    unnamed x1 -> x0, blocking collectives: 8.91 us -> none
    dot_general x9 -> x8, matrix products: 36.9 us -> 32 us  [dot(): return lax.dot_general(a, b, (dims, ((), ())), preferred_element_type=F32)]
  transfers between devices with their start and end apart: 12 -> 3, of which waited for: 7 -> 0; matrix products, arithmetic and copies ran while one was open for 9% -> 11% of each run, Pallas kernels for 0% -> 31%
where the time goes in v2:
time: 301 us; the launch traced here: 299 us
  Pallas kernels  226 us (75%)
  matrix products  32 us (11%)
  between operations  14.4 us (5%)
  local copies, waits for them, and re-layouts  14.2 us (5%)
  starting transfers between devices  5.58 us (2%)
  other arithmetic  3.79 us (1%)
    pallas_call x6, Pallas kernels, kernel_call(): pl.pallas_call(body, out_shape=outs, in_specs=[whole] * len(args), out_sp...  226 us
    dot_general x8, matrix products, dot(): return lax.dot_general(a, b, (dims, ((), ())), preferred_element_type=F32)  32 us
  transfers between devices with their start and end apart: 3, of which 0 were waited for; matrix products, arithmetic and copies ran while one was open for 11% of the time, Pallas kernels for 31%

profile of v2, /device:TPU:1, one launch (start us, length us, event | category | flops | bytes accessed | tf_op | source)
XLA Modules:
  0.0 298.9 jit_solution(2185542475693373007)
XLA Ops:
  7.2 1.3 pad_maximum_fusion
  8.6 0.9 copy.49
  9.7 16.3 %shard_map.86 = (bf16[2,288,512]{2,1,0:T(8,128)(2,1)}, bf16[288,512]{1,0:T(8,128)(2,1)}) custom-call(bf16[3,4,288,128]{3,2,1,0:T(8,128)(2,1)S(1)} %bitcast.73), custom_call_target="tpu_custom_call" | custom-call | tf_op jit(solution)/shard_map/pallas_call | solution.py:54
  26.0 1.9 reshape.103
  29.7 44.2 %shard_map.87 = (bf16[4,160,4096]{2,1,0:T(8,128)(2,1)}, bf16[8,40,1792]{2,1,0:T(8,128)(2,1)S(1)}, f32[8,40,128]{2,1,0:T(8,128)S(1)}) custom-call(bf16[160,4096]{1,0:T(8,128)(2,1)S(1)} %bitcast.72, bf16[40,1792]{1,0:T(8,128)(2,1)S(1)} %dynamic_slice.3.mine, f32[40,128]{1,0:T(8,128)S(1)} %pad.18.meta), custom_call_target="tpu_custom_call" | custom-call | tf_op jit(solution)/shard_map/pallas_call | solution.py:54
  74.9 0.6 and.45
  75.5 0.9 convolution_convert_fusion.2
  76.4 24.7 %shard_map.88 = bf16[16,24,3584]{2,1,0:T(8,128)(2,1)S(1)} custom-call(bf16[16,24,1792]{2,1,0:T(8,128)(2,1)S(1)} %bitcast.71), custom_call_target="tpu_custom_call" | custom-call | tf_op jit(solution)/shard_map/pallas_call | solution.py:54
  101.0 4.6 %fusion.3 = f32[384,512]{1,0:T(8,128)} fusion(bf16[384,3584]{1,0:T(8,128)(2,1)S(1)} %bitcast.74, bf16[1,2,3584,512]{3,2,1,0:T(8,128)(2,1)} %param.10), kind=kOutput, calls=%fused_computation.5 | convolution fusion | flops 1409286144 | bytes 7208960 | tf_op jit(solution)/shard_map/dot_general | solution.py:22
  105.6 8.1 %convolution_convert_fusion = bf16[384,3584]{1,0:T(8,128)(2,1)} fusion(bf16[1,512,3584]{2,1,0:T(8,128)(2,1)} %param.11, bf16[384,3584]{1,0:T(8,128)(2,1)S(1)} %bitcast.75, bf16[1,2,3584,512]{3,2,1,0:T(8,128)(2,1)} %param.10, f32[384,512]{1,0:T(8,128)} %fusion.3), kind=kOutput, calls=%fused_computation | convolution fusion | flops 2821128192 | bytes 13631488 | tf_op jit(solution)/shard_map/dot_general | solution.py:22
  113.7 1.8 copy-done
  115.5 24.6 %shard_map.89 = bf16[16,24,1792]{2,1,0:T(8,128)(2,1)S(1)} custom-call(bf16[16,24,3584]{2,1,0:T(8,128)(2,1)S(1)} %bitcast.76), custom_call_target="tpu_custom_call" | custom-call | tf_op jit(solution)/shard_map/pallas_call | solution.py:54
  141.1 1.1 fusion.11
  142.2 2.4 reshape.114
  145.5 3.4 %copy.54 = bf16[36,2,8,2048]{3,2,0,1:T(8,128)(2,1)} copy(bf16[36,2,8,2048]{3,2,1,0:T(8,128)(2,1)} %bitcast.84) | data formatting | bytes 4718592 | tf_op jit(solution)/shard_map/reshape | solution.py:448
  148.9 5.3 %all-to-all-start = ((bf16[288,2,2048]{2,0,1:T(8,128)(2,1)}), bf16[288,2,2048]{2,0,1:T(8,128)(2,1)}, u32[]{:S(2)}, u32[]{:S(2)}) async-start(bf16[288,2,2048]{2,0,1:T(8,128)(2,1)} %bitcast.81), calls=%async_computation | async-start | bytes 4718592 | tf_op jit(solution)/shard_map/all_to_all | solution.py:448
  154.2 5.4 %fusion.15 = f32[640,288]{0,1:T(8,128)S(1)} fusion(bf16[640,4096]{1,0:T(8,128)(2,1)} %bitcast.87, bf16[2,288,4096]{2,1,0:T(8,128)(2,1)} %all-gather.3.cloned.1.call-done), kind=kOutput, calls=%fused_computation.20 | convolution fusion | flops 1509949440 | bytes 8339456 | tf_op jit(solution)/shard_map/dot_general | solution.py:22
  159.6 4.5 %fusion.23 = bf16[640,288]{0,1:T(8,128)(2,1)S(1)} fusion(bf16[640,4096]{1,0:T(8,128)(2,1)} %bitcast.88, bf16[2,288,4096]{2,1,0:T(8,128)(2,1)S(1)} %copy-done.4, f32[640,288]{0,1:T(8,128)S(1)} %fusion.15), kind=kOutput, calls=%fused_computation.25 | convolution fusion | flops 1511055360 | bytes 8708096 | tf_op jit(solution)/shard_map/dot_general | solution.py:22
  164.1 2.3 all_gather.10
  166.4 5.4 %convolution_convert_fusion.1 = bf16[640,2048]{1,0:T(8,128)(2,1)} fusion(bf16[640,576]{0,1:T(8,128)(2,1)S(1)} %all_gather.10, bf16[576,2048]{1,0:T(8,128)(2,1)} %bitcast.8), kind=kOutput, calls=%fused_computation.9 | convolution fusion | flops 1511260160 | bytes 5718016 | tf_op jit(solution)/shard_map/dot_general | solution.py:22
  171.9 76.3 %shard_map.90 = (bf16[16,40,2048]{2,1,0:T(8,128)(2,1)S(1)}, f32[40,128]{1,0:T(8,128)S(1)}) custom-call(bf16[16,40,2048]{2,1,0:T(8,128)(2,1)} %bitcast.83, bf16[8,40,2048]{2,1,0:T(8,128)(2,1)S(1)} %reshape.115.teacher), custom_call_target="tpu_custom_call" | custom-call | tf_op jit(solution)/shard_map/pallas_call | solution.py:54
  248.1 2.0 multiply_convert_fusion.term
  250.2 40.1 %shard_map.91 = (bf16[4,288,128]{2,1,0:T(8,128)(2,1)S(1)}, f32[8,40,128]{2,1,0:T(8,128)S(1)}) custom-call(bf16[576,2048]{1,0:T(8,128)(2,1)S(1)} %multiply_convert_fusion.term, f32[40,128]{1,0:T(8,128)S(1)} %get-tuple-element.27.loss), custom_call_target="tpu_custom_call" | custom-call | tf_op jit(solution)/shard_map/pallas_call | solution.py:54
  291.2 0.8 convert_element_type.72
  (48 shorter events, 5.7 us)
Async XLA Ops:
  7.2 138.3 %all-gather.5.cloned.1.call-start = ((), (), s32[]{:S(2)}) async-start(), calls=%async_computation.2 | async-start | bytes 2654208 | tf_op jit(solution)/shard_map/all_gather | solution.py:407
  7.2 18.8 %copy-start.1 = (bf16[160,3584]{1,0:T(8,128)(2,1)S(1)}, bf16[160,3584]{1,0:T(8,128)(2,1)}, u32[]{:S(2)}) copy-start(bf16[160,3584]{1,0:T(8,128)(2,1)} %param.7) | copy-start | bytes 3440644
  27.9 0.9 copy-start.2
  27.9 0.9 copy-start.3
  28.9 125.2 %all-gather.3.cloned.1.call-start = ((), (), s32[]{:S(2)}) async-start(), calls=%async_computation.1 | async-start | bytes 5308416 | tf_op jit(solution)/shard_map/all_gather | solution.py:406
  113.7 1.8 copy-start
  148.9 17.6 %all-to-all-start = ((bf16[288,2,2048]{2,0,1:T(8,128)(2,1)}), bf16[288,2,2048]{2,0,1:T(8,128)(2,1)}, u32[]{:S(2)}, u32[]{:S(2)}) async-start(bf16[288,2,2048]{2,0,1:T(8,128)(2,1)} %bitcast.81), calls=%async_computation | async-start | bytes 4718592 | tf_op jit(solution)/shard_map/all_to_all | solution.py:448
  154.2 5.4 %copy-start.4 = (bf16[2,288,4096]{2,1,0:T(8,128)(2,1)S(1)}, bf16[2,288,4096]{2,1,0:T(8,128)(2,1)}, u32[]{:S(2)}) copy-start(bf16[2,288,4096]{2,1,0:T(8,128)(2,1)} %all-gather.3.cloned.1.call-done) | copy-start | bytes 14155780
Sparse Core Ops, SparseCore 0:
  29.1 46.2 all-gather.4
  77.1 59.3 all-gather.2

commit v3 on v2

--- a/solution.py
+++ b/solution.py
@@ -73,42 +73,35 @@
     return sorted(steps, key=far, reverse=True)
 
 
-def weights_kernel(parts, inner, outer, send, recv, own):
-    z, x, r, y = here()
-    greet([(z, (x + d) % NX, r, y) for d in (1, 2, 3)])
-    copies = []
-    for d in (2, 1, 3):
-        to = (x + d) % NX
-        device = (z, to, r, y)
-        for kind in (0, 1, 2):
-            dst = outer.at[:, lanes_at(x, 128)] if kind == 2 else inner.at[kind, :, lanes_at(x, 128)]
-            copies.append(remote(parts.at[kind, to], dst, send.at[d - 1, kind], recv.at[d - 1, kind], device))
-            copies[-1].start()
-    local = []
-    for kind in (0, 1, 2):
-        dst = outer.at[:, lanes_at(x, 128)] if kind == 2 else inner.at[kind, :, lanes_at(x, 128)]
-        local.append(pltpu.make_async_copy(parts.at[kind, x], dst, own.at[kind]))
-        local[-1].start()
-    for copy in copies + local:
-        copy.wait()
-
-
-def tokens_kernel(nz, padded, mine, meta, plane, column, metas, xs, xr, ys, yr, cs, cr, zs, zr, ms, mr, own):
+def tokens_kernel(nz, padded, mine, meta, parts, plane, column, metas, shard, xs, xr, ys, yr, cs, cr, zs, zr, ms, mr, ws, wr, own):
     z, x, r, y = here()
     up, down = (z + 1) % nz, (z + nz - 1) % nz
     ny = lax.axis_size("col")
     north, south = (y + 1) % ny, (y + ny - 1) % ny
     sibling = (z, x, 1 - r, y)
-    greet(
-        [(z, (x + d) % NX, r, y) for d in (1, 2, 3)]
-        + [(z, x, r, north), (z, x, r, south), (up, x, r, y), (down, x, r, y), sibling]
-    )
+    per = nz // 2
+    core = z // per
+    plane_z = per * r + z % per
+    moves = core != r
+    others = [(z, (x + d) % NX, r, y) for d in (1, 2, 3)]
+    others += [(plane_z, (x + d) % NX, core, y) for d in (1, 2, 3)]
+    others += [(z, x, r, north), (z, x, r, south), (up, x, r, y), (down, x, r, y), sibling]
+
+    @pl.when(moves)
+    def _():
+        greet(others + [(plane_z, x, core, y)])
+
+    @pl.when(jnp.logical_not(moves))
+    def _():
+        greet(others)
+
     rows, wide = padded.shape
     high, span = rows // 2, wide // 2
     quarter = span // 2
     mine_rows = pl.ds(pl.multiple_of(r * high, high), high)
     parity = y % 2
     held = lanes_at(parity, span)
+    slot = lanes_at(x, 128)
     started = []
 
     def go(copy):
@@ -120,6 +113,8 @@
         pltpu.make_async_copy(padded, plane.at[x], own.at[0]),
         pltpu.make_async_copy(mine, column.at[z], own.at[1]),
         pltpu.make_async_copy(meta, metas.at[z], own.at[2]),
+        pltpu.make_async_copy(parts.at[0, x], shard.at[0, :, slot], own.at[3]),
+        pltpu.make_async_copy(parts.at[1, x], shard.at[1, :, slot], own.at[4]),
     ]
     for copy in local:
         copy.start()
@@ -153,6 +148,23 @@
     for d in (2, 1, 3):
         device = (z, (x + d) % NX, r, y)
         from_x[d] = go(remote(padded.at[mine_rows, held], plane.at[x, mine_rows, held], xs.at[d - 1], xr.at[d - 1], device))
+    weights = []
+    for d in (2, 1, 3):
+        to = (x + d) % NX
+        for kind in (0, 1):
+            weights.append(go(remote(parts.at[kind, to], shard.at[kind, :, slot], ws.at[d, kind], wr.at[d, kind], (z, to, r, y))))
+        weights.append(go(remote(parts.at[2, to], shard.at[2, :, slot], ws.at[d, 2], wr.at[d, 2], (plane_z, to, core, y))))
+    down_own = remote(parts.at[2, x], shard.at[2, :, slot], ws.at[0, 2], wr.at[0, 2], (plane_z, x, core, y))
+    down_here = pltpu.make_async_copy(parts.at[2, x], shard.at[2, :, slot], own.at[5])
+
+    @pl.when(moves)
+    def _():
+        down_own.start()
+
+    @pl.when(jnp.logical_not(moves))
+    def _():
+        down_here.start()
+
     turn = 0
     from_sib, from_y = [], []
     for d in (1, 3, 2):
@@ -172,11 +184,20 @@
         source = (x + NX - d) % NX
         piece = plane.at[source, mine_rows, lanes_at((1 - parity) * 2 + side, quarter)]
         from_sib.append(go(remote(piece, piece, cs.at[1 + side, d - 1], cr.at[1 + side, d - 1], sibling)))
+    arrived(weights)
     arrived(from_sib)
     for copy in started:
         copy.wait_send()
     for copy in local:
         copy.wait()
+
+    @pl.when(moves)
+    def _():
+        down_own.wait()
+
+    @pl.when(jnp.logical_not(moves))
+    def _():
+        down_here.wait()
 
 
 def dispatch_kernel(outgoing, got, send, recv, fsend, frecv, own):
@@ -241,67 +262,120 @@
         copy.wait_send()
 
 
-def ring_sum(nz, z, up, down, chunks, slabs, low, top, came, leave, send, recv):
-    half = nz // 2
-    far = (z + half) % nz
-    copies = [
-        remote(chunks.at[(far,) + low], came.at[(0, 0) + low], send.at[0, 0], recv.at[0, 0], up),
-        remote(chunks.at[(far,) + top], came.at[(1, 0) + top], send.at[1, 0], recv.at[1, 0], down),
-    ]
-    for copy in copies:
+def ring_sum(n, i, up, down, ref, where, subs, came, leave, send, recv, copies):
+    half = n // 2
+
+    def go(way, s, u, src, dst):
+        copy = remote(src, dst, send.at[way, s, u], recv.at[way, s, u], (up, down)[way])
         copy.start()
+        copies[way, s, u] = copy
+
+    for u, (whole, low, top) in enumerate(subs):
+        for way, part in ((0, low), (1, top)):
+            go(way, 0, u, ref.at[where((i + half) % n, part)], came.at[(way, 0) + part])
+    yield
     for s in range(1, half):
+        for u, (whole, low, top) in enumerate(subs):
+            for way in (0, 1):
+                d = (i + half - s) % n if way == 0 else (i + half + s) % n
+                copies[way, s - 1, u].wait_recv()
+                summed, plain = whole, None
+                if s == 1:
+                    summed, plain = (low, top) if way == 0 else (top, low)
+                    leave[(way, 0) + plain] = ref[where(d, plain)]
+                value = ref[where(d, summed)].astype(F32) + came[(way, s - 1) + summed].astype(F32)
+                leave[(way, s - 1) + summed] = value.astype(BF)
+                go(way, s, u, leave.at[(way, s - 1) + whole], came.at[(way, s) + whole])
+        yield
+    for u in range(len(subs)):
+        for way in (0, 1):
+            copies[way, half - 1, u].wait_recv()
+
+
+def ring_gather(n, i, up, down, ref, where, whole, low, top, send, recv, copies):
+    half = n // 2
+    for s in range(half):
         for way, device in ((0, up), (1, down)):
-            d = (z + half - s) % nz if way == 0 else (z + half + s) % nz
-            copies[2 * (s - 1) + way].wait_recv()
-            for slab in slabs:
-                if s == 1 and slab[0] != way:
-                    leave[(way, s - 1) + slab[1]] = chunks[(d,) + slab[1]]
-                else:
-                    value = chunks[(d,) + slab[1]].astype(F32) + came[(way, s - 1) + slab[1]].astype(F32)
-                    leave[(way, s - 1) + slab[1]] = value.astype(BF)
-            copies.append(remote(leave.at[way, s - 1], came.at[way, s], send.at[way, s], recv.at[way, s], device))
-            copies[-1].start()
-    return copies
-
-
-def gap_kernel(nz, parts, teacher, gaps, loss, arrived, came, leave, total, send, recv, zsend, zrecv, gsend, grecv):
+            d = (i + n - s) % n if way == 0 else (i + s) % n
+            if s:
+                copies[way, s - 1].wait_recv()
+            part = whole if s < half - 1 else (low, top)[way]
+            piece = ref.at[where(d, part)]
+            copies[way, s] = remote(piece, piece, send.at[way, s, 0], recv.at[way, s, 0], device)
+            copies[way, s].start()
+        yield
+    for way in (0, 1):
+        copies[way, half - 1].wait_recv()
+
+
+def together(*rings):
+    rings = list(rings)
+    while rings:
+        for ring in list(rings):
+            try:
+                next(ring)
+            except StopIteration:
+                rings.remove(ring)
+
+
+def gap_kernel(nz, parts, teacher, gaps, loss, xcame, xleave, ycame, yleave, xsum, ysum, xcame2, xleave2, ycame2, yleave2,
+               tcame, tleave, total, send, recv):
     z, x, r, y = here()
     ny = lax.axis_size("col")
-    steps = plane_steps(ny)
     up, down = ((z + 1) % nz, x, r, y), ((z + nz - 1) % nz, x, r, y)
-    greet([(z, (x + dx) % NX, r, (y + dy) % ny) for dx, dy in steps] + [up, down])
-    me = x * ny + y
-    half = teacher.shape[2] // 2
-    low, top = (slice(None), pl.ds(0, half)), (slice(None), pl.ds(half, half))
-    sends = []
-    for k, (dx, dy) in enumerate(steps):
-        tx, ty = (x + dx) % NX, (y + dy) % ny
-        sends.append(remote(parts.at[tx * ny + ty], arrived.at[k], send.at[k], recv.at[k], (z, tx, r, ty)))
-        sends[-1].start()
-    ring = ring_sum(nz, z, up, down, teacher, [(0, low), (1, top)], low, top, came, leave, zsend, zrecv)
-    total[...] = parts[me].astype(F32) - teacher[z].astype(F32)
-    for k in reversed(range(len(steps))):
-        sends[k].wait_recv()
-        total[...] += arrived[k].astype(F32)
-    for way in (0, 1):
-        ring[-2 + way].wait_recv()
-        total[...] -= came[way, nz // 2 - 1].astype(F32)
-    gaps[me] = total[...].astype(BF)
-    outs = []
-    for k, (dx, dy) in enumerate(steps):
-        tx, ty = (x + dx) % NX, (y + dy) % ny
-        outs.append(remote(gaps.at[me], gaps.at[me], gsend.at[k], grecv.at[k], (z, tx, r, ty)))
-        outs[-1].start()
+    east, west = (z, (x + 1) % NX, r, y), (z, (x + NX - 1) % NX, r, y)
+    north, south = (z, x, r, (y + 1) % ny), (z, x, r, (y + ny - 1) % ny)
+    greet([east, west, north, south, up, down])
+    span = teacher.shape[2]
+    wing = span // 2
+    every = slice(None)
+    first, second = pl.ds(0, wing), pl.ds(wing, wing)
+    copies = [{} for _ in range(9)]
+
+    def sems(k):
+        return send.at[k], recv.at[k], copies[k]
+
+    def trio(axis_size):
+        return (pl.ds(0, axis_size),), (pl.ds(0, axis_size // 2),), (pl.ds(axis_size // 2, axis_size // 2),)
+
+    def lanes(start, size):
+        return tuple((every, pl.ds(start + o, s)) for o, s in ((0, size), (0, size // 2), (size // 2, size // 2)))
+
+    teach = ring_sum(nz, z, up, down, teacher, lambda d, p: (d,) + p, [lanes(0, span)], tcame, tleave, *sems(0))
+    ring_x = ring_sum(NX, x, east, west, parts, lambda d, p: (d,) + p + (every, first), [trio(ny)], xcame, xleave, *sems(1))
+    ring_y = ring_sum(ny, y, north, south, parts, lambda d, p: p + (d, every, second), [trio(NX)], ycame, yleave, *sems(2))
+    next(ring_x)
+    next(ring_y)
+    next(teach)
+    together(ring_x, ring_y)
+    xsum[...] = (parts[x, :, :, first].astype(F32) + xcame[0, NX // 2 - 1].astype(F32) + xcame[1, NX // 2 - 1].astype(F32)).astype(BF)
+    ring_y = ring_sum(ny, y, north, south, xsum, lambda d, p: (d,) + p, [lanes(0, wing)], ycame2, yleave2, *sems(3))
+    next(ring_y)
+    ysum[...] = (parts[:, y, :, second].astype(F32) + ycame[0, ny // 2 - 1].astype(F32) + ycame[1, ny // 2 - 1].astype(F32)).astype(BF)
+    ring_x = ring_sum(NX, x, east, west, ysum, lambda d, p: (d,) + p, [lanes(0, wing)], xcame2, xleave2, *sems(4))
+    next(ring_x)
+    together(teach, ring_y, ring_x)
+    taught = teacher[z].astype(F32) + tcame[0, nz // 2 - 1].astype(F32) + tcame[1, nz // 2 - 1].astype(F32)
+    total[...] = -taught
+    total[:, first] += xsum[y].astype(F32) + ycame2[0, ny // 2 - 1].astype(F32) + ycame2[1, ny // 2 - 1].astype(F32)
+    total[:, second] += ysum[x].astype(F32) + xcame2[0, NX // 2 - 1].astype(F32) + xcame2[1, NX // 2 - 1].astype(F32)
+    gaps[x, y] = total[...].astype(BF)
+    gather_y = ring_gather(ny, y, north, south, gaps, lambda d, p: (x, d) + p, *lanes(0, wing), *sems(5))
+    gather_x = ring_gather(NX, x, east, west, gaps, lambda d, p: (d, y) + p, *lanes(wing, wing), *sems(6))
+    next(gather_y)
+    next(gather_x)
     squares = jnp.zeros(loss.shape, F32)
-    for tile in range(total.shape[1] // 128):
+    for tile in range(span // 128):
         value = total[:, pl.ds(tile * 128, 128)]
         squares += value * value
     loss[...] = squares
-    for copy in outs:
-        copy.wait()
-    for copy in sends + ring:
-        copy.wait_send()
+    together(gather_y, gather_x)
+    gather_x = ring_gather(NX, x, east, west, gaps, lambda d, p: (d,) + p + (every, first), *trio(ny), *sems(7))
+    gather_y = ring_gather(ny, y, north, south, gaps, lambda d, p: p + (d, every, second), *trio(NX), *sems(8))
+    together(gather_x, gather_y)
+    for group in copies:
+        for copy in group.values():
+            copy.wait_send()
 
 
 def grad_kernel(nz, term, loss, grad, losses, chunks, came, leave, total, send, recv, csend, crecv, xsend, xrecv, lsend, lrecv, own):
@@ -309,10 +383,9 @@
     ny = lax.axis_size("col")
     up, down = ((z + 1) % nz, x, r, y), ((z + nz - 1) % nz, x, r, y)
     sibling = (z, x, 1 - r, y)
-    mates = [(d, (z, x, r, (y + d) % ny)) for d in range(1, ny)]
-    mates += [(ny + d, (z, x, 1 - r, (y + d) % ny)) for d in range(ny)]
+    mates = [(z, x, r, (y + d) % ny) for d in range(1, ny)] + [(z, x, 1 - r, (y + d) % ny) for d in range(ny)]
     across = [(d, (x + d) % NX) for d in (2, 1, 3)]
-    greet([up, down] + [m for _, m in mates] + [(z, tx, r, y) for _, tx in across])
+    greet([up, down] + mates + [(z, tx, r, y) for _, tx in across])
     rows, span = chunks.shape[1], chunks.shape[2]
     keep = pl.ds(pl.multiple_of(r * rows, rows), rows)
     give = pl.ds(pl.multiple_of((1 - r) * rows, rows), rows)
@@ -328,18 +401,19 @@
     local.append(pltpu.make_async_copy(loss, losses.at[slot], own.at[per]))
     local[-1].start()
     tells = []
-    for k, (_, device) in enumerate(mates):
+    for k, device in enumerate(mates):
         tells.append(remote(loss, losses.at[slot], lsend.at[k], lrecv.at[k], device))
         tells[-1].start()
     for copy in local:
         copy.wait()
     for copy in swaps:
         copy.wait_recv()
-    half = rows // 2
-    low, top = (pl.ds(0, half), slice(None)), (pl.ds(half, half), slice(None))
-    ring = ring_sum(nz, z, up, down, chunks, [(0, low), (1, top)], low, top, came, leave, send, recv)
-    for way in (0, 1):
-        ring[-2 + way].wait_recv()
+    subs = []
+    for u in (0, 1):
+        band = pl.ds(u * (rows // 2), rows // 2)
+        subs.append(((band, pl.ds(0, span)), (band, pl.ds(0, span // 2)), (band, pl.ds(span // 2, span // 2))))
+    ring = {}
+    together(ring_sum(nz, z, up, down, chunks, lambda d, p: (d,) + p, subs, came, leave, send, recv, ring))
     value = chunks[z].astype(F32) + came[0, per - 1].astype(F32) + came[1, per - 1].astype(F32)
     total[...] = value.astype(BF)
     lanes = span // NX
@@ -352,7 +426,7 @@
     last.wait()
     for copy in outs + tells:
         copy.wait()
-    for copy in swaps + ring:
+    for copy in swaps + list(ring.values()):
         copy.wait_send()
 
 
@@ -392,27 +466,18 @@
     parts = pad_lanes(parts)
     lanes = parts.shape[-1]
     wide = blocks * lanes
-    inner, outer = kernel_call(
-        weights_kernel, 0,
-        [shape((2, sub, NX * lanes), BF), shape((sub, NX * lanes), BF)],
-        [dma(3, 3), dma(3, 3), dma(3)],
-        parts.reshape(3, NX, sub, lanes),
-    )
     padded = pad_lanes(tokens.reshape(tok, blocks, blk)).reshape(tok, wide)
     mine = lax.dynamic_slice(tokens, (y * block, r * half), (block, half))
     meta = jnp.concatenate([routes.astype(F32), route_weights], axis=1)
     meta = jnp.pad(meta, ((0, 0), (0, 128 - 2 * top)))
-    inner, outer, padded, mine, meta = lax.optimization_barrier((inner, outer, padded, mine, meta))
-    inner = lax.all_gather(inner, "z", axis=2, tiled=True)
-    outer = lax.all_gather(outer, "z", axis=1, tiled=True)
-
     steps = nz // 2
-    plane_tokens, column, metas = kernel_call(
+    plane_tokens, column, metas, shard = kernel_call(
         functools.partial(tokens_kernel, nz), 1,
-        [shape((NX, tok, wide), BF), shape((nz, block, half), BF), shape((nz, block, 128), F32)],
-        [dma(3), dma(3), dma(2, 3), dma(2, 3), dma(3, 3), dma(3, 3)] + [dma(2, steps)] * 4 + [dma(3)],
-        padded, mine, meta,
-    )
+        [shape((NX, tok, wide), BF), shape((nz, block, half), BF), shape((nz, block, 128), F32), shape((3, sub, NX * lanes), BF)],
+        [dma(3), dma(3), dma(2, 3), dma(2, 3), dma(3, 3), dma(3, 3)] + [dma(2, steps)] * 4 + [dma(4, 3)] * 2 + [dma(6)],
+        padded, mine, meta, parts.reshape(3, NX, sub, lanes),
+    )
+    student = lax.all_gather(shard, "z", axis=2, tiled=True)
     routes_z = metas[:, :, :top].astype(jnp.int32)
     place, combine = routing(routes_z, metas[:, :, top:2 * top], z, ny, cap)
     slots = nz * cap
@@ -441,22 +506,21 @@
     teacher = pad_lanes(teacher.reshape(nz, block, blocks // nr, blk)).reshape(nz, block, wide // nr)
 
     plane_tokens = plane_tokens.reshape(NX * tok, wide)
-    gate = dot(plane_tokens, inner[0], ((1,), (1,)))
-    up = dot(plane_tokens, inner[1], ((1,), (1,)))
+    gate = dot(plane_tokens, student[0], ((1,), (1,)))
+    up = dot(plane_tokens, student[1], ((1,), (1,)))
     hidden = (jax.nn.silu(gate) * up).astype(BF)
     hidden_both = lax.all_gather(hidden, "row", axis=1, tiled=True)
-    outer_both = lax.all_to_all(outer.reshape(sub, nr, wide // nr), "row", split_axis=1, concat_axis=0, tiled=True)
-    outer_both = outer_both.reshape(nr * sub, wide // nr)
-    y_part = dot(hidden_both, outer_both, ((1,), (0,))).astype(BF)
     span = wide // nr
+    y_part = sum(dot(hidden_both[:, i * sub:(i + 1) * sub], student[2, :, i * span:(i + 1) * span], ((1,), (0,))) for i in range(nr)).astype(BF)
+    wing = span // 2
+    buffers = [(2, 2, ny, block, wing), (2, 1, ny, block, wing), (2, 2, NX, block, wing), (2, 1, NX, block, wing)]
+    buffers += [(ny, block, wing), (NX, block, wing)] + [(2, 2, block, wing), (2, 1, block, wing)] * 2
+    buffers += [(2, steps, block, span), (2, steps - 1, block, span)]
     gap_round, loss = kernel_call(
         functools.partial(gap_kernel, nz), 4,
-        [shape((experts, block, span), BF), shape((block, 128), F32)],
-        [pltpu.VMEM((experts - 1, block, span), BF)]
-        + [pltpu.VMEM((2, steps, block, span), BF), pltpu.VMEM((2, steps - 1, block, span), BF)]
-        + [pltpu.VMEM((block, span), F32)]
-        + [dma(experts - 1)] * 2 + [dma(2, steps)] * 2 + [dma(experts - 1)] * 2,
-        y_part.reshape(experts, block, span), teacher,
+        [shape((NX, ny, block, span), BF), shape((block, 128), F32)],
+        [pltpu.VMEM(b, BF) for b in buffers] + [pltpu.VMEM((block, span), F32)] + [dma(9, 2, steps, 1)] * 2,
+        y_part.reshape(NX, ny, block, span), teacher,
     )
     term = (dot(hidden_both, gap_round.reshape(experts * block, span), ((0,), (0,))) / tok).astype(BF)
     chunk = NX * lanes
@@ -465,7 +529,7 @@
         [shape((NX, sub, lanes), BF), shape((nr * ny, block, 128), F32)],
         [pltpu.VMEM((nz, sub, chunk), BF), pltpu.VMEM((2, steps, sub, chunk), BF)]
         + [pltpu.VMEM((2, steps - 1, sub, chunk), BF), pltpu.VMEM((sub, chunk), BF)]
-        + [dma(2, steps)] * 2 + [dma(steps)] * 2 + [dma(3)] * 2 + [dma(2 * ny - 1)] * 2 + [dma(steps + 2)],
+        + [dma(2, steps, 2)] * 2 + [dma(steps)] * 2 + [dma(3)] * 2 + [dma(2 * ny - 1)] * 2 + [dma(steps + 2)],
         term, loss,
     )
     token_loss = jnp.sum(losses.reshape(nr, ny * block, 128), axis=(0, 2)) / width

time: 301 us -> 265 us (0.88)
  Pallas kernels: 226 us -> 191 us
  waiting for transfers between devices: 0.56 us -> 6.29 us
  starting transfers between devices: 5.58 us -> 0.04 us
    pallas_call x6 -> x5, Pallas kernels: 226 us -> 191 us  [kernel_call(): pl.pallas_call(body, out_shape=outs, in_specs=[whole] * len(args), out_sp...]
    all_gather x2 -> x1, waiting for transfers between devices: 0.02 us -> 6.28 us  [on_device(): student = lax.all_gather(shard, 'z', axis=2, tiled=True)]
    all_to_all x1 -> x0, starting transfers between devices: 5.32 us -> none  [on_device(): lax.all_to_all(outer.reshape(sub, nr, wide // nr), 'row', split_axis=1, c...]
    reshape x1 -> x0, local copies, waits for them, and re-layouts: 3.35 us -> none  [on_device(): outer.reshape(sub, nr, wide // nr)]
    dot_general x8 -> x9, matrix products: 32 us -> 31.3 us  [dot(): return lax.dot_general(a, b, (dims, ((), ())), preferred_element_type=F32)]
  transfers between devices with their start and end apart: 3 -> 1, of which waited for: 0 -> 1; matrix products, arithmetic and copies ran while one was open for 11% -> 8% of each run, Pallas kernels for 31% -> 18%
where the time goes in v3:
time: 265 us; the launch traced here: 264 us
  Pallas kernels  191 us (72%)
  matrix products  31.3 us (12%)
  between operations  14.3 us (5%)
  local copies, waits for them, and re-layouts  13.8 us (5%)
  waiting for transfers between devices  6.29 us (2%)
  other arithmetic  5.08 us (2%)
  blocking collectives  2.9 us (1%)
    pallas_call x5, Pallas kernels, kernel_call(): pl.pallas_call(body, out_shape=outs, in_specs=[whole] * len(args), out_sp...  191 us
    dot_general x9, matrix products, dot(): return lax.dot_general(a, b, (dims, ((), ())), preferred_element_type=F32)  31.3 us
    all_gather x1, waiting for transfers between devices, on_device(): student = lax.all_gather(shard, 'z', axis=2, tiled=True)  6.28 us
  transfers between devices with their start and end apart: 1, of which 1 were waited for; matrix products, arithmetic and copies ran while one was open for 8% of the time, Pallas kernels for 18%

profile of v3, /device:TPU:1, one launch (start us, length us, event | category | flops | bytes accessed | tf_op | source)
XLA Modules:
  0.0 264.4 jit_solution(15266992906815482490)
XLA Ops:
  8.7 1.3 pad_maximum_fusion
  9.9 0.9 copy.45
  10.9 3.0 %reshape.95 = bf16[160,32,112]{2,1,0:T(8,128)(2,1)S(1)} reshape(bf16[160,3584]{1,0:T(8,128)(2,1)} %param.7) | data formatting | bytes 2293760 | tf_op jit(solution)/shard_map/reshape | solution.py:469
  14.9 0.9 dynamic_slice.3.mine
  15.8 47.0 %shard_map.86 = (bf16[4,160,4096]{2,1,0:T(8,128)(2,1)}, bf16[8,40,1792]{2,1,0:T(8,128)(2,1)S(1)}, f32[8,40,128]{2,1,0:T(8,128)S(1)}, bf16[3,288,512]{2,1,0:T(8,128)(2,1)S(1)}) custom-call(bf16[160,4096]{1,0:T(8,128)(2,1)S(1)} %bitcast.67, bf16[40,1792]{1,0:T(8,128)(2,1)S(1)} %dynamic_slice.3.mine, f32[40,128]{1,0:T(8,128)S(1)} %pad.17.meta, ...), custom_call_target="tpu_custom_call" | custom-call | tf_op jit(solution)/shard_map/pallas_call | solution.py:54
  62.9 0.9 copy-done.1
  65.6 0.9 convolution_convert_fusion.1
  66.5 24.6 %shard_map.87 = bf16[16,24,3584]{2,1,0:T(8,128)(2,1)S(1)} custom-call(bf16[16,24,1792]{2,1,0:T(8,128)(2,1)S(1)} %bitcast.66), custom_call_target="tpu_custom_call" | custom-call | tf_op jit(solution)/shard_map/pallas_call | solution.py:54
  91.1 4.6 %fusion.3 = f32[384,512]{1,0:T(8,128)} fusion(bf16[384,3584]{1,0:T(8,128)(2,1)S(1)} %bitcast.69, bf16[1,2,3584,512]{3,2,1,0:T(8,128)(2,1)} %param.10), kind=kOutput, calls=%fused_computation.6 | convolution fusion | flops 1409286144 | bytes 7208960 | tf_op jit(solution)/shard_map/dot_general | solution.py:22
  95.7 8.2 %convolution_convert_fusion = bf16[384,3584]{1,0:T(8,128)(2,1)} fusion(bf16[1,512,3584]{2,1,0:T(8,128)(2,1)} %param.11, bf16[384,3584]{1,0:T(8,128)(2,1)S(1)} %bitcast.70, bf16[1,2,3584,512]{3,2,1,0:T(8,128)(2,1)} %param.10, f32[384,512]{1,0:T(8,128)} %fusion.3), kind=kOutput, calls=%fused_computation | convolution fusion | flops 2821128192 | bytes 13631488 | tf_op jit(solution)/shard_map/dot_general | solution.py:22
  103.9 1.8 copy-done
  105.7 23.9 %shard_map.88 = bf16[16,24,1792]{2,1,0:T(8,128)(2,1)S(1)} custom-call(bf16[16,24,3584]{2,1,0:T(8,128)(2,1)S(1)} %bitcast.71), custom_call_target="tpu_custom_call" | custom-call | tf_op jit(solution)/shard_map/pallas_call | solution.py:54
  130.4 1.1 fusion.11
  131.5 2.4 reshape.105
  134.7 6.3 %all-gather.2.cloned.1.call-done = bf16[3,288,4096]{2,1,0:T(8,128)(2,1)} async-done(((bf16[3,288,512]{2,1,0:T(8,128)(2,1)}), bf16[3,288,4096]{2,1,0:T(8,128)(2,1)}) %all-gather.2.cloned.1.call-update) | async-done | bytes 7077904 | tf_op jit(solution)/shard_map/all_gather | solution.py:480
  141.0 5.4 %fusion.15 = f32[640,288]{0,1:T(8,128)S(1)} fusion(bf16[640,4096]{1,0:T(8,128)(2,1)} %bitcast.80, bf16[3,288,4096]{2,1,0:T(8,128)(2,1)} %all-gather.2.cloned.1.call-done), kind=kOutput, calls=%fused_computation.19 | convolution fusion | flops 1509949440 | bytes 8339456 | tf_op jit(solution)/shard_map/dot_general | solution.py:22
  146.4 4.5 %fusion.23 = bf16[640,288]{0,1:T(8,128)(2,1)S(1)} fusion(bf16[640,4096]{1,0:T(8,128)(2,1)} %bitcast.81, bf16[3,288,4096]{2,1,0:T(8,128)(2,1)S(1)} %copy-done.2, f32[640,288]{0,1:T(8,128)S(1)} %fusion.15), kind=kOutput, calls=%fused_computation.24 | convolution fusion | flops 1511055360 | bytes 8708096 | tf_op jit(solution)/shard_map/dot_general | solution.py:22
  151.0 2.9 %all_gather.7 = bf16[640,576]{0,1:T(8,128)(2,1)S(1)} all-gather(bf16[640,288]{0,1:T(8,128)(2,1)S(1)} %fusion.23), channel_id=1, replica_groups=mesh['z'=8,'x'=4,'row'=2,'col'=4] {'row'}, dimensions={1}, use_global_device_ids=true | all-gather | bytes 1105920 | tf_op jit(solution)/shard_map/all_gather | solution.py:512
  153.9 1.6 fusion.24
  155.4 3.1 %add_convert_fusion = bf16[640,2048]{1,0:T(8,128)(2,1)} fusion(f32[640,2048]{1,0:T(8,128)S(1)} %fusion.24, bf16[3,288,4096]{2,1,0:T(8,128)(2,1)S(1)} %copy-done.2, bf16[640,576]{0,1:T(8,128)(2,1)S(1)} %all_gather.7), kind=kOutput, calls=%fused_computation.1 | convolution fusion | flops 757596160 | bytes 9412608 | tf_op jit(solution)/shard_map/dot_general | solution.py:22
  158.5 50.3 %shard_map.89 = (bf16[4,4,40,2048]{3,2,1,0:T(8,128)(2,1)S(1)}, f32[40,128]{1,0:T(8,128)S(1)}) custom-call(bf16[4,4,40,2048]{3,2,1,0:T(8,128)(2,1)} %bitcast.76, bf16[8,40,2048]{2,1,0:T(8,128)(2,1)S(1)} %reshape.106.teacher), custom_call_target="tpu_custom_call" | custom-call | tf_op jit(solution)/shard_map/pallas_call | solution.py:54
  208.8 2.0 multiply_convert_fusion.term
  210.8 44.9 %shard_map.90 = (bf16[4,288,128]{2,1,0:T(8,128)(2,1)S(1)}, f32[8,40,128]{2,1,0:T(8,128)S(1)}) custom-call(bf16[576,2048]{1,0:T(8,128)(2,1)S(1)} %multiply_convert_fusion.term, f32[40,128]{1,0:T(8,128)S(1)} %get-tuple-element.15.loss), custom_call_target="tpu_custom_call" | custom-call | tf_op jit(solution)/shard_map/pallas_call | solution.py:54
  256.7 0.8 convert_element_type.72
  (38 shorter events, 6.9 us)
Async XLA Ops:
  7.2 133.9 %all-gather.2.cloned.1.call-start = ((), (), s32[]{:S(2)}) async-start(), calls=%async_computation | async-start | bytes 7962624 | tf_op jit(solution)/shard_map/all_gather | solution.py:480
  62.8 0.9 copy-start.1
  103.9 1.8 copy-start
  141.0 5.4 %copy-start.2 = (bf16[3,288,4096]{2,1,0:T(8,128)(2,1)S(1)}, bf16[3,288,4096]{2,1,0:T(8,128)(2,1)}, u32[]{:S(2)}) copy-start(bf16[3,288,4096]{2,1,0:T(8,128)(2,1)} %all-gather.2.cloned.1.call-done) | copy-start | bytes 21233668
Sparse Core Ops, SparseCore 0:
  63.9 77.0 all-gather.1

commit v4 on v3

--- a/solution.py
+++ b/solution.py
@@ -49,12 +49,12 @@
     return pl.ds(pl.multiple_of(start * size, size), size)
 
 
-def kernel_call(body, number, outs, scratch, *args):
+def kernel_call(body, number, outs, scratch, *args, specs=None):
     whole = pl.BlockSpec(memory_space=pltpu.VMEM)
     return pl.pallas_call(
         body,
         out_shape=outs,
-        in_specs=[whole] * len(args),
+        in_specs=specs or [whole] * len(args),
         out_specs=[whole] * len(outs),
         scratch_shapes=scratch,
         compiler_params=pltpu.CompilerParams(
@@ -73,51 +73,73 @@
     return sorted(steps, key=far, reverse=True)
 
 
-def tokens_kernel(nz, padded, mine, meta, parts, plane, column, metas, shard, xs, xr, ys, yr, cs, cr, zs, zr, ms, mr, ws, wr, own):
+def weights_kernel(nz, parts, shard, send, recv, own):
+    z, x, r, y = here()
+    per = nz // 2
+    core = z // per
+    plane_z = per * r + z % per
+    moves = core != r
+    peers = [(z, (x + d) % NX, r, y) for d in (1, 2, 3)]
+    peers += [(plane_z, (x + d) % NX, core, y) for d in (1, 2, 3)]
+
+    @pl.when(moves)
+    def _():
+        greet(peers + [(plane_z, x, core, y)])
+
+    @pl.when(jnp.logical_not(moves))
+    def _():
+        greet(peers)
+
+    slot = lanes_at(x, 128)
+    copies = []
+    for d in (2, 1, 3):
+        to = (x + d) % NX
+        for kind in (2, 0, 1):
+            device = (plane_z, to, core, y) if kind == 2 else (z, to, r, y)
+            copies.append(remote(parts.at[kind, to], shard.at[kind, :, slot], send.at[d, kind], recv.at[d, kind], device))
+            copies[-1].start()
+    for kind in (0, 1):
+        copies.append(pltpu.make_async_copy(parts.at[kind, x], shard.at[kind, :, slot], own.at[kind]))
+        copies[-1].start()
+    down_own = remote(parts.at[2, x], shard.at[2, :, slot], send.at[0, 2], recv.at[0, 2], (plane_z, x, core, y))
+    down_here = pltpu.make_async_copy(parts.at[2, x], shard.at[2, :, slot], own.at[2])
+
+    @pl.when(moves)
+    def _():
+        down_own.start()
+        down_own.wait()
+
+    @pl.when(jnp.logical_not(moves))
+    def _():
+        down_here.start()
+        down_here.wait()
+
+    for copy in copies:
+        copy.wait()
+
+
+def tokens_kernel(nz, padded, mine, meta, plane, column, metas, xs, xr, ys, yr, cs, cr, zs, zr, ms, mr, own):
     z, x, r, y = here()
     up, down = (z + 1) % nz, (z + nz - 1) % nz
     ny = lax.axis_size("col")
     north, south = (y + 1) % ny, (y + ny - 1) % ny
     sibling = (z, x, 1 - r, y)
-    per = nz // 2
-    core = z // per
-    plane_z = per * r + z % per
-    moves = core != r
-    others = [(z, (x + d) % NX, r, y) for d in (1, 2, 3)]
-    others += [(plane_z, (x + d) % NX, core, y) for d in (1, 2, 3)]
-    others += [(z, x, r, north), (z, x, r, south), (up, x, r, y), (down, x, r, y), sibling]
-
-    @pl.when(moves)
-    def _():
-        greet(others + [(plane_z, x, core, y)])
-
-    @pl.when(jnp.logical_not(moves))
-    def _():
-        greet(others)
-
+    greet(
+        [(z, (x + d) % NX, r, y) for d in (1, 2, 3)]
+        + [(z, x, r, north), (z, x, r, south), (up, x, r, y), (down, x, r, y), sibling]
+    )
     rows, wide = padded.shape
     high, span = rows // 2, wide // 2
     quarter = span // 2
     mine_rows = pl.ds(pl.multiple_of(r * high, high), high)
     parity = y % 2
     held = lanes_at(parity, span)
-    slot = lanes_at(x, 128)
     started = []
 
     def go(copy):
         copy.start()
         started.append(copy)
         return copy
-
-    local = [
-        pltpu.make_async_copy(padded, plane.at[x], own.at[0]),
-        pltpu.make_async_copy(mine, column.at[z], own.at[1]),
-        pltpu.make_async_copy(meta, metas.at[z], own.at[2]),
-        pltpu.make_async_copy(parts.at[0, x], shard.at[0, :, slot], own.at[3]),
-        pltpu.make_async_copy(parts.at[1, x], shard.at[1, :, slot], own.at[4]),
-    ]
-    for copy in local:
-        copy.start()
 
     def z_step(s):
         half = mine.shape[1] // 2
@@ -143,122 +165,139 @@
         for copy in copies:
             copy.wait_recv()
 
-    ring = z_step(1)
-    from_x = {}
-    for d in (2, 1, 3):
+    def x_step(d):
         device = (z, (x + d) % NX, r, y)
-        from_x[d] = go(remote(padded.at[mine_rows, held], plane.at[x, mine_rows, held], xs.at[d - 1], xr.at[d - 1], device))
-    weights = []
-    for d in (2, 1, 3):
-        to = (x + d) % NX
-        for kind in (0, 1):
-            weights.append(go(remote(parts.at[kind, to], shard.at[kind, :, slot], ws.at[d, kind], wr.at[d, kind], (z, to, r, y))))
-        weights.append(go(remote(parts.at[2, to], shard.at[2, :, slot], ws.at[d, 2], wr.at[d, 2], (plane_z, to, core, y))))
-    down_own = remote(parts.at[2, x], shard.at[2, :, slot], ws.at[0, 2], wr.at[0, 2], (plane_z, x, core, y))
-    down_here = pltpu.make_async_copy(parts.at[2, x], shard.at[2, :, slot], own.at[5])
-
-    @pl.when(moves)
-    def _():
-        down_own.start()
-
-    @pl.when(jnp.logical_not(moves))
-    def _():
-        down_here.start()
-
-    turn = 0
+        return go(remote(padded.at[mine_rows, held], plane.at[x, mine_rows, held], xs.at[d - 1], xr.at[d - 1], device))
+
     from_sib, from_y = [], []
-    for d in (1, 3, 2):
-        arrived(ring)
-        turn += 1
-        ring = z_step(turn + 1)
-        from_x[d].wait_recv()
+
+    def onward(d, copy):
+        copy.wait_recv()
         source = (x + NX - d) % NX
         for side, device in ((0, (z, x, r, north)), (1, (z, x, r, south))):
             piece = plane.at[source, mine_rows, lanes_at(parity * 2 + side, quarter)]
             from_y.append((d, side, go(remote(piece, piece, ys.at[side, d - 1], yr.at[side, d - 1], device))))
         piece = plane.at[source, mine_rows, held]
         from_sib.append(go(remote(piece, piece, cs.at[0, d - 1], cr.at[0, d - 1], sibling)))
+
+    first, third = x_step(1), x_step(3)
+    ring = z_step(1)
+    local = [
+        pltpu.make_async_copy(padded, plane.at[x], own.at[0]),
+        pltpu.make_async_copy(mine, column.at[z], own.at[1]),
+        pltpu.make_async_copy(meta, metas.at[z], own.at[2]),
+    ]
+    for copy in local:
+        copy.start()
     arrived(ring)
+    ring = z_step(2)
+    onward(1, first)
+    second = x_step(2)
+    onward(3, third)
+    arrived(ring)
+    ring = z_step(3)
+    arrived(ring)
+    ring = z_step(4)
+    onward(2, second)
     for d, side, copy in from_y:
         copy.wait_recv()
         source = (x + NX - d) % NX
         piece = plane.at[source, mine_rows, lanes_at((1 - parity) * 2 + side, quarter)]
         from_sib.append(go(remote(piece, piece, cs.at[1 + side, d - 1], cr.at[1 + side, d - 1], sibling)))
-    arrived(weights)
+    arrived(ring)
     arrived(from_sib)
     for copy in started:
         copy.wait_send()
     for copy in local:
         copy.wait()
 
-    @pl.when(moves)
-    def _():
-        down_own.wait()
-
-    @pl.when(jnp.logical_not(moves))
-    def _():
-        down_here.wait()
-
-
-def dispatch_kernel(outgoing, got, send, recv, fsend, frecv, own):
+
+def teacher_kernel(outgoing, inner, outer, back, w_in, w_out, got, act, part, other, total,
+                   send, recv, fsend, frecv, csend, crecv, bsend, brecv, own):
     z, x, r, y = here()
     ny = lax.axis_size("col")
-    steps = plane_steps(ny)
+    steps = plane_steps(ny)[::-1]
     sibling = (z, x, 1 - r, y)
     greet([(z, (x + dx) % NX, r, (y + dy) % ny) for dx, dy in steps] + [sibling])
+    steps = [(0, 0)] + steps
     me = x * ny + y
-    mine = lanes_at(r, outgoing.shape[2])
-    local = pltpu.make_async_copy(outgoing.at[me], got.at[me, :, mine], own.at[0])
+    half = outgoing.shape[2]
+    keep, give = lanes_at(r, half), lanes_at(1 - r, half)
+    near = len(steps) // 2
+    groups = (range(near), range(near, len(steps)))
+    local = pltpu.make_async_copy(outgoing.at[me], got.at[0, :, keep], own.at[0])
     local.start()
-    sends, forwards = [], []
+    loads = [pltpu.make_async_copy(inner, w_in, own.at[1]), pltpu.make_async_copy(outer, w_out, own.at[2])]
+    sends, forwards, swaps, returns = {}, {}, {}, []
+
+    def forward(k, src):
+        forwards[k] = remote(src, got.at[k, :, keep], fsend.at[k], frecv.at[k], sibling)
+        forwards[k].start()
+
     for k, (dx, dy) in enumerate(steps):
-        tx, ty = (x + dx) % NX, (y + dy) % ny
-        sends.append(remote(outgoing.at[tx * ny + ty], got.at[me, :, mine], send.at[k], recv.at[k], (z, tx, r, ty)))
-        sends[-1].start()
-    forwards.append(remote(outgoing.at[me], got.at[me, :, mine], fsend.at[len(steps)], frecv.at[len(steps)], sibling))
-    forwards[-1].start()
-    for k, (dx, dy) in reversed(list(enumerate(steps))):
-        sends[k].wait_recv()
-        source = (x + NX - dx) % NX * ny + (y + ny - dy) % ny
-        piece = got.at[source, :, mine]
-        forwards.append(remote(piece, piece, fsend.at[k], frecv.at[k], sibling))
-        forwards[-1].start()
-    for copy in forwards:
+        if k:
+            tx, ty = (x + dx) % NX, (y + dy) % ny
+            sends[k] = remote(outgoing.at[tx * ny + ty], got.at[k, :, keep], send.at[k], recv.at[k], (z, tx, r, ty))
+            sends[k].start()
+        if k == near - 1:
+            loads[0].start()
+    loads[1].start()
+    forward(0, outgoing.at[me])
+
+    def finish(g):
+        swaps[g].wait_recv()
+        for k in groups[g]:
+            dx, dy = steps[k]
+            tx, ty = (x + NX - dx) % NX, (y + ny - dy) % ny
+            value = (part[k, :, keep].astype(F32) + other[k].astype(F32)).astype(BF)
+            if k:
+                total[k] = value
+                returns.append(remote(total.at[k], back.at[me], bsend.at[k], brecv.at[k], (z, tx, r, ty)))
+                returns[-1].start()
+            else:
+                back[me] = value
+
+    for g, group in enumerate(groups):
+        slots = pl.ds(group[0], near)
+        for k in group:
+            if k:
+                sends[k].wait_recv()
+                forward(k, got.at[k, :, keep])
+        if g == 0:
+            local.wait()
+            loads[0].wait()
+        for k in group:
+            forwards[k].wait_recv()
+        rows = near * outgoing.shape[1]
+        tile = w_in.shape[2] // 2
+
+        @pl.loop(0, 2)
+        def _(j):
+            lhs = got[slots].reshape(rows, got.shape[2])
+            cut = pl.ds(pl.multiple_of(j * tile, tile), tile)
+            gate = jnp.dot(lhs, w_in[0, :, cut], preferred_element_type=F32)
+            up = jnp.dot(lhs, w_in[1, :, cut], preferred_element_type=F32)
+            act[:, cut] = (gate / (1.0 + jnp.exp(-gate)) * up).astype(BF)
+
+        if g == 0:
+            loads[1].wait()
+        wide = half // 2
+
+        def down(side):
+            @pl.loop(0, 2)
+            def _(j):
+                cut = pl.ds(pl.multiple_of(side * half + j * wide, wide), wide)
+                value = jnp.dot(act[...], w_out[:, cut], preferred_element_type=F32).astype(BF)
+                part[slots, :, cut] = value.reshape(near, outgoing.shape[1], wide)
+
+        down(1 - r)
+        swaps[g] = remote(part.at[slots, :, give], other.at[slots], csend.at[g], crecv.at[g], sibling)
+        swaps[g].start()
+        down(r)
+        finish(g)
+    for copy in returns:
         copy.wait()
-    for copy in sends:
-        copy.wait_send()
-    local.wait()
-
-
-def return_kernel(part, back, other, total, send, recv, csend, crecv):
-    z, x, r, y = here()
-    ny = lax.axis_size("col")
-    steps = plane_steps(ny)
-    sibling = (z, x, 1 - r, y)
-    greet([(z, (x + dx) % NX, r, (y + dy) % ny) for dx, dy in steps] + [sibling])
-    me = x * ny + y
-    half = back.shape[2]
-    keep, give = lanes_at(r, half), lanes_at(1 - r, half)
-    steps = steps + [(0, 0)]
-    swaps, sends = [], []
-    for k, (dx, dy) in enumerate(steps):
-        to = (x + dx) % NX * ny + (y + dy) % ny
-        swaps.append(remote(part.at[to, :, give], other.at[to], csend.at[k], crecv.at[k], sibling))
-        swaps[-1].start()
-    for k, (dx, dy) in enumerate(steps):
-        tx, ty = (x + dx) % NX, (y + dy) % ny
-        to = tx * ny + ty
-        swaps[k].wait_recv()
-        value = (part[to, :, keep].astype(F32) + other[to].astype(F32)).astype(BF)
-        if dx or dy:
-            total[to] = value
-            sends.append(remote(total.at[to], back.at[me], send.at[k], recv.at[k], (z, tx, r, ty)))
-            sends[-1].start()
-        else:
-            back[me] = value
-    for copy in sends:
-        copy.wait()
-    for copy in swaps:
+    for copy in list(sends.values()) + list(forwards.values()) + list(swaps.values()):
         copy.wait_send()
 
 
@@ -318,8 +357,7 @@
                 rings.remove(ring)
 
 
-def gap_kernel(nz, parts, teacher, gaps, loss, xcame, xleave, ycame, yleave, xsum, ysum, xcame2, xleave2, ycame2, yleave2,
-               tcame, tleave, total, send, recv):
+def gap_kernel(nz, count, parts, teacher, gaps, loss, tcame, tleave, total, send, recv, *buffers):
     z, x, r, y = here()
     ny = lax.axis_size("col")
     up, down = ((z + 1) % nz, x, r, y), ((z + nz - 1) % nz, x, r, y)
@@ -327,10 +365,9 @@
     north, south = (z, x, r, (y + 1) % ny), (z, x, r, (y + ny - 1) % ny)
     greet([east, west, north, south, up, down])
     span = teacher.shape[2]
-    wing = span // 2
+    wing = span // count
     every = slice(None)
-    first, second = pl.ds(0, wing), pl.ds(wing, wing)
-    copies = [{} for _ in range(9)]
+    copies = [{} for _ in range(4 * count + 1)]
 
     def sems(k):
         return send.at[k], recv.at[k], copies[k]
@@ -341,38 +378,45 @@
     def lanes(start, size):
         return tuple((every, pl.ds(start + o, s)) for o, s in ((0, size), (0, size // 2), (size // 2, size // 2)))
 
-    teach = ring_sum(nz, z, up, down, teacher, lambda d, p: (d,) + p, [lanes(0, span)], tcame, tleave, *sems(0))
-    ring_x = ring_sum(NX, x, east, west, parts, lambda d, p: (d,) + p + (every, first), [trio(ny)], xcame, xleave, *sems(1))
-    ring_y = ring_sum(ny, y, north, south, parts, lambda d, p: p + (d, every, second), [trio(NX)], ycame, yleave, *sems(2))
-    next(ring_x)
-    next(ring_y)
-    next(teach)
-    together(ring_x, ring_y)
-    xsum[...] = (parts[x, :, :, first].astype(F32) + xcame[0, NX // 2 - 1].astype(F32) + xcame[1, NX // 2 - 1].astype(F32)).astype(BF)
-    ring_y = ring_sum(ny, y, north, south, xsum, lambda d, p: (d,) + p, [lanes(0, wing)], ycame2, yleave2, *sems(3))
-    next(ring_y)
-    ysum[...] = (parts[:, y, :, second].astype(F32) + ycame[0, ny // 2 - 1].astype(F32) + ycame[1, ny // 2 - 1].astype(F32)).astype(BF)
-    ring_x = ring_sum(NX, x, east, west, ysum, lambda d, p: (d,) + p, [lanes(0, wing)], xcame2, xleave2, *sems(4))
-    next(ring_x)
-    together(teach, ring_y, ring_x)
-    taught = teacher[z].astype(F32) + tcame[0, nz // 2 - 1].astype(F32) + tcame[1, nz // 2 - 1].astype(F32)
-    total[...] = -taught
-    total[:, first] += xsum[y].astype(F32) + ycame2[0, ny // 2 - 1].astype(F32) + ycame2[1, ny // 2 - 1].astype(F32)
-    total[:, second] += ysum[x].astype(F32) + xcame2[0, NX // 2 - 1].astype(F32) + xcame2[1, NX // 2 - 1].astype(F32)
-    gaps[x, y] = total[...].astype(BF)
-    gather_y = ring_gather(ny, y, north, south, gaps, lambda d, p: (x, d) + p, *lanes(0, wing), *sems(5))
-    gather_x = ring_gather(NX, x, east, west, gaps, lambda d, p: (d, y) + p, *lanes(wing, wing), *sems(6))
-    next(gather_y)
-    next(gather_x)
+    along_x, along_y = (NX, x, east, west), (ny, y, north, south)
+
+    def flow(f):
+        start = f * wing
+        cut = pl.ds(start, wing)
+        came, leave, mid, came2, leave2 = buffers[5 * f:5 * f + 5]
+        x_first = f < count // 2
+        one, two = (along_x, along_y) if x_first else (along_y, along_x)
+
+        def outer(d, p):
+            return (d,) + p + (every, cut) if x_first else p + (d, every, cut)
+
+        def inner(d, p):
+            return (x, d) + p if x_first else (d, y) + p
+
+        yield from ring_sum(*one, parts, outer, [trio(two[0])], came, leave, *sems(4 * f))
+        last = one[0] // 2 - 1
+        kept = parts[x, :, :, cut] if x_first else parts[:, y, :, cut]
+        mid[...] = (kept.astype(F32) + came[0, last].astype(F32) + came[1, last].astype(F32)).astype(BF)
+        yield from ring_sum(*two, mid, lambda d, p: (d,) + p, [lanes(0, wing)], came2, leave2, *sems(4 * f + 1))
+        last = two[0] // 2 - 1
+        student = mid[two[1]].astype(F32) + came2[0, last].astype(F32) + came2[1, last].astype(F32)
+        last = nz // 2 - 1
+        taught = teacher[z, :, cut].astype(F32) + tcame[0, last, :, cut].astype(F32) + tcame[1, last, :, cut].astype(F32)
+        gap = student - taught
+        gaps[x, y, :, cut] = gap.astype(BF)
+        total[:, cut] = gap
+        yield from ring_gather(*two, gaps, inner, *lanes(start, wing), *sems(4 * f + 2))
+        yield from ring_gather(*one, gaps, outer, *trio(two[0]), *sems(4 * f + 3))
+
+    teach = ring_sum(nz, z, up, down, teacher, lambda d, p: (d,) + p, [lanes(0, span)], tcame, tleave, *sems(4 * count))
+    half = count // 2
+    flows = [flow(k) for pair in zip(range(half), range(half, count)) for k in pair]
+    together(teach, *flows)
     squares = jnp.zeros(loss.shape, F32)
     for tile in range(span // 128):
         value = total[:, pl.ds(tile * 128, 128)]
         squares += value * value
     loss[...] = squares
-    together(gather_y, gather_x)
-    gather_x = ring_gather(NX, x, east, west, gaps, lambda d, p: (d,) + p + (every, first), *trio(ny), *sems(7))
-    gather_y = ring_gather(ny, y, north, south, gaps, lambda d, p: p + (d, every, second), *trio(NX), *sems(8))
-    together(gather_x, gather_y)
     for group in copies:
         for copy in group.values():
             copy.wait_send()
@@ -466,38 +510,40 @@
     parts = pad_lanes(parts)
     lanes = parts.shape[-1]
     wide = blocks * lanes
+    (shard,) = kernel_call(
+        functools.partial(weights_kernel, nz), 0,
+        [shape((3, sub, NX * lanes), BF)],
+        [dma(4, 3), dma(4, 3), dma(3)],
+        parts.reshape(3, NX, sub, lanes),
+    )
     padded = pad_lanes(tokens.reshape(tok, blocks, blk)).reshape(tok, wide)
     mine = lax.dynamic_slice(tokens, (y * block, r * half), (block, half))
     meta = jnp.concatenate([routes.astype(F32), route_weights], axis=1)
     meta = jnp.pad(meta, ((0, 0), (0, 128 - 2 * top)))
+    shard, mine = lax.optimization_barrier((shard, mine))
+    student = lax.all_gather(shard, "z", axis=2, tiled=True)
+
     steps = nz // 2
-    plane_tokens, column, metas, shard = kernel_call(
+    plane_tokens, column, metas = kernel_call(
         functools.partial(tokens_kernel, nz), 1,
-        [shape((NX, tok, wide), BF), shape((nz, block, half), BF), shape((nz, block, 128), F32), shape((3, sub, NX * lanes), BF)],
-        [dma(3), dma(3), dma(2, 3), dma(2, 3), dma(3, 3), dma(3, 3)] + [dma(2, steps)] * 4 + [dma(4, 3)] * 2 + [dma(6)],
-        padded, mine, meta, parts.reshape(3, NX, sub, lanes),
-    )
-    student = lax.all_gather(shard, "z", axis=2, tiled=True)
+        [shape((NX, tok, wide), BF), shape((nz, block, half), BF), shape((nz, block, 128), F32)],
+        [dma(3), dma(3), dma(2, 3), dma(2, 3), dma(3, 3), dma(3, 3)] + [dma(2, steps)] * 4 + [dma(3)],
+        padded, mine, meta,
+    )
     routes_z = metas[:, :, :top].astype(jnp.int32)
     place, combine = routing(routes_z, metas[:, :, top:2 * top], z, ny, cap)
     slots = nz * cap
     outgoing = dot(place, column.reshape(nz * block, half), ((0,), (0,))).astype(BF)
-    (arrived,) = kernel_call(
-        dispatch_kernel, 2,
-        [shape((experts, slots, width), BF)],
-        [dma(experts)] * 4 + [dma(1)],
-        outgoing.reshape(experts, slots, half),
-    )
-    arrived = arrived.reshape(experts * slots, width)
-    gate = dot(arrived, teacher_in[0, 0], ((1,), (0,)))
-    up = dot(arrived, teacher_in[0, 1], ((1,), (0,)))
-    act = (jax.nn.silu(gate) * up).astype(BF)
-    part = dot(act, teacher_out[0], ((1,), (0,))).astype(BF)
+    hid = teacher_in.shape[3]
+    whole, far = pl.BlockSpec(memory_space=pltpu.VMEM), pl.BlockSpec(memory_space=pl.ANY)
+    buffers = [(2, width, hid), (hid, width), (experts, slots, width), (experts // 2 * slots, hid)]
+    buffers += [(experts, slots, width)] + [(experts, slots, half)] * 2
     (back,) = kernel_call(
-        return_kernel, 3,
+        teacher_kernel, 2,
         [shape((experts, slots, half), BF)],
-        [pltpu.VMEM((experts, slots, half), BF)] * 2 + [dma(experts)] * 4,
-        part.reshape(experts, slots, width),
+        [pltpu.VMEM(b, BF) for b in buffers] + [dma(experts)] * 4 + [dma(2)] * 2 + [dma(experts)] * 2 + [dma(3)],
+        outgoing.reshape(experts, slots, half), teacher_in[0], teacher_out[0],
+        specs=[whole, far, far],
     )
     back = back.reshape(experts * slots, half)
     high = combine.astype(BF)
@@ -512,14 +558,19 @@
     hidden_both = lax.all_gather(hidden, "row", axis=1, tiled=True)
     span = wide // nr
     y_part = sum(dot(hidden_both[:, i * sub:(i + 1) * sub], student[2, :, i * span:(i + 1) * span], ((1,), (0,))) for i in range(nr)).astype(BF)
-    wing = span // 2
-    buffers = [(2, 2, ny, block, wing), (2, 1, ny, block, wing), (2, 2, NX, block, wing), (2, 1, NX, block, wing)]
-    buffers += [(ny, block, wing), (NX, block, wing)] + [(2, 2, block, wing), (2, 1, block, wing)] * 2
-    buffers += [(2, steps, block, span), (2, steps - 1, block, span)]
+    count = 4
+    wing = span // count
+    buffers = [(2, steps, block, span), (2, steps - 1, block, span)]
+    flows = []
+    for f in range(count):
+        one, two = (NX, ny) if f < count // 2 else (ny, NX)
+        flows += [(2, one // 2, two, block, wing), (2, one // 2 - 1, two, block, wing), (two, block, wing)]
+        flows += [(2, two // 2, block, wing), (2, two // 2 - 1, block, wing)]
     gap_round, loss = kernel_call(
-        functools.partial(gap_kernel, nz), 4,
+        functools.partial(gap_kernel, nz, count), 4,
         [shape((NX, ny, block, span), BF), shape((block, 128), F32)],
-        [pltpu.VMEM(b, BF) for b in buffers] + [pltpu.VMEM((block, span), F32)] + [dma(9, 2, steps, 1)] * 2,
+        [pltpu.VMEM(b, BF) for b in buffers] + [pltpu.VMEM((block, span), F32)] + [dma(4 * count + 1, 2, steps, 1)] * 2
+        + [pltpu.VMEM(b, BF) for b in flows],
         y_part.reshape(NX, ny, block, span), teacher,
     )
     term = (dot(hidden_both, gap_round.reshape(experts * block, span), ((0,), (0,))) / tok).astype(BF)

time: 265 us -> 229 us (0.86)
  Pallas kernels: 191 us -> 177 us
  matrix products: 31.3 us -> 18.5 us
  waiting for transfers between devices: 6.29 us -> 0.04 us
  local copies, waits for them, and re-layouts: 13.8 us -> 9.23 us
    pallas_call x5, Pallas kernels: 191 us -> 177 us  [kernel_call(): pl.pallas_call(body, out_shape=outs, in_specs=specs or [whole] * len(args...]
    dot_general x9 -> x7, matrix products: 31.3 us -> 18.5 us  [dot(): return lax.dot_general(a, b, (dims, ((), ())), preferred_element_type=F32)]
    all_gather x1, waiting for transfers between devices: 6.28 us -> 0.02 us  [on_device(): student = lax.all_gather(shard, 'z', axis=2, tiled=True)]
    unnamed x9 -> x11, local copies, waits for them, and re-layouts: 4.42 us -> 1.73 us
  transfers between devices with their start and end apart: 1 -> 1, of which waited for: 1 -> 0; matrix products, arithmetic and copies ran while one was open for 8% -> 5% of each run, Pallas kernels for 18% -> 35%
where the time goes in v4:
time: 229 us; the launch traced here: 228 us
  Pallas kernels  177 us (77%)
  matrix products  18.5 us (8%)
  between operations  14.4 us (6%)
  local copies, waits for them, and re-layouts  9.23 us (4%)
  blocking collectives  4.93 us (2%)
  other arithmetic  3.7 us (2%)
    pallas_call x5, Pallas kernels, kernel_call(): pl.pallas_call(body, out_shape=outs, in_specs=specs or [whole] * len(args...  177 us
    dot_general x7, matrix products, dot(): return lax.dot_general(a, b, (dims, ((), ())), preferred_element_type=F32)  18.5 us
    all_gather x1, blocking collectives, on_device(): hidden_both = lax.all_gather(hidden, 'row', axis=1, tiled=True)  4.93 us
  transfers between devices with their start and end apart: 1, of which 0 were waited for; matrix products, arithmetic and copies ran while one was open for 5% of the time, Pallas kernels for 35%

profile of v4, /device:TPU:1, one launch (start us, length us, event | category | flops | bytes accessed | tf_op | source)
XLA Modules:
  0.0 228.3 jit_solution(3065857436703668448)
XLA Ops:
  7.2 1.3 pad_maximum_fusion
  8.5 0.9 copy.45
  9.6 18.7 %shard_map.86 = bf16[3,288,512]{2,1,0:T(8,128)(2,1)} custom-call(bf16[3,4,288,128]{3,2,1,0:T(8,128)(2,1)S(1)} %bitcast.51), custom_call_target="tpu_custom_call" | custom-call | tf_op jit(solution)/shard_map/pallas_call | solution.py:54
  28.4 1.8 reshape.89
  30.7 0.6 copy.48
  31.3 38.8 %shard_map.87 = (bf16[4,160,4096]{2,1,0:T(8,128)(2,1)}, bf16[8,40,1792]{2,1,0:T(8,128)(2,1)S(1)}, f32[8,40,128]{2,1,0:T(8,128)S(1)}) custom-call(bf16[160,4096]{1,0:T(8,128)(2,1)S(1)} %bitcast.50, bf16[40,1792]{1,0:T(8,128)(2,1)S(1)} %dynamic_slice.3.mine, f32[40,128]{1,0:T(8,128)S(1)} %pad.18.meta), custom_call_target="tpu_custom_call" | custom-call | tf_op jit(solution)/shard_map/pallas_call | solution.py:54
  71.3 0.6 and.45
  72.2 0.5 select_n.22
  72.7 0.9 convolution_convert_fusion
  73.5 41.0 %shard_map.88 = bf16[16,24,1792]{2,1,0:T(8,128)(2,1)S(1)} custom-call(bf16[16,24,1792]{2,1,0:T(8,128)(2,1)S(1)} %bitcast.49, bf16[2,3584,512]{2,1,0:T(8,128)(2,1)} %bitcast.57, bf16[512,3584]{1,0:T(8,128)(2,1)} %bitcast.59), custom_call_target="tpu_custom_call" | custom-call | tf_op jit(solution)/shard_map/pallas_call | solution.py:54
  114.6 1.1 fusion.4
  115.7 2.4 %reshape.97 = bf16[8,40,16,112]{3,2,1,0:T(8,128)(2,1)S(1)} reshape(bf16[320,1792]{1,0:T(8,128)(2,1)S(1)} %fusion.4) | data formatting | bytes 2293760 | tf_op jit(solution)/shard_map/reshape | solution.py:552
  118.1 0.3 pad.19
  118.4 0.8 reshape.98.teacher
  119.2 5.4 %fusion.8 = f32[640,288]{0,1:T(8,128)S(1)} fusion(bf16[640,4096]{1,0:T(8,128)(2,1)} %bitcast.62, bf16[3,288,4096]{2,1,0:T(8,128)(2,1)} %all-gather.2.cloned.1.call-done), kind=kOutput, calls=%fused_computation.11 | convolution fusion | flops 1509949440 | bytes 8339456 | tf_op jit(solution)/shard_map/dot_general | solution.py:22
  124.6 4.5 %fusion.10 = bf16[640,288]{0,1:T(8,128)(2,1)S(1)} fusion(bf16[640,4096]{1,0:T(8,128)(2,1)} %bitcast.63, bf16[3,288,4096]{2,1,0:T(8,128)(2,1)S(1)} %copy-done.1, f32[640,288]{0,1:T(8,128)S(1)} %fusion.8), kind=kOutput, calls=%fused_computation.14 | convolution fusion | flops 1511055360 | bytes 8708096 | tf_op jit(solution)/shard_map/dot_general | solution.py:22
  129.2 4.9 %all_gather.7 = bf16[640,576]{0,1:T(8,128)(2,1)S(1)} all-gather(bf16[640,288]{0,1:T(8,128)(2,1)S(1)} %fusion.10), channel_id=1, replica_groups=mesh['z'=8,'x'=4,'row'=2,'col'=4] {'row'}, dimensions={1}, use_global_device_ids=true | all-gather | bytes 1105920 | tf_op jit(solution)/shard_map/all_gather | solution.py:558
  134.1 1.5 fusion.11
  135.7 3.1 %add_convert_fusion = bf16[640,2048]{1,0:T(8,128)(2,1)} fusion(f32[640,2048]{1,0:T(8,128)S(1)} %fusion.11, bf16[3,288,4096]{2,1,0:T(8,128)(2,1)S(1)} %copy-done.1, bf16[640,576]{0,1:T(8,128)(2,1)S(1)} %all_gather.7), kind=kOutput, calls=%fused_computation | convolution fusion | flops 757596160 | bytes 9412608 | tf_op jit(solution)/shard_map/dot_general | solution.py:22
  138.7 39.9 %shard_map.89 = (bf16[4,4,40,2048]{3,2,1,0:T(8,128)(2,1)S(1)}, f32[40,128]{1,0:T(8,128)S(1)}) custom-call(bf16[4,4,40,2048]{3,2,1,0:T(8,128)(2,1)} %bitcast.56, bf16[8,40,2048]{2,1,0:T(8,128)(2,1)S(1)} %reshape.98.teacher), custom_call_target="tpu_custom_call" | custom-call | tf_op jit(solution)/shard_map/pallas_call | solution.py:54
  178.6 2.0 multiply_convert_fusion.term
  180.7 38.9 %shard_map.90 = (bf16[4,288,128]{2,1,0:T(8,128)(2,1)S(1)}, f32[8,40,128]{2,1,0:T(8,128)S(1)}) custom-call(bf16[576,2048]{1,0:T(8,128)(2,1)S(1)} %multiply_convert_fusion.term, f32[40,128]{1,0:T(8,128)S(1)} %get-tuple-element.17.loss), custom_call_target="tpu_custom_call" | custom-call | tf_op jit(solution)/shard_map/pallas_call | solution.py:54
  219.8 0.6 broadcast_multiply_fusion
  220.6 0.8 convert_element_type.64
  (38 shorter events, 2.5 us)
Async XLA Ops:
  7.2 112.0 %all-gather.2.cloned.1.call-start = ((), (), s32[]{:S(2)}) async-start(), calls=%async_computation | async-start | bytes 7962624 | tf_op jit(solution)/shard_map/all_gather | solution.py:524
  8.5 19.9 %copy-start = (bf16[160,3584]{1,0:T(8,128)(2,1)S(1)}, bf16[160,3584]{1,0:T(8,128)(2,1)}, u32[]{:S(2)}) copy-start(bf16[160,3584]{1,0:T(8,128)(2,1)} %param.7) | copy-start | bytes 3440644
  9.6 20.7 %copy-start.2 = (s32[40,8]{0,1:T(8,128)S(1)}, s32[40,8]{0,1:T(8,128)}, u32[]{:S(2)}) copy-start(s32[40,8]{0,1:T(8,128)} %param.8) | copy-start | bytes 3844
  9.6 20.7 %copy-start.3 = (f32[40,8]{0,1:T(8,128)S(1)}, f32[40,8]{0,1:T(8,128)}, u32[]{:S(2)}) copy-start(f32[40,8]{0,1:T(8,128)} %param.9) | copy-start | bytes 3844
  119.2 5.4 %copy-start.1 = (bf16[3,288,4096]{2,1,0:T(8,128)(2,1)S(1)}, bf16[3,288,4096]{2,1,0:T(8,128)(2,1)}, u32[]{:S(2)}) copy-start(bf16[3,288,4096]{2,1,0:T(8,128)(2,1)} %all-gather.2.cloned.1.call-done) | copy-start | bytes 21233668
Sparse Core Ops, SparseCore 0:
  28.5 89.8 all-gather.1

commit v5 on v4

v5 whole, which is shorter than its diff:
```python
import functools

import jax
import jax.numpy as jnp
from jax import lax
from jax.experimental import pallas as pl
from jax.experimental.pallas import tpu as pltpu
from jax.sharding import Mesh, PartitionSpec as P

NX = 4
MESH = pl.DeviceIdType.MESH
F32 = jnp.float32
BF = jnp.bfloat16


def split_mesh(mesh):
    dp, row, col = mesh.devices.shape
    return Mesh(mesh.devices.reshape(dp // NX, NX, row, col), ("z", "x", "row", "col"))


def dot(a, b, dims):
    return lax.dot_general(a, b, (dims, ((), ())), preferred_element_type=F32)


def pad_lanes(a):
    lanes = a.shape[-1]
    wide = -(-lanes // 128) * 128
    return jnp.pad(a, [(0, 0)] * (a.ndim - 1) + [(0, wide - lanes)])


def here():
    return tuple(lax.axis_index(a) for a in ("z", "x", "row", "col"))


def remote(src, dst, send, recv, device):
    return pltpu.make_async_remote_copy(
        src_ref=src, dst_ref=dst, send_sem=send, recv_sem=recv, device_id=device, device_id_type=MESH
    )


def greet(devices):
    barrier = pltpu.get_barrier_semaphore()
    for device in devices:
        pl.semaphore_signal(barrier, inc=1, device_id=device, device_id_type=MESH)
    pl.semaphore_wait(barrier, len(devices))


def lanes_at(start, size):
    return pl.ds(pl.multiple_of(start * size, size), size)


def kernel_call(body, number, outs, scratch, *args, specs=None, out_specs=None):
    whole = pl.BlockSpec(memory_space=pltpu.VMEM)
    return pl.pallas_call(
        body,
        out_shape=outs,
        in_specs=specs or [whole] * len(args),
        out_specs=out_specs or [whole] * len(outs),
        scratch_shapes=scratch,
        compiler_params=pltpu.CompilerParams(
            collective_id=number, has_side_effects=True, vmem_limit_bytes=56 * 1024 * 1024
        ),
    )(*args)


def dma(*shape):
    return pltpu.SemaphoreType.DMA(shape)


def plane_steps(ny):
    steps = [(dx, dy) for dx in range(NX) for dy in range(ny) if dx or dy]
    far = lambda s: min(s[0], NX - s[0]) + min(s[1], ny - s[1])
    return sorted(steps, key=far, reverse=True)


def token_gather(padded, plane, xs, xr, ys, yr, cs, cr, own, started):
    z, x, r, y = here()
    ny = lax.axis_size("col")
    north, south = (y + 1) % ny, (y + ny - 1) % ny
    sibling = (z, x, 1 - r, y)
    rows, wide = padded.shape
    high, span = rows // 2, wide // 2
    quarter = span // 2
    mine_rows = pl.ds(pl.multiple_of(r * high, high), high)
    parity = y % 2
    held = lanes_at(parity, span)

    def go(copy):
        copy.start()
        started.append(copy)
        return copy

    def x_step(d):
        device = (z, (x + d) % NX, r, y)
        return go(remote(padded.at[mine_rows, held], plane.at[x, mine_rows, held], xs.at[d - 1], xr.at[d - 1], device))

    from_sib, from_y = [], []

    def onward(d, copy):
        copy.wait_recv()
        source = (x + NX - d) % NX
        for side, device in ((0, (z, x, r, north)), (1, (z, x, r, south))):
            piece = plane.at[source, mine_rows, lanes_at(parity * 2 + side, quarter)]
            from_y.append((d, side, go(remote(piece, piece, ys.at[side, d - 1], yr.at[side, d - 1], device))))
        piece = plane.at[source, mine_rows, held]
        from_sib.append(go(remote(piece, piece, cs.at[0, d - 1], cr.at[0, d - 1], sibling)))

    def inward():
        while from_y:
            d, side, copy = from_y.pop(0)
            copy.wait_recv()
            source = (x + NX - d) % NX
            piece = plane.at[source, mine_rows, lanes_at((1 - parity) * 2 + side, quarter)]
            from_sib.append(go(remote(piece, piece, cs.at[1 + side, d - 1], cr.at[1 + side, d - 1], sibling)))

    first, third = x_step(1), x_step(3)
    local = pltpu.make_async_copy(padded, plane.at[x], own)
    local.start()
    yield
    onward(1, first)
    onward(3, third)
    second = x_step(2)
    yield
    inward()
    onward(2, second)
    yield
    inward()
    for copy in from_sib:
        copy.wait_recv()
    local.wait()


def block_gather(nz, mine, meta, column, metas, zs, zr, ms, mr, own, started):
    z, x, r, y = here()
    up, down = (z + 1) % nz, (z + nz - 1) % nz
    half = mine.shape[1] // 2

    def go(copy):
        copy.start()
        started.append(copy)
        return copy

    local = [pltpu.make_async_copy(mine, column.at[z], own.at[0]), pltpu.make_async_copy(meta, metas.at[z], own.at[1])]
    for copy in local:
        copy.start()
    ring = []
    for s in range(1, nz // 2 + 1):
        for copy in ring:
            copy.wait_recv()
        a, b = (z + nz - s + 1) % nz, (z + s - 1) % nz
        one, two, three, four = (mine, mine, meta, meta) if s == 1 else (column.at[a], column.at[b], metas.at[a], metas.at[b])
        to_a, to_b = column.at[a], column.at[b]
        if s == nz // 2:
            low, top = pl.ds(0, half), pl.ds(half, half)
            one, to_a, two, to_b = column.at[a, :, low], column.at[a, :, low], column.at[b, :, top], column.at[b, :, top]
        ring = [
            go(remote(one, to_a, zs.at[0, s - 1], zr.at[0, s - 1], (up, x, r, y))),
            go(remote(two, to_b, zs.at[1, s - 1], zr.at[1, s - 1], (down, x, r, y))),
            go(remote(three, metas.at[a], ms.at[0, s - 1], mr.at[0, s - 1], (up, x, r, y))),
        ]
        if s < nz // 2:
            ring.append(go(remote(four, metas.at[b], ms.at[1, s - 1], mr.at[1, s - 1], (down, x, r, y))))
        yield
    for copy in ring:
        copy.wait_recv()
    for copy in local:
        copy.wait()


def place_rows(nz, cap, column, metas, outgoing, weighted):
    z = lax.axis_index("z")
    block, half = column.shape[1], column.shape[2]
    experts = outgoing.shape[0]
    top = metas.shape[1] // 2
    count = nz * block
    named = jnp.concatenate([metas[b, :top, :block] for b in range(nz)], axis=1)
    weights = jnp.concatenate([metas[b, top:, :block] for b in range(nz)], axis=1)
    ids = (z * experts + lax.broadcasted_iota(jnp.int32, (experts, 1), 0)).astype(F32)
    hit = jnp.zeros((experts, count), F32)
    weight = jnp.zeros((experts, count), F32)
    for k in range(top):
        hit += jnp.where(named[k:k + 1] == ids, 1.0, 0.0)
        weight += jnp.where(named[k:k + 1] == ids, weights[k:k + 1], 0.0)
    before, after = lax.broadcasted_iota(jnp.int32, (count, count), 0), lax.broadcasted_iota(jnp.int32, (count, count), 1)
    earlier = jnp.where((before < after) & (before // block == after // block), 1.0, 0.0).astype(BF)
    slot = jnp.dot(hit.astype(BF), earlier, preferred_element_type=F32)
    lane = lax.broadcasted_iota(jnp.int32, (nz, count), 1) // block
    inside = jnp.where(lane == lax.broadcasted_iota(jnp.int32, (nz, count), 0), 1.0, 0.0)
    rows = column[...].reshape(count, half)
    for s in range(cap):
        chosen = jnp.where(slot == float(s), hit, 0.0)
        placing = (chosen[:, None, :] * inside[None]).reshape(experts * nz, count).astype(BF)
        value = jnp.dot(placing, rows, preferred_element_type=F32).astype(BF)
        outgoing[:, s * nz:(s + 1) * nz, :] = value.reshape(experts, nz, half)
        chosen = jnp.where(slot == float(s), weight, 0.0)
        weighted[s] = (chosen[:, None, :] * inside[None]).reshape(experts * nz, count)


def weigh_rows(nz, cap, weighted, back, teacher, blk):
    experts, half = back.shape[0], back.shape[2]
    count = weighted.shape[2]
    total = jnp.zeros((count, half), F32)
    for s in range(cap):
        rows = back[:, s * nz:(s + 1) * nz, :].reshape(experts * nz, half)
        value = weighted[s]
        high = value.astype(BF)
        low = (value - high.astype(F32)).astype(BF)
        for term in (high, low):
            total += lax.dot_general(term, rows, (((0,), (0,)), ((), ())), preferred_element_type=F32)
    lanes = -(-blk // 128) * 128
    empty = jnp.zeros((count, lanes - blk), F32)
    for b in range(half // blk):
        piece = jnp.concatenate([total[:, b * blk:(b + 1) * blk], empty], axis=1).astype(BF)
        teacher[:, :, b * lanes:(b + 1) * lanes] = piece.reshape(nz, count // nz, lanes)


def front_kernel(nz, cap, blk, parts, mine, meta, padded, inner, outer, hidden, student_down, teacher,
                 student, plane, metas, weighted, back, w_in, w_out, column, outgoing, got, act, part, other, total,
                 ws, wr, rs, rr, zs, zr, ms, mr, xs, xr, ys, yr, cs, cr, send, recv, fsend, frecv, csend, crecv, bsend, brecv, own):
    z, x, r, y = here()
    ny = lax.axis_size("col")
    steps = plane_steps(ny)[::-1]
    sibling = (z, x, 1 - r, y)
    up, down_z = ((z + 1) % nz, x, r, y), ((z + nz - 1) % nz, x, r, y)
    per = nz // 2
    core = z // per
    plane_z = per * r + z % per
    moves = core != r
    loads = [pltpu.make_async_copy(inner, w_in, own.at[1]), pltpu.make_async_copy(outer, w_out, own.at[2])]
    for copy in loads:
        copy.start()
    peers = [(z, (x + dx) % NX, r, (y + dy) % ny) for dx, dy in steps]
    peers += [sibling, up, down_z] + [(plane_z, (x + d) % NX, core, y) for d in (1, 2, 3)]

    @pl.when(moves)
    def _():
        greet(peers + [(plane_z, x, core, y)])

    @pl.when(jnp.logical_not(moves))
    def _():
        greet(peers)

    started = []
    blocks = block_gather(nz, mine, meta, column, metas, zs, zr, ms, mr, own.at[pl.ds(3, 2)], started)
    tokens = token_gather(padded, plane, xs, xr, ys, yr, cs, cr, own.at[5], started)
    next(blocks)

    span = NX * 128
    exchange = [[], [], []]
    homes = [student.at[0], student.at[1], student_down]
    lane = pl.ds(pl.multiple_of(z * span + x * 128, 128), 128)
    lane_down = pl.ds(pl.multiple_of(plane_z * span + x * 128, 128), 128)
    for kind in (0, 1, 2):
        for d in (2, 1, 3):
            to = (x + d) % NX
            device, cut = ((plane_z, to, core, y), lane_down) if kind == 2 else ((z, to, r, y), lane)
            copy = remote(parts.at[kind, to], homes[kind].at[:, cut], ws.at[d, kind], wr.at[d, kind], device)
            copy.start()
            started.append(copy)
            exchange[kind].append(copy)
    down_own = remote(parts.at[2, x], student_down.at[:, lane_down], ws.at[0, 2], wr.at[0, 2], (plane_z, x, core, y))
    down_here = pltpu.make_async_copy(parts.at[2, x], student_down.at[:, lane], own.at[6])

    @pl.when(moves)
    def _():
        down_own.start()

    @pl.when(jnp.logical_not(moves))
    def _():
        down_here.start()

    local = [pltpu.make_async_copy(parts.at[k, x], student.at[k, :, lane], own.at[7 + k]) for k in (0, 1)]
    for copy in local:
        copy.start()
    next(tokens)

    def chunk(d, p):
        return (slice(None), pl.ds(pl.multiple_of(d * span + p[0], 128), p[1]))

    rings = [{}, {}, {}]
    gathers = [
        ring_gather(nz, z, up, down_z, homes[kind], chunk, (0, span), (0, span // 2), (span // 2, span // 2),
                    rs.at[kind], rr.at[kind], rings[kind])
        for kind in range(3)
    ]

    def serve(*kinds):
        for kind in kinds:
            next(gathers[kind], None)

    for _ in range(per - 1):
        next(blocks)
    for copy in local:
        copy.wait()
    for kind in (0, 1):
        for copy in exchange[kind]:
            copy.wait_recv()
        next(gathers[kind])
    for copy in exchange[2]:
        copy.wait_recv()

    @pl.when(moves)
    def _():
        down_own.wait()

    @pl.when(jnp.logical_not(moves))
    def _():
        down_here.wait()

    next(tokens)
    next(blocks, None)

    place_rows(nz, cap, column, metas, outgoing, weighted)
    steps = [(0, 0)] + steps
    me = x * ny + y
    half = outgoing.shape[2]
    keep, give = lanes_at(r, half), lanes_at(1 - r, half)
    near = len(steps) // 2
    groups = (range(near), range(near, len(steps)))
    sends, forwards, swaps, returns = {}, {}, {}, []

    def forward(k, src):
        forwards[k] = remote(src, got.at[k, :, keep], fsend.at[k], frecv.at[k], sibling)
        forwards[k].start()

    for k, (dx, dy) in enumerate(steps):
        if k:
            tx, ty = (x + dx) % NX, (y + dy) % ny
            sends[k] = remote(outgoing.at[tx * ny + ty], got.at[k, :, keep], send.at[k], recv.at[k], (z, tx, r, ty))
            sends[k].start()
    own_rows = pltpu.make_async_copy(outgoing.at[me], got.at[0, :, keep], own.at[0])
    own_rows.start()
    forward(0, outgoing.at[me])
    serve(0, 1)

    def finish(g):
        swaps[g].wait_recv()
        for k in groups[g]:
            dx, dy = steps[k]
            tx, ty = (x + NX - dx) % NX, (y + ny - dy) % ny
            value = (part[k, :, keep].astype(F32) + other[k].astype(F32)).astype(BF)
            if k:
                total[k] = value
                returns.append(remote(total.at[k], back.at[me], bsend.at[k], brecv.at[k], (z, tx, r, ty)))
                returns[-1].start()
            else:
                back[me] = value

    for g, group in enumerate(groups):
        slots = pl.ds(group[0], near)
        for k in group:
            if k:
                sends[k].wait_recv()
                forward(k, got.at[k, :, keep])
        if g == 0:
            own_rows.wait()
            loads[0].wait()
        for k in group:
            forwards[k].wait_recv()
        rows = near * outgoing.shape[1]
        tile = w_in.shape[2] // 2

        @pl.loop(0, 2)
        def _(j):
            lhs = got[slots].reshape(rows, got.shape[2])
            cut = pl.ds(pl.multiple_of(j * tile, tile), tile)
            gate = jnp.dot(lhs, w_in[0, :, cut], preferred_element_type=F32)
            up_part = jnp.dot(lhs, w_in[1, :, cut], preferred_element_type=F32)
            act[:, cut] = (gate / (1.0 + jnp.exp(-gate)) * up_part).astype(BF)

        if g == 0:
            loads[1].wait()
        wide = half // 2

        def down(side):
            @pl.loop(0, 2)
            def _(j):
                cut = pl.ds(pl.multiple_of(side * half + j * wide, wide), wide)
                value = jnp.dot(act[...], w_out[:, cut], preferred_element_type=F32).astype(BF)
                part[slots, :, cut] = value.reshape(near, outgoing.shape[1], wide)

        down(1 - r)
        swaps[g] = remote(part.at[slots, :, give], other.at[slots], csend.at[g], crecv.at[g], sibling)
        swaps[g].start()
        down(r)
        if g == 0:
            serve(0, 1)
        finish(g)
        next(tokens, None)
        if g == 1:
            serve(0, 1, 2)

    serve(0, 1)
    tok = plane.shape[1]
    for i in range(NX // 2):
        rows = plane[2 * i:2 * i + 2].reshape(2 * tok, plane.shape[2])
        gate = lax.dot_general(rows, student[0], (((1,), (1,)), ((), ())), preferred_element_type=F32)
        up_part = lax.dot_general(rows, student[1], (((1,), (1,)), ((), ())), preferred_element_type=F32)
        hidden[2 * i * tok:2 * (i + 1) * tok] = (gate / (1.0 + jnp.exp(-gate)) * up_part).astype(BF)
        serve(2)
    for copy in returns:
        copy.wait_recv()
    weigh_rows(nz, cap, weighted, back, teacher, blk)
    serve(2)
    serve(2)
    for copy in started + returns + list(sends.values()) + list(forwards.values()) + list(swaps.values()):
        copy.wait_send()
    for ring in rings:
        for copy in ring.values():
            copy.wait_send()


def ring_sum(n, i, up, down, ref, where, subs, came, leave, send, recv, copies):
    half = n // 2

    def go(way, s, u, src, dst):
        copy = remote(src, dst, send.at[way, s, u], recv.at[way, s, u], (up, down)[way])
        copy.start()
        copies[way, s, u] = copy

    for u, (whole, low, top) in enumerate(subs):
        for way, part in ((0, low), (1, top)):
            go(way, 0, u, ref.at[where((i + half) % n, part)], came.at[(way, 0) + part])
    yield
    for s in range(1, half):
        for u, (whole, low, top) in enumerate(subs):
            for way in (0, 1):
                d = (i + half - s) % n if way == 0 else (i + half + s) % n
                copies[way, s - 1, u].wait_recv()
                summed, plain = whole, None
                if s == 1:
                    summed, plain = (low, top) if way == 0 else (top, low)
                    leave[(way, 0) + plain] = ref[where(d, plain)]
                value = ref[where(d, summed)].astype(F32) + came[(way, s - 1) + summed].astype(F32)
                leave[(way, s - 1) + summed] = value.astype(BF)
                go(way, s, u, leave.at[(way, s - 1) + whole], came.at[(way, s) + whole])
        yield
    for u in range(len(subs)):
        for way in (0, 1):
            copies[way, half - 1, u].wait_recv()


def ring_gather(n, i, up, down, ref, where, whole, low, top, send, recv, copies):
    half = n // 2
    for s in range(half):
        for way, device in ((0, up), (1, down)):
            d = (i + n - s) % n if way == 0 else (i + s) % n
            if s:
                copies[way, s - 1].wait_recv()
            part = whole if s < half - 1 else (low, top)[way]
            piece = ref.at[where(d, part)]
            copies[way, s] = remote(piece, piece, send.at[way, s, 0], recv.at[way, s, 0], device)
            copies[way, s].start()
        yield
    for way in (0, 1):
        copies[way, half - 1].wait_recv()


def together(*rings):
    rings = list(rings)
    while rings:
        for ring in list(rings):
            try:
                next(ring)
            except StopIteration:
                rings.remove(ring)


def tail_kernel(nz, count, tok, hidden, weights, teacher, grad, losses, hid, w_out, tcame, tleave, chunks, give, came, leave, total, loss,
                send, recv, zsend, zrecv, csend, crecv, hsend, hrecv, xsend, xrecv, lsend, lrecv, own, *buffers):
    z, x, r, y = here()
    ny = lax.axis_size("col")
    up, down = ((z + 1) % nz, x, r, y), ((z + nz - 1) % nz, x, r, y)
    east, west = (z, (x + 1) % NX, r, y), (z, (x + NX - 1) % NX, r, y)
    north, south = (z, x, r, (y + 1) % ny), (z, x, r, (y + ny - 1) % ny)
    sibling = (z, x, 1 - r, y)
    mates = [(z, x, r, (y + d) % ny) for d in range(1, ny)] + [(z, x, 1 - r, (y + d) % ny) for d in range(ny)]
    across = [(d, (x + d) % NX) for d in (2, 1, 3)]
    load = pltpu.make_async_copy(weights, w_out, own.at[0])
    load.start()
    keep_hid = pltpu.make_async_copy(hidden, hid.at[r], own.at[1])
    keep_hid.start()
    greet([up, down] + mates + [(z, tx, r, y) for _, tx in across])
    span = teacher.shape[2]
    wing = span // count
    per = nz // 2
    every = slice(None)
    copies = [{} for _ in range(4 * count + 1)]
    swap_hid = remote(hidden, hid.at[r], hsend, hrecv, sibling)
    swap_hid.start()
    loss[...] = jnp.zeros_like(loss)

    def sems(k):
        return send.at[k], recv.at[k], copies[k]

    def trio(axis_size):
        return (pl.ds(0, axis_size),), (pl.ds(0, axis_size // 2),), (pl.ds(axis_size // 2, axis_size // 2),)

    def lanes(size):
        return tuple((every, pl.ds(o, s)) for o, s in ((0, size), (0, size // 2), (size // 2, size // 2)))

    along_x, along_y = (NX, x, east, west), (ny, y, north, south)
    swaps = []

    def flow(f):
        cut = pl.ds(f * wing, wing)
        parts, gaps, scame, sleave, mid, came2, leave2 = buffers[7 * f:7 * f + 7]
        x_first = f < count // 2
        one, two = (along_x, along_y) if x_first else (along_y, along_x)

        def outer(d, p):
            return (d,) + p if x_first else p + (d,)

        def inner(d, p):
            return (x, d) + p if x_first else (d, y) + p

        @pl.loop(0, NX)
        def _(i):
            rows = pl.ds(pl.multiple_of(i * tok, tok), tok)
            value = jnp.dot(hid[0, rows], w_out[:, cut], preferred_element_type=F32)
            value += jnp.dot(hid[1, rows], w_out[:, pl.ds(span + f * wing, wing)], preferred_element_type=F32)
            parts[i] = value.astype(BF).reshape(parts.shape[1:])

        yield from ring_sum(*one, parts, outer, [trio(two[0])], scame, sleave, *sems(4 * f))
        last = one[0] // 2 - 1
        kept = parts[x] if x_first else parts[:, y]
        mid[...] = (kept.astype(F32) + scame[0, last].astype(F32) + scame[1, last].astype(F32)).astype(BF)
        yield from ring_sum(*two, mid, lambda d, p: (d,) + p, [lanes(wing)], came2, leave2, *sems(4 * f + 1))
        last = two[0] // 2 - 1
        student = mid[two[1]].astype(F32) + came2[0, last].astype(F32) + came2[1, last].astype(F32)
        taught = teacher[z, :, cut].astype(F32) + tcame[0, per - 1, :, cut].astype(F32) + tcame[1, per - 1, :, cut].astype(F32)
        gap = student - taught
        gaps[x, y] = gap.astype(BF)
        square = gap * gap
        loss[...] += sum(square[:, t * 128:(t + 1) * 128] for t in range(wing // 128))
        yield from ring_gather(*two, gaps, inner, *lanes(wing), *sems(4 * f + 2))
        yield from ring_gather(*one, gaps, outer, *trio(two[0]), *sems(4 * f + 3))
        whole = gaps[...].reshape(NX * tok, wing)

        def term(core):
            value = lax.dot_general(hid[core], whole, (((0,), (0,)), ((), ())), preferred_element_type=F32)
            return (value / tok).astype(BF)

        give[f] = term(1 - r)
        slot = r * per + f
        swaps.append(remote(give.at[f], chunks.at[slot], csend.at[f], crecv.at[f], sibling))
        swaps[-1].start()
        chunks[slot] = term(r)

    teach = ring_sum(nz, z, up, down, teacher, lambda d, p: (d,) + p, [lanes(span)], tcame, tleave, *sems(4 * count))
    next(teach)
    load.wait()
    keep_hid.wait()
    swap_hid.wait_recv()
    half = count // 2
    flows = [flow(k) for pair in zip(range(half), range(half, count)) for k in pair]
    for one in flows:
        next(one)
    together(teach, *flows)
    place = r * ny + y
    tells = [remote(loss, losses.at[place], lsend.at[k], lrecv.at[k], device) for k, device in enumerate(mates)]
    keep_loss = pltpu.make_async_copy(loss, losses.at[place], own.at[2])
    for copy in tells + [keep_loss]:
        copy.start()
    for copy in swaps:
        copy.wait_recv()
    rows, span = chunks.shape[1], chunks.shape[2]
    subs = []
    for u in (0, 1):
        band = pl.ds(u * (rows // 2), rows // 2)
        subs.append(((band, pl.ds(0, span)), (band, pl.ds(0, span // 2)), (band, pl.ds(span // 2, span // 2))))
    ring = {}
    together(ring_sum(nz, z, up, down, chunks, lambda d, p: (d,) + p, subs, came, leave, zsend, zrecv, ring))
    value = chunks[z].astype(F32) + came[0, per - 1].astype(F32) + came[1, per - 1].astype(F32)
    total[...] = value.astype(BF)
    size = span // NX
    outs = []
    for d, tx in across:
        outs.append(remote(total.at[:, lanes_at(tx, size)], grad.at[x], xsend.at[d - 1], xrecv.at[d - 1], (z, tx, r, y)))
        outs[-1].start()
    last = pltpu.make_async_copy(total.at[:, lanes_at(x, size)], grad.at[x], own.at[3])
    last.start()
    for copy in [last, keep_loss] + outs + tells:
        copy.wait()
    for copy in swaps + [swap_hid] + list(ring.values()) + [c for group in copies for c in group.values()]:
        copy.wait_send()


def on_device(tokens, routes, route_weights, teacher_in, teacher_out, student_in, student_out):
    nz, nr, ny = lax.axis_size("z"), lax.axis_size("row"), lax.axis_size("col")
    z, x, r, y = here()
    tok, width = tokens.shape
    block, top = routes.shape
    blk = student_in.shape[1]
    ff = student_in.shape[2]
    sub = ff // NX
    half = width // nr
    experts = NX * ny
    cap = max(2, 3 * block * top // (2 * nz * experts))
    blocks = nz * NX
    shape = jax.ShapeDtypeStruct

    parts = jnp.concatenate([jnp.swapaxes(student_in, 1, 2), student_out[None]], axis=0)
    parts = pad_lanes(parts)
    lanes = parts.shape[-1]
    wide = blocks * lanes
    steps = nz // 2
    slots = nz * cap
    hid = teacher_in.shape[3]
    mine = lax.dynamic_slice(tokens, (y * block, r * half), (block, half))
    meta = jnp.concatenate([routes.astype(F32), route_weights], axis=1).T
    meta = jnp.pad(meta, ((0, 0), (0, 128 - block)))
    padded = pad_lanes(tokens.reshape(tok, blocks, blk)).reshape(tok, wide)
    whole, far = pl.BlockSpec(memory_space=pltpu.VMEM), pl.BlockSpec(memory_space=pl.ANY)
    bf, f32 = (lambda *b: pltpu.VMEM(b, BF)), (lambda *b: pltpu.VMEM(b, F32))
    buffers = [bf(2, sub, wide), bf(NX, tok, wide), f32(nz, 2 * top, 128), f32(cap, experts * nz, nz * block), bf(experts, slots, half)]
    buffers += [bf(2, width, hid), bf(hid, width), bf(nz, block, half), bf(experts, slots, half), bf(experts, slots, width)]
    buffers += [bf(experts // 2 * slots, hid), bf(experts, slots, width)] + [bf(experts, slots, half)] * 2
    sems = [(4, 3)] * 2 + [(3, 2, steps, 1)] * 2 + [(2, steps)] * 4 + [(3,)] * 2 + [(2, 3)] * 2 + [(3, 3)] * 2
    sems += [(experts,)] * 4 + [(2,)] * 2 + [(experts,)] * 2 + [(9,)]
    hidden, student_down, teacher = kernel_call(
        functools.partial(front_kernel, nz, cap, blk), 0,
        [shape((NX * tok, sub), BF), shape((sub, wide), BF), shape((nz, block, wide // nr), BF)],
        buffers + [dma(*b) for b in sems],
        parts.reshape(3, NX, sub, lanes), mine, meta, padded, teacher_in[0], teacher_out[0],
        specs=[whole, whole, whole, whole, far, far],
    )

    span = wide // nr
    count = steps
    wing = span // count
    chunk = NX * lanes
    flows = []
    for f in range(count):
        one, two = (NX, ny) if f < count // 2 else (ny, NX)
        flows += [(NX, ny, block, wing)] * 2
        flows += [(2, one // 2, two, block, wing), (2, one // 2 - 1, two, block, wing), (two, block, wing)]
        flows += [(2, two // 2, block, wing), (2, two // 2 - 1, block, wing)]
    buffers = [(nr, NX * tok, sub), (sub, wide), (2, steps, block, span), (2, steps - 1, block, span), (nz, sub, chunk), (steps, sub, chunk)]
    buffers += [(2, steps, sub, chunk), (2, steps - 1, sub, chunk), (sub, chunk)]
    grad, losses = kernel_call(
        functools.partial(tail_kernel, nz, count, tok), 4,
        [shape((NX, sub, lanes), BF), shape((nr * ny, block, 128), F32)],
        [pltpu.VMEM(b, BF) for b in buffers] + [pltpu.VMEM((block, 128), F32)]
        + [dma(4 * count + 1, 2, steps, 1)] * 2 + [dma(2, steps, 2)] * 2 + [dma(steps)] * 2 + [pltpu.SemaphoreType.DMA] * 2 + [dma(3)] * 2
        + [dma(2 * ny - 1)] * 2 + [dma(4)]
        + [pltpu.VMEM(b, BF) for b in flows],
        hidden, student_down, teacher,
        specs=[whole, far, whole],
    )
    token_loss = jnp.sum(losses.reshape(nr, ny * block, 128), axis=(0, 2)) / width
    grad = grad.reshape(ff, lanes)[:, :blk].astype(F32)
    return token_loss, grad


def solution(mesh):
    dp = ("z", "x")
    in_specs = (
        P(dp, None),
        P(dp + ("col",), None),
        P(dp + ("col",), None),
        P(dp + ("col",), None, None, "row"),
        P(dp + ("col",), "row", None),
        P(None, dp, ("row", "col")),
        P(("row", "col"), dp),
    )
    out_specs = (P(dp), P(("row", "col"), dp))
    return jax.shard_map(
        on_device, mesh=split_mesh(mesh), in_specs=in_specs, out_specs=out_specs, check_vma=False
    )
```

time: 229 us -> 215 us (0.939)
  Pallas kernels: 177 us -> 200 us
  matrix products: 18.5 us -> 0 us
  between operations: 14.4 us -> 0.7 us
  blocking collectives: 4.93 us -> 0 us
    pallas_call x5 -> x2, Pallas kernels: 177 us -> 200 us  [kernel_call(): pl.pallas_call(body, out_shape=outs, in_specs=specs or [whole] * len(args...]
    dot_general x7 -> x0, matrix products: 18.5 us -> none  [dot(): return lax.dot_general(a, b, (dims, ((), ())), preferred_element_type=F32)]
    all_gather x1 -> x0, blocking collectives: 4.93 us -> none  [on_device(): hidden_both = lax.all_gather(hidden, 'row', axis=1, tiled=True)]
    reshape x2 -> x0, local copies, waits for them, and re-layouts: 3.13 us -> none  [the longest x1 2.35 us: on_device(): teacher.reshape(nz, block, blocks // nr, blk)]
  transfers between devices with their start and end apart: 1 -> 0, of which waited for: 0 -> 0; matrix products, arithmetic and copies ran while one was open for 5% -> 0% of each run, Pallas kernels for 35% -> 0%
where the time goes in v5:
time: 215 us
  Pallas kernels  200 us (93%)
  local copies, waits for them, and re-layouts  9.19 us (4%)
  other arithmetic  5.08 us (2%)
    pallas_call x2, Pallas kernels, kernel_call(): pl.pallas_call(body, out_shape=outs, in_specs=specs or [whole] * len(args...  200 us

profile of v5, /device:TPU:1, one launch (start us, length us, event | category | flops | bytes accessed | tf_op | source)
XLA Modules:
  0.0 214.5 jit_solution(15382308622308485437)
XLA Ops:
  0.6 0.7 convert_element_type.12
  1.3 0.7 maximum_bitcast_fusion
  2.0 0.6 pad.13.meta
  2.6 1.6 dynamic_slice.3.mine
  4.2 1.3 pad_maximum_fusion
  5.5 0.0 copy-start
  5.5 0.9 copy.14
  6.4 1.1 pad.12.clone
  7.5 0.0 copy-done
  7.5 1.8 reshape.19
  9.4 0.3 pad.14
  9.6 1.6 copy.17
  11.3 111.2 %shard_map.86 = (bf16[640,288]{1,0:T(8,128)(2,1)}, bf16[288,4096]{1,0:T(8,128)(2,1)}, bf16[8,40,2048]{2,1,0:T(8,128)(2,1)}) custom-call(bf16[3,4,288,128]{3,2,1,0:T(8,128)(2,1)} %bitcast.17, bf16[40,1792]{1,0:T(8,128)(2,1)} %dynamic_slice.3.mine, f32[16,128]{1,0:T(8,128)} %pad.13.meta, bf16[160,4096]{1,0:T(8,128)(2,1)} %bitcast.14, ...), custom_call_target="tpu_custom_call" | custom-call | tf_op jit(solution)/shard_map/pallas_call | solution.py:54
  122.5 88.3 %shard_map.87 = (bf16[4,288,128]{2,1,0:T(8,128)(2,1)}, f32[8,40,128]{2,1,0:T(8,128)}) custom-call(bf16[640,288]{1,0:T(8,128)(2,1)} %get-tuple-element.7.hidden, bf16[288,4096]{1,0:T(8,128)(2,1)} %get-tuple-element.8.weights, bf16[8,40,2048]{2,1,0:T(8,128)(2,1)} %get-tuple-element.9.teacher), custom_call_target="tpu_custom_call" | custom-call | tf_op jit(solution)/shard_map/pallas_call | solution.py:54
  210.9 1.0 reduce_sum.10
  211.9 0.1 reduce_sum.14
  212.0 0.6 broadcast_multiply_fusion
  212.6 1.1 copy.13
  213.7 0.8 convert_element_type.13
  (1 shorter events, 0.0 us)
Async XLA Ops:
  5.5 2.1 copy-start

commit v6 on v5

--- a/solution.py
+++ b/solution.py
@@ -73,12 +73,12 @@
     return sorted(steps, key=far, reverse=True)
 
 
-def token_gather(padded, plane, xs, xr, ys, yr, cs, cr, own, started):
+def token_gather(tokens, blk, plane, xs, xr, ys, yr, cs, cr, started):
     z, x, r, y = here()
     ny = lax.axis_size("col")
     north, south = (y + 1) % ny, (y + ny - 1) % ny
     sibling = (z, x, 1 - r, y)
-    rows, wide = padded.shape
+    rows, wide = plane.shape[1], plane.shape[2]
     high, span = rows // 2, wide // 2
     quarter = span // 2
     mine_rows = pl.ds(pl.multiple_of(r * high, high), high)
@@ -92,7 +92,8 @@
 
     def x_step(d):
         device = (z, (x + d) % NX, r, y)
-        return go(remote(padded.at[mine_rows, held], plane.at[x, mine_rows, held], xs.at[d - 1], xr.at[d - 1], device))
+        piece = plane.at[x, mine_rows, held]
+        return go(remote(piece, piece, xs.at[d - 1], xr.at[d - 1], device))
 
     from_sib, from_y = [], []
 
@@ -113,9 +114,19 @@
             piece = plane.at[source, mine_rows, lanes_at((1 - parity) * 2 + side, quarter)]
             from_sib.append(go(remote(piece, piece, cs.at[1 + side, d - 1], cr.at[1 + side, d - 1], sibling)))
 
+    band = 32
+    lanes = -(-blk // 128) * 128
+
+    @pl.loop(0, rows // band)
+    def _(i):
+        cut = pl.ds(pl.multiple_of(i * band, band), band)
+        value = tokens[cut].astype(F32)
+        empty = jnp.zeros((band, lanes - blk), F32)
+        for b in range(wide // lanes):
+            piece = jnp.concatenate([value[:, b * blk:(b + 1) * blk], empty], axis=1)
+            plane[x, cut, b * lanes:(b + 1) * lanes] = piece.astype(BF)
+
     first, third = x_step(1), x_step(3)
-    local = pltpu.make_async_copy(padded, plane.at[x], own)
-    local.start()
     yield
     onward(1, first)
     onward(3, third)
@@ -127,7 +138,6 @@
     inward()
     for copy in from_sib:
         copy.wait_recv()
-    local.wait()
 
 
 def block_gather(nz, mine, meta, column, metas, zs, zr, ms, mr, own, started):
@@ -214,68 +224,45 @@
         teacher[:, :, b * lanes:(b + 1) * lanes] = piece.reshape(nz, count // nz, lanes)
 
 
-def front_kernel(nz, cap, blk, parts, mine, meta, padded, inner, outer, hidden, student_down, teacher,
-                 student, plane, metas, weighted, back, w_in, w_out, column, outgoing, got, act, part, other, total,
-                 ws, wr, rs, rr, zs, zr, ms, mr, xs, xr, ys, yr, cs, cr, send, recv, fsend, frecv, csend, crecv, bsend, brecv, own):
+def front_kernel(nz, cap, blk, parts, meta, own_tokens, inner, outer, hidden, down_both, teacher,
+                 student, student_down, mine, plane, metas, weighted, back, w_in, w_out, column, outgoing, got, act, part, other, total,
+                 ws, wr, rs, rr, zs, zr, ms, mr, xs, xr, ys, yr, cs, cr, send, recv, fsend, frecv, csend, crecv, bsend, brecv, dsend, drecv, own):
     z, x, r, y = here()
     ny = lax.axis_size("col")
     steps = plane_steps(ny)[::-1]
     sibling = (z, x, 1 - r, y)
     up, down_z = ((z + 1) % nz, x, r, y), ((z + nz - 1) % nz, x, r, y)
     per = nz // 2
-    core = z // per
-    plane_z = per * r + z % per
-    moves = core != r
     loads = [pltpu.make_async_copy(inner, w_in, own.at[1]), pltpu.make_async_copy(outer, w_out, own.at[2])]
     for copy in loads:
         copy.start()
     peers = [(z, (x + dx) % NX, r, (y + dy) % ny) for dx, dy in steps]
-    peers += [sibling, up, down_z] + [(plane_z, (x + d) % NX, core, y) for d in (1, 2, 3)]
-
-    @pl.when(moves)
-    def _():
-        greet(peers + [(plane_z, x, core, y)])
-
-    @pl.when(jnp.logical_not(moves))
-    def _():
-        greet(peers)
-
+    greet(peers + [sibling, up, down_z])
     started = []
+    block, half = mine.shape
+    mine[...] = own_tokens[pl.ds(pl.multiple_of(y * block, 8), block), lanes_at(r, half)]
     blocks = block_gather(nz, mine, meta, column, metas, zs, zr, ms, mr, own.at[pl.ds(3, 2)], started)
-    tokens = token_gather(padded, plane, xs, xr, ys, yr, cs, cr, own.at[5], started)
+    tokens = token_gather(own_tokens, blk, plane, xs, xr, ys, yr, cs, cr, started)
     next(blocks)
 
     span = NX * 128
     exchange = [[], [], []]
     homes = [student.at[0], student.at[1], student_down]
-    lane = pl.ds(pl.multiple_of(z * span + x * 128, 128), 128)
-    lane_down = pl.ds(pl.multiple_of(plane_z * span + x * 128, 128), 128)
+    lane = lanes_at(x, 128)
     for kind in (0, 1, 2):
         for d in (2, 1, 3):
             to = (x + d) % NX
-            device, cut = ((plane_z, to, core, y), lane_down) if kind == 2 else ((z, to, r, y), lane)
-            copy = remote(parts.at[kind, to], homes[kind].at[:, cut], ws.at[d, kind], wr.at[d, kind], device)
+            copy = remote(parts.at[kind, to], homes[kind].at[z, :, lane], ws.at[d - 1, kind], wr.at[d - 1, kind], (z, to, r, y))
             copy.start()
             started.append(copy)
             exchange[kind].append(copy)
-    down_own = remote(parts.at[2, x], student_down.at[:, lane_down], ws.at[0, 2], wr.at[0, 2], (plane_z, x, core, y))
-    down_here = pltpu.make_async_copy(parts.at[2, x], student_down.at[:, lane], own.at[6])
-
-    @pl.when(moves)
-    def _():
-        down_own.start()
-
-    @pl.when(jnp.logical_not(moves))
-    def _():
-        down_here.start()
-
-    local = [pltpu.make_async_copy(parts.at[k, x], student.at[k, :, lane], own.at[7 + k]) for k in (0, 1)]
+    local = [pltpu.make_async_copy(parts.at[k, x], homes[k].at[z, :, lane], own.at[5 + k]) for k in range(3)]
     for copy in local:
         copy.start()
     next(tokens)
 
     def chunk(d, p):
-        return (slice(None), pl.ds(pl.multiple_of(d * span + p[0], 128), p[1]))
+        return (d, slice(None), pl.ds(*p))
 
     rings = [{}, {}, {}]
     gathers = [
@@ -288,32 +275,22 @@
         for kind in kinds:
             next(gathers[kind], None)
 
-    for _ in range(per - 1):
+    for _ in range(per - 2):
         next(blocks)
-    for copy in local:
-        copy.wait()
-    for kind in (0, 1):
+    for kind in range(3):
+        local[kind].wait()
         for copy in exchange[kind]:
             copy.wait_recv()
-        next(gathers[kind])
-    for copy in exchange[2]:
-        copy.wait_recv()
-
-    @pl.when(moves)
-    def _():
-        down_own.wait()
-
-    @pl.when(jnp.logical_not(moves))
-    def _():
-        down_here.wait()
-
+        if kind < 2:
+            serve(kind)
+        if kind == 0:
+            next(blocks)
     next(tokens)
     next(blocks, None)
 
     place_rows(nz, cap, column, metas, outgoing, weighted)
     steps = [(0, 0)] + steps
     me = x * ny + y
-    half = outgoing.shape[2]
     keep, give = lanes_at(r, half), lanes_at(1 - r, half)
     near = len(steps) // 2
     groups = (range(near), range(near, len(steps)))
@@ -384,25 +361,42 @@
         swaps[g].start()
         down(r)
         if g == 0:
+            serve(0, 1, 2)
+        finish(g)
+        if g == 1:
             serve(0, 1)
-        finish(g)
         next(tokens, None)
-        if g == 1:
-            serve(0, 1, 2)
-
-    serve(0, 1)
+
+    serve(0, 1, 2)
     tok = plane.shape[1]
+
+    def units(kind, i):
+        total = jnp.zeros((2 * tok, student.shape[2]), F32)
+        for d in range(nz):
+            rows = plane[2 * i:2 * i + 2, :, d * span:(d + 1) * span].reshape(2 * tok, span)
+            total += lax.dot_general(rows, student[kind, d], (((1,), (1,)), ((), ())), preferred_element_type=F32)
+        return total
+
     for i in range(NX // 2):
-        rows = plane[2 * i:2 * i + 2].reshape(2 * tok, plane.shape[2])
-        gate = lax.dot_general(rows, student[0], (((1,), (1,)), ((), ())), preferred_element_type=F32)
-        up_part = lax.dot_general(rows, student[1], (((1,), (1,)), ((), ())), preferred_element_type=F32)
-        hidden[2 * i * tok:2 * (i + 1) * tok] = (gate / (1.0 + jnp.exp(-gate)) * up_part).astype(BF)
+        gate = units(0, i)
+        hidden[2 * i * tok:2 * (i + 1) * tok] = (gate / (1.0 + jnp.exp(-gate)) * units(1, i)).astype(BF)
         serve(2)
     for copy in returns:
         copy.wait_recv()
-    weigh_rows(nz, cap, weighted, back, teacher, blk)
-    serve(2)
-    serve(2)
+    changes = []
+    for i in (1, 2, 3, 0):
+        if i == 0:
+            weigh_rows(nz, cap, weighted, back, teacher, blk)
+            serve(2)
+        q = (z + i) % per
+        src = student_down.at[(1 - r) * per + q]
+        changes.append(remote(src, down_both.at[r, q], dsend.at[i], drecv.at[i], sibling))
+        changes[-1].start()
+    local = [pltpu.make_async_copy(student_down.at[r * per + q], down_both.at[r, q], own.at[5 + q]) for q in range(per)]
+    for copy in local:
+        copy.start()
+    for copy in local + changes:
+        copy.wait()
     for copy in started + returns + list(sends.values()) + list(forwards.values()) + list(swaps.values()):
         copy.wait_send()
     for ring in rings:
@@ -517,8 +511,8 @@
         @pl.loop(0, NX)
         def _(i):
             rows = pl.ds(pl.multiple_of(i * tok, tok), tok)
-            value = jnp.dot(hid[0, rows], w_out[:, cut], preferred_element_type=F32)
-            value += jnp.dot(hid[1, rows], w_out[:, pl.ds(span + f * wing, wing)], preferred_element_type=F32)
+            value = jnp.dot(hid[0, rows], w_out[0, f], preferred_element_type=F32)
+            value += jnp.dot(hid[1, rows], w_out[1, f], preferred_element_type=F32)
             parts[i] = value.astype(BF).reshape(parts.shape[1:])
 
         yield from ring_sum(*one, parts, outer, [trio(two[0])], scame, sleave, *sems(4 * f))
@@ -607,23 +601,21 @@
     steps = nz // 2
     slots = nz * cap
     hid = teacher_in.shape[3]
-    mine = lax.dynamic_slice(tokens, (y * block, r * half), (block, half))
     meta = jnp.concatenate([routes.astype(F32), route_weights], axis=1).T
     meta = jnp.pad(meta, ((0, 0), (0, 128 - block)))
-    padded = pad_lanes(tokens.reshape(tok, blocks, blk)).reshape(tok, wide)
     whole, far = pl.BlockSpec(memory_space=pltpu.VMEM), pl.BlockSpec(memory_space=pl.ANY)
     bf, f32 = (lambda *b: pltpu.VMEM(b, BF)), (lambda *b: pltpu.VMEM(b, F32))
-    buffers = [bf(2, sub, wide), bf(NX, tok, wide), f32(nz, 2 * top, 128), f32(cap, experts * nz, nz * block), bf(experts, slots, half)]
+    buffers = [bf(2, nz, sub, NX * lanes), bf(nz, sub, NX * lanes), bf(block, half), bf(NX, tok, wide), f32(nz, 2 * top, 128), f32(cap, experts * nz, nz * block), bf(experts, slots, half)]
     buffers += [bf(2, width, hid), bf(hid, width), bf(nz, block, half), bf(experts, slots, half), bf(experts, slots, width)]
     buffers += [bf(experts // 2 * slots, hid), bf(experts, slots, width)] + [bf(experts, slots, half)] * 2
-    sems = [(4, 3)] * 2 + [(3, 2, steps, 1)] * 2 + [(2, steps)] * 4 + [(3,)] * 2 + [(2, 3)] * 2 + [(3, 3)] * 2
-    sems += [(experts,)] * 4 + [(2,)] * 2 + [(experts,)] * 2 + [(9,)]
+    sems = [(3, 3)] * 2 + [(3, 2, steps, 1)] * 2 + [(2, steps)] * 4 + [(3,)] * 2 + [(2, 3)] * 2 + [(3, 3)] * 2
+    sems += [(experts,)] * 4 + [(2,)] * 2 + [(experts,)] * 2 + [(steps,)] * 2 + [(9,)]
     hidden, student_down, teacher = kernel_call(
         functools.partial(front_kernel, nz, cap, blk), 0,
-        [shape((NX * tok, sub), BF), shape((sub, wide), BF), shape((nz, block, wide // nr), BF)],
+        [shape((NX * tok, sub), BF), shape((nr, steps, sub, NX * lanes), BF), shape((nz, block, wide // nr), BF)],
         buffers + [dma(*b) for b in sems],
-        parts.reshape(3, NX, sub, lanes), mine, meta, padded, teacher_in[0], teacher_out[0],
-        specs=[whole, whole, whole, whole, far, far],
+        parts.reshape(3, NX, sub, lanes), meta, tokens, teacher_in[0], teacher_out[0],
+        specs=[whole, whole, whole, far, far],
     )
 
     span = wide // nr
@@ -636,7 +628,7 @@
         flows += [(NX, ny, block, wing)] * 2
         flows += [(2, one // 2, two, block, wing), (2, one // 2 - 1, two, block, wing), (two, block, wing)]
         flows += [(2, two // 2, block, wing), (2, two // 2 - 1, block, wing)]
-    buffers = [(nr, NX * tok, sub), (sub, wide), (2, steps, block, span), (2, steps - 1, block, span), (nz, sub, chunk), (steps, sub, chunk)]
+    buffers = [(nr, NX * tok, sub), (nr, steps, sub, chunk), (2, steps, block, span), (2, steps - 1, block, span), (nz, sub, chunk), (steps, sub, chunk)]
     buffers += [(2, steps, sub, chunk), (2, steps - 1, sub, chunk), (sub, chunk)]
     grad, losses = kernel_call(
         functools.partial(tail_kernel, nz, count, tok), 4,

time: 215 us -> 202 us (0.940)
  Pallas kernels: 200 us -> 193 us
  local copies, waits for them, and re-layouts: 9.19 us -> 3.84 us
    pallas_call x2, Pallas kernels: 200 us -> 193 us  [kernel_call(): pl.pallas_call(body, out_shape=outs, in_specs=specs or [whole] * len(args...]
where the time goes in v6:
time: 202 us
  Pallas kernels  193 us (96%)
  other arithmetic  5.08 us (3%)
  local copies, waits for them, and re-layouts  3.84 us (2%)
    pallas_call x2, Pallas kernels, kernel_call(): pl.pallas_call(body, out_shape=outs, in_specs=specs or [whole] * len(args...  193 us

profile of v6, /device:TPU:1, one launch (start us, length us, event | category | flops | bytes accessed | tf_op | source)
XLA Modules:
  0.0 202.1 jit_solution(3599729936430332509)
XLA Ops:
  0.6 0.7 convert_element_type.10
  1.3 0.7 maximum_bitcast_fusion
  2.0 0.6 pad.9.meta
  2.6 1.3 pad_maximum_fusion
  3.9 0.9 copy.14
  4.8 1.1 pad.8.clone
  5.9 106.4 %shard_map.86 = (bf16[640,288]{1,0:T(8,128)(2,1)}, bf16[2,4,288,512]{3,2,1,0:T(8,128)(2,1)}, bf16[8,40,2048]{2,1,0:T(8,128)(2,1)}) custom-call(bf16[3,4,288,128]{3,2,1,0:T(8,128)(2,1)} %bitcast.11, f32[16,128]{1,0:T(8,128)} %pad.9.meta, bf16[160,3584]{1,0:T(8,128)(2,1)} %own_tokens.1, bf16[2,3584,512]{2,1,0:T(8,128)(2,1)} %bitcast.9, bf16[512,3584]{1,0:T(8,128)(2,1)} %bitcast.10), custom_call_target="tpu_custom_call" | custom-call | tf_op jit(solution)/shard_map/pallas_call | solution.py:54
  112.3 86.1 %shard_map.87 = (bf16[4,288,128]{2,1,0:T(8,128)(2,1)}, f32[8,40,128]{2,1,0:T(8,128)}) custom-call(bf16[640,288]{1,0:T(8,128)(2,1)} %get-tuple-element.7.hidden, bf16[2,4,288,512]{3,2,1,0:T(8,128)(2,1)} %get-tuple-element.8.weights, bf16[8,40,2048]{2,1,0:T(8,128)(2,1)} %get-tuple-element.9.teacher), custom_call_target="tpu_custom_call" | custom-call | tf_op jit(solution)/shard_map/pallas_call | solution.py:54
  198.4 1.0 reduce_sum.10
  199.5 0.1 reduce_sum.14
  199.6 0.6 broadcast_multiply_fusion
  200.1 1.1 copy.13
  201.3 0.8 convert_element_type.11
  (1 shorter events, 0.0 us)

commit v7 on v6

--- a/solution.py
+++ b/solution.py
@@ -265,8 +265,30 @@
         return (d, slice(None), pl.ds(*p))
 
     rings = [{}, {}, {}]
+    idle = 128 - blk
+    riders = 2 * NX - 1
+    packed = riders * idle == blk
+    last = slice(span - 128, span)
+
+    def spot(d, i):
+        return i // NX, d, slice(None), slice(i % NX * 128, (i % NX + 1) * 128)
+
+    def pack():
+        value = student[1, z, :, last].astype(F32)
+        for i in range(riders):
+            kept = student[spot(z, i)].astype(F32)[:, :blk]
+            student[spot(z, i)] = jnp.concatenate([kept, value[:, i * idle:(i + 1) * idle]], axis=1).astype(BF)
+
+    def unpack():
+        @pl.loop(0, nz)
+        def _(d):
+            pieces = [student[spot(d, i)].astype(F32)[:, blk:] for i in range(riders)]
+            empty = jnp.zeros((student.shape[2], idle), F32)
+            student[1, d, :, last] = jnp.concatenate(pieces + [empty], axis=1).astype(BF)
+
+    sizes = [span, span - 128 if packed else span, span]
     gathers = [
-        ring_gather(nz, z, up, down_z, homes[kind], chunk, (0, span), (0, span // 2), (span // 2, span // 2),
+        ring_gather(nz, z, up, down_z, homes[kind], chunk, (0, sizes[kind]), (0, span // 2), (span // 2, sizes[kind] - span // 2),
                     rs.at[kind], rr.at[kind], rings[kind])
         for kind in range(3)
     ]
@@ -281,8 +303,10 @@
         local[kind].wait()
         for copy in exchange[kind]:
             copy.wait_recv()
-        if kind < 2:
-            serve(kind)
+        if kind == 1:
+            if packed:
+                pack()
+            serve(0, 1)
         if kind == 0:
             next(blocks)
     next(tokens)
@@ -364,10 +388,12 @@
             serve(0, 1, 2)
         finish(g)
         if g == 1:
-            serve(0, 1)
+            serve(0, 1, 2)
         next(tokens, None)
 
     serve(0, 1, 2)
+    if packed:
+        unpack()
     tok = plane.shape[1]
 
     def units(kind, i):
@@ -380,7 +406,8 @@
     for i in range(NX // 2):
         gate = units(0, i)
         hidden[2 * i * tok:2 * (i + 1) * tok] = (gate / (1.0 + jnp.exp(-gate)) * units(1, i)).astype(BF)
-        serve(2)
+        if i == 0:
+            serve(2)
     for copy in returns:
         copy.wait_recv()
     changes = []
@@ -404,7 +431,7 @@
             copy.wait_send()
 
 
-def ring_sum(n, i, up, down, ref, where, subs, came, leave, send, recv, copies):
+def ring_sum(n, i, up, down, ref, where, subs, came, leave, send, recv, copies, done=None):
     half = n // 2
 
     def go(way, s, u, src, dst):
@@ -432,6 +459,8 @@
     for u in range(len(subs)):
         for way in (0, 1):
             copies[way, half - 1, u].wait_recv()
+        if done:
+            done(u)
 
 
 def ring_gather(n, i, up, down, ref, where, whole, low, top, send, recv, copies):
@@ -564,17 +593,23 @@
         band = pl.ds(u * (rows // 2), rows // 2)
         subs.append(((band, pl.ds(0, span)), (band, pl.ds(0, span // 2)), (band, pl.ds(span // 2, span // 2))))
     ring = {}
-    together(ring_sum(nz, z, up, down, chunks, lambda d, p: (d,) + p, subs, came, leave, zsend, zrecv, ring))
-    value = chunks[z].astype(F32) + came[0, per - 1].astype(F32) + came[1, per - 1].astype(F32)
-    total[...] = value.astype(BF)
     size = span // NX
     outs = []
-    for d, tx in across:
-        outs.append(remote(total.at[:, lanes_at(tx, size)], grad.at[x], xsend.at[d - 1], xrecv.at[d - 1], (z, tx, r, y)))
-        outs[-1].start()
-    last = pltpu.make_async_copy(total.at[:, lanes_at(x, size)], grad.at[x], own.at[3])
-    last.start()
-    for copy in [last, keep_loss] + outs + tells:
+
+    def spread(u):
+        band = subs[u][0][0]
+        value = chunks[z, band].astype(F32) + came[0, per - 1, band].astype(F32) + came[1, per - 1, band].astype(F32)
+        total[band] = value.astype(BF)
+        for d, tx in across:
+            copy = remote(total.at[band, lanes_at(tx, size)], grad.at[x, band], xsend.at[d - 1, u], xrecv.at[d - 1, u], (z, tx, r, y))
+            copy.start()
+            outs.append(copy)
+        copy = pltpu.make_async_copy(total.at[band, lanes_at(x, size)], grad.at[x, band], own.at[3 + u])
+        copy.start()
+        outs.append(copy)
+
+    together(ring_sum(nz, z, up, down, chunks, lambda d, p: (d,) + p, subs, came, leave, zsend, zrecv, ring, spread))
+    for copy in [keep_loss] + outs + tells:
         copy.wait()
     for copy in swaps + [swap_hid] + list(ring.values()) + [c for group in copies for c in group.values()]:
         copy.wait_send()
@@ -634,8 +669,8 @@
         functools.partial(tail_kernel, nz, count, tok), 4,
         [shape((NX, sub, lanes), BF), shape((nr * ny, block, 128), F32)],
         [pltpu.VMEM(b, BF) for b in buffers] + [pltpu.VMEM((block, 128), F32)]
-        + [dma(4 * count + 1, 2, steps, 1)] * 2 + [dma(2, steps, 2)] * 2 + [dma(steps)] * 2 + [pltpu.SemaphoreType.DMA] * 2 + [dma(3)] * 2
-        + [dma(2 * ny - 1)] * 2 + [dma(4)]
+        + [dma(4 * count + 1, 2, steps, 1)] * 2 + [dma(2, steps, 2)] * 2 + [dma(steps)] * 2 + [pltpu.SemaphoreType.DMA] * 2 + [dma(3, 2)] * 2
+        + [dma(2 * ny - 1)] * 2 + [dma(5)]
         + [pltpu.VMEM(b, BF) for b in flows],
         hidden, student_down, teacher,
         specs=[whole, far, whole],

time: 202 us -> 198 us (0.980)
  Pallas kernels: 193 us -> 188 us
    pallas_call x2, Pallas kernels: 193 us -> 188 us  [kernel_call(): pl.pallas_call(body, out_shape=outs, in_specs=specs or [whole] * len(args...]
where the time goes in v7:
time: 198 us
  Pallas kernels  188 us (95%)
  other arithmetic  5.08 us (3%)
  local copies, waits for them, and re-layouts  3.84 us (2%)
    pallas_call x2, Pallas kernels, kernel_call(): pl.pallas_call(body, out_shape=outs, in_specs=specs or [whole] * len(args...  188 us

profile of v7, /device:TPU:1, one launch (start us, length us, event | category | flops | bytes accessed | tf_op | source)
XLA Modules:
  0.0 198.0 jit_solution(17302793565512366011)
XLA Ops:
  0.6 0.7 convert_element_type.10
  1.3 0.7 maximum_bitcast_fusion
  2.0 0.6 pad.9.meta
  2.6 1.3 pad_maximum_fusion
  3.9 0.9 copy.14
  4.8 1.1 pad.8.clone
  5.9 102.8 %shard_map.86 = (bf16[640,288]{1,0:T(8,128)(2,1)}, bf16[2,4,288,512]{3,2,1,0:T(8,128)(2,1)}, bf16[8,40,2048]{2,1,0:T(8,128)(2,1)}) custom-call(bf16[3,4,288,128]{3,2,1,0:T(8,128)(2,1)} %bitcast.11, f32[16,128]{1,0:T(8,128)} %pad.9.meta, bf16[160,3584]{1,0:T(8,128)(2,1)} %own_tokens.1, bf16[2,3584,512]{2,1,0:T(8,128)(2,1)} %bitcast.9, bf16[512,3584]{1,0:T(8,128)(2,1)} %bitcast.10), custom_call_target="tpu_custom_call" | custom-call | tf_op jit(solution)/shard_map/pallas_call | solution.py:54
  108.7 85.6 %shard_map.87 = (bf16[4,288,128]{2,1,0:T(8,128)(2,1)}, f32[8,40,128]{2,1,0:T(8,128)}) custom-call(bf16[640,288]{1,0:T(8,128)(2,1)} %get-tuple-element.7.hidden, bf16[2,4,288,512]{3,2,1,0:T(8,128)(2,1)} %get-tuple-element.8.weights, bf16[8,40,2048]{2,1,0:T(8,128)(2,1)} %get-tuple-element.9.teacher), custom_call_target="tpu_custom_call" | custom-call | tf_op jit(solution)/shard_map/pallas_call | solution.py:54
  194.3 1.0 reduce_sum.10
  195.3 0.1 reduce_sum.14
  195.4 0.6 broadcast_multiply_fusion
  196.0 1.1 copy.13
  197.2 0.8 convert_element_type.11
  (1 shorter events, 0.0 us)

commit v8 on v7

--- a/solution.py
+++ b/solution.py
@@ -405,12 +405,13 @@
 
     for i in range(NX // 2):
         gate = units(0, i)
-        hidden[2 * i * tok:2 * (i + 1) * tok] = (gate / (1.0 + jnp.exp(-gate)) * units(1, i)).astype(BF)
+        hidden[r, 2 * i * tok:2 * (i + 1) * tok] = (gate / (1.0 + jnp.exp(-gate)) * units(1, i)).astype(BF)
         if i == 0:
             serve(2)
     for copy in returns:
         copy.wait_recv()
-    changes = []
+    changes = [remote(hidden.at[r], hidden.at[r], dsend.at[per], drecv.at[per], sibling)]
+    changes[0].start()
     for i in (1, 2, 3, 0):
         if i == 0:
             weigh_rows(nz, cap, weighted, back, teacher, blk)
@@ -489,8 +490,8 @@
                 rings.remove(ring)
 
 
-def tail_kernel(nz, count, tok, hidden, weights, teacher, grad, losses, hid, w_out, tcame, tleave, chunks, give, came, leave, total, loss,
-                send, recv, zsend, zrecv, csend, crecv, hsend, hrecv, xsend, xrecv, lsend, lrecv, own, *buffers):
+def tail_kernel(nz, count, tok, hid, weights, teacher, grad, losses, w_out, tcame, tleave, chunks, give, came, leave, total, loss,
+                send, recv, zsend, zrecv, csend, crecv, xsend, xrecv, lsend, lrecv, own, *buffers):
     z, x, r, y = here()
     ny = lax.axis_size("col")
     up, down = ((z + 1) % nz, x, r, y), ((z + nz - 1) % nz, x, r, y)
@@ -501,16 +502,12 @@
     across = [(d, (x + d) % NX) for d in (2, 1, 3)]
     load = pltpu.make_async_copy(weights, w_out, own.at[0])
     load.start()
-    keep_hid = pltpu.make_async_copy(hidden, hid.at[r], own.at[1])
-    keep_hid.start()
     greet([up, down] + mates + [(z, tx, r, y) for _, tx in across])
     span = teacher.shape[2]
     wing = span // count
     per = nz // 2
     every = slice(None)
     copies = [{} for _ in range(4 * count + 1)]
-    swap_hid = remote(hidden, hid.at[r], hsend, hrecv, sibling)
-    swap_hid.start()
     loss[...] = jnp.zeros_like(loss)
 
     def sems(k):
@@ -573,8 +570,6 @@
     teach = ring_sum(nz, z, up, down, teacher, lambda d, p: (d,) + p, [lanes(span)], tcame, tleave, *sems(4 * count))
     next(teach)
     load.wait()
-    keep_hid.wait()
-    swap_hid.wait_recv()
     half = count // 2
     flows = [flow(k) for pair in zip(range(half), range(half, count)) for k in pair]
     for one in flows:
@@ -589,8 +584,8 @@
         copy.wait_recv()
     rows, span = chunks.shape[1], chunks.shape[2]
     subs = []
-    for u in (0, 1):
-        band = pl.ds(u * (rows // 2), rows // 2)
+    for u in range(3):
+        band = pl.ds(u * (rows // 3), rows // 3)
         subs.append(((band, pl.ds(0, span)), (band, pl.ds(0, span // 2)), (band, pl.ds(span // 2, span // 2))))
     ring = {}
     size = span // NX
@@ -611,7 +606,7 @@
     together(ring_sum(nz, z, up, down, chunks, lambda d, p: (d,) + p, subs, came, leave, zsend, zrecv, ring, spread))
     for copy in [keep_loss] + outs + tells:
         copy.wait()
-    for copy in swaps + [swap_hid] + list(ring.values()) + [c for group in copies for c in group.values()]:
+    for copy in swaps + list(ring.values()) + [c for group in copies for c in group.values()]:
         copy.wait_send()
 
 
@@ -644,10 +639,10 @@
     buffers += [bf(2, width, hid), bf(hid, width), bf(nz, block, half), bf(experts, slots, half), bf(experts, slots, width)]
     buffers += [bf(experts // 2 * slots, hid), bf(experts, slots, width)] + [bf(experts, slots, half)] * 2
     sems = [(3, 3)] * 2 + [(3, 2, steps, 1)] * 2 + [(2, steps)] * 4 + [(3,)] * 2 + [(2, 3)] * 2 + [(3, 3)] * 2
-    sems += [(experts,)] * 4 + [(2,)] * 2 + [(experts,)] * 2 + [(steps,)] * 2 + [(9,)]
+    sems += [(experts,)] * 4 + [(2,)] * 2 + [(experts,)] * 2 + [(steps + 1,)] * 2 + [(9,)]
     hidden, student_down, teacher = kernel_call(
         functools.partial(front_kernel, nz, cap, blk), 0,
-        [shape((NX * tok, sub), BF), shape((nr, steps, sub, NX * lanes), BF), shape((nz, block, wide // nr), BF)],
+        [shape((nr, NX * tok, sub), BF), shape((nr, steps, sub, NX * lanes), BF), shape((nz, block, wide // nr), BF)],
         buffers + [dma(*b) for b in sems],
         parts.reshape(3, NX, sub, lanes), meta, tokens, teacher_in[0], teacher_out[0],
         specs=[whole, whole, whole, far, far],
@@ -663,14 +658,14 @@
         flows += [(NX, ny, block, wing)] * 2
         flows += [(2, one // 2, two, block, wing), (2, one // 2 - 1, two, block, wing), (two, block, wing)]
         flows += [(2, two // 2, block, wing), (2, two // 2 - 1, block, wing)]
-    buffers = [(nr, NX * tok, sub), (nr, steps, sub, chunk), (2, steps, block, span), (2, steps - 1, block, span), (nz, sub, chunk), (steps, sub, chunk)]
+    buffers = [(nr, steps, sub, chunk), (2, steps, block, span), (2, steps - 1, block, span), (nz, sub, chunk), (steps, sub, chunk)]
     buffers += [(2, steps, sub, chunk), (2, steps - 1, sub, chunk), (sub, chunk)]
     grad, losses = kernel_call(
         functools.partial(tail_kernel, nz, count, tok), 4,
         [shape((NX, sub, lanes), BF), shape((nr * ny, block, 128), F32)],
         [pltpu.VMEM(b, BF) for b in buffers] + [pltpu.VMEM((block, 128), F32)]
-        + [dma(4 * count + 1, 2, steps, 1)] * 2 + [dma(2, steps, 2)] * 2 + [dma(steps)] * 2 + [pltpu.SemaphoreType.DMA] * 2 + [dma(3, 2)] * 2
-        + [dma(2 * ny - 1)] * 2 + [dma(5)]
+        + [dma(4 * count + 1, 2, steps, 1)] * 2 + [dma(2, steps, 3)] * 2 + [dma(steps)] * 2 + [dma(3, 3)] * 2
+        + [dma(2 * ny - 1)] * 2 + [dma(6)]
         + [pltpu.VMEM(b, BF) for b in flows],
         hidden, student_down, teacher,
         specs=[whole, far, whole],

time: 198 us -> 195 us (0.985)
  Pallas kernels: 188 us -> 185 us
    pallas_call x2, Pallas kernels: 188 us -> 185 us  [kernel_call(): pl.pallas_call(body, out_shape=outs, in_specs=specs or [whole] * len(args...]
where the time goes in v8:
time: 195 us; the launch traced here: 194 us
  Pallas kernels  185 us (95%)
  other arithmetic  5.08 us (3%)
  local copies, waits for them, and re-layouts  3.86 us (2%)
    pallas_call x2, Pallas kernels, kernel_call(): pl.pallas_call(body, out_shape=outs, in_specs=specs or [whole] * len(args...  185 us

profile of v8, /device:TPU:1, one launch (start us, length us, event | category | flops | bytes accessed | tf_op | source)
XLA Modules:
  0.0 194.4 jit_solution(6096345592535539574)
XLA Ops:
  0.6 0.7 convert_element_type.10
  1.3 0.7 maximum_bitcast_fusion
  2.0 0.6 pad.9.meta
  2.6 1.3 pad_maximum_fusion
  3.9 0.9 copy.14
  4.8 1.1 pad.8.clone
  5.9 103.0 %shard_map.86 = (bf16[2,640,288]{2,1,0:T(8,128)(2,1)}, bf16[2,4,288,512]{3,2,1,0:T(8,128)(2,1)}, bf16[8,40,2048]{2,1,0:T(8,128)(2,1)}) custom-call(bf16[3,4,288,128]{3,2,1,0:T(8,128)(2,1)} %bitcast.11, f32[16,128]{1,0:T(8,128)} %pad.9.meta, bf16[160,3584]{1,0:T(8,128)(2,1)} %own_tokens.1, bf16[2,3584,512]{2,1,0:T(8,128)(2,1)} %bitcast.9, ...), custom_call_target="tpu_custom_call" | custom-call | tf_op jit(solution)/shard_map/pallas_call | solution.py:54
  108.9 81.9 %shard_map.87 = (bf16[4,288,128]{2,1,0:T(8,128)(2,1)}, f32[8,40,128]{2,1,0:T(8,128)}) custom-call(bf16[2,640,288]{2,1,0:T(8,128)(2,1)} %get-tuple-element.7.hid, bf16[2,4,288,512]{3,2,1,0:T(8,128)(2,1)} %get-tuple-element.8.weights, bf16[8,40,2048]{2,1,0:T(8,128)(2,1)} %get-tuple-element.9.teacher), custom_call_target="tpu_custom_call" | custom-call | tf_op jit(solution)/shard_map/pallas_call | solution.py:54
  190.7 1.0 reduce_sum.10
  191.8 0.1 reduce_sum.14
  191.9 0.6 broadcast_multiply_fusion
  192.4 1.1 copy.13
  193.6 0.8 convert_element_type.11
  (1 shorter events, 0.0 us)

commit v9 on v8

--- a/solution.py
+++ b/solution.py
@@ -410,6 +410,7 @@
             serve(2)
     for copy in returns:
         copy.wait_recv()
+    local = []
     changes = [remote(hidden.at[r], hidden.at[r], dsend.at[per], drecv.at[per], sibling)]
     changes[0].start()
     for i in (1, 2, 3, 0):
@@ -420,9 +421,8 @@
         src = student_down.at[(1 - r) * per + q]
         changes.append(remote(src, down_both.at[r, q], dsend.at[i], drecv.at[i], sibling))
         changes[-1].start()
-    local = [pltpu.make_async_copy(student_down.at[r * per + q], down_both.at[r, q], own.at[5 + q]) for q in range(per)]
-    for copy in local:
-        copy.start()
+        local.append(pltpu.make_async_copy(student_down.at[r * per + q], down_both.at[r, q], own.at[5 + i]))
+        local[-1].start()
     for copy in local + changes:
         copy.wait()
     for copy in started + returns + list(sends.values()) + list(forwards.values()) + list(swaps.values()):
@@ -584,8 +584,8 @@
         copy.wait_recv()
     rows, span = chunks.shape[1], chunks.shape[2]
     subs = []
-    for u in range(3):
-        band = pl.ds(u * (rows // 3), rows // 3)
+    for u in range(6):
+        band = pl.ds(u * (rows // 6), rows // 6)
         subs.append(((band, pl.ds(0, span)), (band, pl.ds(0, span // 2)), (band, pl.ds(span // 2, span // 2))))
     ring = {}
     size = span // NX
@@ -664,8 +664,8 @@
         functools.partial(tail_kernel, nz, count, tok), 4,
         [shape((NX, sub, lanes), BF), shape((nr * ny, block, 128), F32)],
         [pltpu.VMEM(b, BF) for b in buffers] + [pltpu.VMEM((block, 128), F32)]
-        + [dma(4 * count + 1, 2, steps, 1)] * 2 + [dma(2, steps, 3)] * 2 + [dma(steps)] * 2 + [dma(3, 3)] * 2
-        + [dma(2 * ny - 1)] * 2 + [dma(6)]
+        + [dma(4 * count + 1, 2, steps, 1)] * 2 + [dma(2, steps, 6)] * 2 + [dma(steps)] * 2 + [dma(3, 6)] * 2
+        + [dma(2 * ny - 1)] * 2 + [dma(9)]
         + [pltpu.VMEM(b, BF) for b in flows],
         hidden, student_down, teacher,
         specs=[whole, far, whole],

time: 195 us -> 195 us (level)
  no operation moved by 1% of the time
where the time goes in v9:
time: 195 us; the launch traced here: 194 us
  Pallas kernels  185 us (95%)
  other arithmetic  5.08 us (3%)
  local copies, waits for them, and re-layouts  3.86 us (2%)
    pallas_call x2, Pallas kernels, kernel_call(): pl.pallas_call(body, out_shape=outs, in_specs=specs or [whole] * len(args...  185 us

profile of v9, /device:TPU:1, one launch (start us, length us, event | category | flops | bytes accessed | tf_op | source)
XLA Modules:
  0.0 194.4 jit_solution(9739020402587180202)
XLA Ops:
  0.6 0.7 convert_element_type.10
  1.3 0.7 maximum_bitcast_fusion
  2.0 0.6 pad.9.meta
  2.6 1.3 pad_maximum_fusion
  3.9 0.9 copy.14
  4.8 1.1 pad.8.clone
  5.9 103.1 %shard_map.86 = (bf16[2,640,288]{2,1,0:T(8,128)(2,1)}, bf16[2,4,288,512]{3,2,1,0:T(8,128)(2,1)}, bf16[8,40,2048]{2,1,0:T(8,128)(2,1)}) custom-call(bf16[3,4,288,128]{3,2,1,0:T(8,128)(2,1)} %bitcast.11, f32[16,128]{1,0:T(8,128)} %pad.9.meta, bf16[160,3584]{1,0:T(8,128)(2,1)} %own_tokens.1, bf16[2,3584,512]{2,1,0:T(8,128)(2,1)} %bitcast.9, ...), custom_call_target="tpu_custom_call" | custom-call | tf_op jit(solution)/shard_map/pallas_call | solution.py:54
  109.1 81.7 %shard_map.87 = (bf16[4,288,128]{2,1,0:T(8,128)(2,1)}, f32[8,40,128]{2,1,0:T(8,128)}) custom-call(bf16[2,640,288]{2,1,0:T(8,128)(2,1)} %get-tuple-element.7.hid, bf16[2,4,288,512]{3,2,1,0:T(8,128)(2,1)} %get-tuple-element.8.weights, bf16[8,40,2048]{2,1,0:T(8,128)(2,1)} %get-tuple-element.9.teacher), custom_call_target="tpu_custom_call" | custom-call | tf_op jit(solution)/shard_map/pallas_call | solution.py:54
  190.7 1.0 reduce_sum.10
  191.8 0.1 reduce_sum.14
  191.9 0.6 broadcast_multiply_fusion
  192.5 1.1 copy.13
  193.6 0.8 convert_element_type.11
  (1 shorter events, 0.0 us)
